TPU v7x, 32 devices: a whole 2x2x4 slice. The times are simulated.
32 devices in a mesh: wide: 8 (over z, x), rep: 4 (over y, core).
Axes of the slice: x: 2, y: 2, z: 4, core: 2. Of those that a mesh axis runs over, the one named last changes fastest.
Arguments:
- tokens: bfloat16 [64, 64, 64, 512], P('rep', 'wide'), may hold values from -8 to 8
- cotangent: float32 [64, 64, 64, 512], P('rep', 'wide'), may hold values from -6 to 6
- norm_gain: float32 [2, 2, 512], replicated, may hold values from 0.5 to 1.5
- norm_shift: float32 [2, 2, 512], replicated, may hold values from -1.75 to 1.75
- mix_in: bfloat16 [2, 512, 128], replicated, may hold values from -0.5 to 0.5
- mix_in_bias: float32 [2, 8, 128], replicated, may hold values from -1.75 to 1.75
- mix_out: bfloat16 [2, 512, 128], replicated, may hold values from -0.5 to 0.5
- mix_out_bias: float32 [2, 8, 128], replicated, may hold values from -1.75 to 1.75
- w_in: bfloat16 [2, 512, 2048], replicated, may hold values from -0.25 to 0.25
- b_in: float32 [2, 2048], replicated, may hold values from -1.75 to 1.75
- w_out: bfloat16 [2, 2048, 512], replicated, may hold values from -0.125 to 0.125
- b_out: float32 [2, 512], replicated, may hold values from -1.75 to 1.75
Outputs:
- output_field: float32 [64, 64, 64, 512], P('rep', 'wide')
- input_grad: float32 [64, 64, 64, 512], P('rep', 'wide')
- gain_grad: float32 [2, 2, 512], replicated
- shift_grad: float32 [2, 2, 512], replicated
- mix_in_grad: float32 [2, 512, 128], P(None, 'wide')
- mix_in_bias_grad: float32 [2, 8, 128], replicated
- mix_out_grad: float32 [2, 512, 128], P(None, 'wide')
- mix_out_bias_grad: float32 [2, 8, 128], replicated
- w_in_grad: float32 [2, 512, 2048], P(None, 'wide')
- b_in_grad: float32 [2, 2048], replicated
- w_out_grad: float32 [2, 2048, 512], P(None, None, 'wide')
- b_out_grad: float32 [2, 512], replicated
All inputs are finite; a program needn't handle non-finite values.
Results may differ from a plain program's by a relative error of at most 0.035.
Values may be sent and summed in bfloat16 or wider, within the bound.
No kernel may reach another device: no remote copies, remote signals or barrier semaphores. Data moves between devices by JAX's collectives and lax.ppermute only.
A program may use at most 704 MiB of HBM per device.

v0:
```python
import math

import jax
import jax.numpy as jnp
from jax import lax
from jax.sharding import PartitionSpec as P

D = 512
NB = 8
BS = 64
KW = 32
KH = 32
H = 64
W = 64
LAYERS = 2


EPSILON = 1e-05
THRESHOLD = 0.1
HIGHEST = lax.Precision.HIGHEST


def dft_tables():
    col_index = jnp.arange(W, dtype=jnp.int32)
    col_freq = jnp.arange(KW, dtype=jnp.int32)
    col_phase = (col_index[:, None] * col_freq[None, :] % W).astype(jnp.float32) * (
        2.0 * math.pi / W
    )
    col_scale = 1.0 / math.sqrt(W)
    forward_cols = jnp.stack([jnp.cos(col_phase), -jnp.sin(col_phase)], axis=1) * col_scale
    doubling = jnp.where(col_freq == 0, 1.0, 2.0).astype(jnp.float32)
    inverse_cols = (
        jnp.stack(
            [jnp.cos(col_phase).T * doubling[:, None], -jnp.sin(col_phase).T * doubling[:, None]],
            axis=0,
        )
        * col_scale
    )
    row_index = jnp.arange(H, dtype=jnp.int32)
    mode_index = jnp.arange(KH, dtype=jnp.int32)
    row_freq = jnp.where(mode_index < KH // 2, mode_index, H - KH + mode_index)
    row_phase = (row_freq[:, None] * row_index[None, :] % H).astype(jnp.float32) * (
        2.0 * math.pi / H
    )
    cosine = jnp.cos(row_phase) / math.sqrt(H)
    sine = jnp.sin(row_phase) / math.sqrt(H)
    forward_rows = jnp.stack([jnp.stack([cosine, sine], -1), jnp.stack([-sine, cosine], -1)], 1)
    inverse_rows = jnp.stack(
        [jnp.stack([cosine.T, -sine.T], -1), jnp.stack([sine.T, cosine.T], -1)], 1
    )
    return (forward_cols, inverse_cols, forward_rows, inverse_rows)


def layer_norm(values, gain_row, shift_row):
    center = values - jnp.mean(values, axis=-1, keepdims=True)
    spread = jnp.mean(center * center, axis=-1, keepdims=True)
    return center * lax.rsqrt(spread + EPSILON) * gain_row + shift_row


def gelu_tanh(values):
    return jax.nn.gelu(values, approximate=True)


def shrink(values):
    return values - THRESHOLD * jnp.tanh(values / THRESHOLD)


def block_matrix(weights, onehot_low):
    picked = jnp.einsum(
        "ac,cbd->abd",
        onehot_low,
        weights.reshape(NB, BS, 2 * BS),
        preferred_element_type=jnp.float32,
    ).astype(jnp.bfloat16)
    real_part = picked[:, :, :BS]
    imag_part = picked[:, :, BS:]
    upper = jnp.concatenate([real_part, imag_part], -1)
    lower = jnp.concatenate([-imag_part, real_part], -1)
    return jnp.concatenate([upper, lower], 1)


def mode_forward(arriving, forward_rows, mixing):
    first_big, first_bias, second_big, second_bias = mixing
    item_count, pair_count = (arriving.shape[0], arriving.shape[1])
    halves = arriving.reshape(item_count, pair_count, H, 2, BS)
    mode_data = jnp.einsum(
        "jphq,iahqb->iajpb", forward_rows, halves, preferred_element_type=jnp.float32
    )
    mode_data = mode_data.reshape(item_count, pair_count, KH, 2 * BS).astype(jnp.bfloat16)
    first_pre = (
        jnp.einsum("iakc,acd->iakd", mode_data, first_big, preferred_element_type=jnp.float32)
        + first_bias[None, :, None, :]
    )
    active = gelu_tanh(first_pre).astype(jnp.bfloat16)
    second = (
        jnp.einsum("iakc,acd->iakd", active, second_big, preferred_element_type=jnp.float32)
        + second_bias[None, :, None, :]
    )
    return (mode_data, first_pre, active, second)


def mode_inverse(second, inverse_rows):
    item_count, pair_count = (second.shape[0], second.shape[1])
    shrunk = shrink(second).astype(jnp.bfloat16).reshape(item_count, pair_count, KH, 2, BS)
    rows_out = jnp.einsum(
        "hpjq,iajqb->iahpb", inverse_rows, shrunk, preferred_element_type=jnp.float32
    )
    return rows_out.reshape(item_count, pair_count, H, 2 * BS).astype(jnp.bfloat16)


def mode_backward(first_pre, second, arrived, forward_rows, inverse_rows, mixing):
    first_big, first_bias, second_big, second_bias = mixing
    item_count, pair_count = (arrived.shape[0], arrived.shape[1])
    halves = arrived.reshape(item_count, pair_count, H, 2, BS)
    d_shrunk = jnp.einsum(
        "hpjq,iahpb->iajqb", inverse_rows, halves, preferred_element_type=jnp.float32
    )
    d_shrunk = d_shrunk.reshape(item_count, pair_count, KH, 2 * BS)
    unused, shrink_pull = jax.vjp(shrink, second)
    d_second = shrink_pull(d_shrunk)[0].astype(jnp.bfloat16)
    d_active = jnp.einsum(
        "iakd,acd->iakc", d_second, second_big, preferred_element_type=jnp.float32
    )
    unused, gelu_pull = jax.vjp(gelu_tanh, first_pre)
    d_first = gelu_pull(d_active)[0].astype(jnp.bfloat16)
    d_modes = jnp.einsum(
        "iakd,acd->iakc", d_first, first_big, preferred_element_type=jnp.float32
    ).astype(jnp.bfloat16)
    d_halves = d_modes.reshape(item_count, pair_count, KH, 2, BS)
    d_rows = jnp.einsum(
        "jphq,iajpb->iahqb", forward_rows, d_halves, preferred_element_type=jnp.float32
    )
    return (
        d_rows.reshape(item_count, pair_count, H, 2 * BS).astype(jnp.bfloat16),
        d_first,
        d_second,
    )


def block_grads(inputs, grads, onehot_full):
    product = jnp.einsum("iakc,iakd->acd", inputs, grads, preferred_element_type=jnp.float32)
    real_grad = product[:, :BS, :BS] + product[:, BS:, BS:]
    imag_grad = product[:, :BS, BS:] - product[:, BS:, :BS]
    pair_grad = jnp.concatenate([real_grad, imag_grad], -1)
    weight_grad = jnp.einsum("ac,abd->cbd", onehot_full, pair_grad, precision=HIGHEST).reshape(
        D, 2 * BS
    )
    bias_terms = jnp.sum(grads.astype(jnp.float32), axis=(0, 2))
    bias_grad = jnp.dot(onehot_full.T, bias_terms, precision=HIGHEST)
    return (weight_grad, bias_grad)


def body(
    tokens,
    cotangent,
    norm_gain,
    norm_shift,
    mix_in,
    mix_in_bias,
    mix_out,
    mix_out_bias,
    w_in,
    b_in,
    w_out,
    b_out,
):
    forward_cols, inverse_cols, forward_rows, inverse_rows = [
        table_item.astype(jnp.bfloat16) for table_item in dft_tables()
    ]
    devices = lax.axis_size("wide")
    per_device = NB * KW // devices
    global_pair = lax.axis_index("wide") * per_device + jnp.arange(per_device, dtype=jnp.int32)
    onehot_full = (global_pair[:, None] // KW == jnp.arange(NB, dtype=jnp.int32)[None, :]).astype(
        jnp.float32
    )
    onehot_low = onehot_full.astype(jnp.bfloat16)
    item_count, rows_dev = (tokens.shape[0], tokens.shape[1])
    current = tokens.astype(jnp.float32)
    stored = []
    for depth_index in range(LAYERS):
        mixing = (
            block_matrix(mix_in[depth_index], onehot_low),
            jnp.dot(onehot_full, mix_in_bias[depth_index], precision=HIGHEST),
            block_matrix(mix_out[depth_index], onehot_low),
            jnp.dot(onehot_full, mix_out_bias[depth_index], precision=HIGHEST),
        )
        normed = layer_norm(current, norm_gain[depth_index, 0], norm_shift[depth_index, 0])
        spectra = jnp.einsum(
            "irwcb,wpk->ickrpb",
            normed.astype(jnp.bfloat16).reshape(item_count, rows_dev, W, NB, BS),
            forward_cols,
            preferred_element_type=jnp.float32,
        )
        spectra = spectra.reshape(item_count, NB * KW, rows_dev, 2 * BS).astype(jnp.bfloat16)
        forward_mode_data, first_pre, forward_active, second = mode_forward(
            lax.all_to_all(spectra, "wide", split_axis=1, concat_axis=2, tiled=True),
            forward_rows,
            mixing,
        )
        returning = lax.all_to_all(
            mode_inverse(second, inverse_rows), "wide", split_axis=2, concat_axis=1, tiled=True
        )
        returned = (returning,)
        back_rows = returned[0].reshape(item_count, NB, KW, rows_dev, 2, BS)
        filtered = jnp.einsum(
            "pkw,ickrpb->irwcb", inverse_cols, back_rows, preferred_element_type=jnp.float32
        )
        middle = current + filtered.reshape(item_count, rows_dev, W, D) + normed
        lowered = layer_norm(middle, norm_gain[depth_index, 1], norm_shift[depth_index, 1]).astype(
            jnp.bfloat16
        )
        hidden_pre = (
            jnp.einsum(
                "irwd,df->irwf", lowered, w_in[depth_index], preferred_element_type=jnp.float32
            )
            + b_in[depth_index]
        )
        hidden_act = gelu_tanh(hidden_pre).astype(jnp.bfloat16)
        branch = (
            jnp.einsum(
                "irwf,fd->irwd", hidden_act, w_out[depth_index], preferred_element_type=jnp.float32
            )
            + b_out[depth_index]
        )
        stored.append(
            (
                current,
                normed,
                spectra,
                middle,
                lowered,
                hidden_pre,
                hidden_act,
                mixing,
                returned[1:],
            )
        )
        current = middle + branch
    upstream = cotangent
    collected = [None] * LAYERS
    for depth_index in reversed(range(LAYERS)):
        (
            layer_input,
            normed,
            spectra,
            middle,
            lowered,
            hidden_pre,
            hidden_act,
            mixing,
            kept_modes,
        ) = stored[depth_index]
        branch_grad = upstream.astype(jnp.bfloat16)
        w_out_part = jnp.einsum(
            "irwf,irwd->fd", hidden_act, branch_grad, preferred_element_type=jnp.float32
        )
        b_out_part = jnp.sum(branch_grad.astype(jnp.float32), axis=(0, 1, 2))
        act_grad = jnp.einsum(
            "irwd,fd->irwf", branch_grad, w_out[depth_index], preferred_element_type=jnp.float32
        )
        unused, gelu_pull = jax.vjp(gelu_tanh, hidden_pre)
        pre_grad = gelu_pull(act_grad)[0].astype(jnp.bfloat16)
        w_in_part = jnp.einsum(
            "irwd,irwf->df", lowered, pre_grad, preferred_element_type=jnp.float32
        )
        b_in_part = jnp.sum(pre_grad.astype(jnp.float32), axis=(0, 1, 2))
        low_grad = jnp.einsum(
            "irwf,df->irwd", pre_grad, w_in[depth_index], preferred_element_type=jnp.float32
        )
        unused, second_norm_pull = jax.vjp(
            layer_norm, middle, norm_gain[depth_index, 1], norm_shift[depth_index, 1]
        )
        mid_norm_grad, gain_second, shift_second = second_norm_pull(low_grad)
        mid_grad = upstream + mid_norm_grad
        filt_grad = mid_grad.astype(jnp.bfloat16).reshape(item_count, rows_dev, W, NB, BS)
        back_grad = jnp.einsum(
            "pkw,irwcb->ickrpb", inverse_cols, filt_grad, preferred_element_type=jnp.float32
        )
        back_grad = back_grad.reshape(item_count, NB * KW, rows_dev, 2 * BS).astype(jnp.bfloat16)
        backward_arriving = lax.all_to_all(spectra, "wide", split_axis=1, concat_axis=2, tiled=True)
        arrived = lax.all_to_all(back_grad, "wide", split_axis=1, concat_axis=2, tiled=True)
        backward_mode_data, backward_first_pre, backward_active, backward_second = mode_forward(
            backward_arriving, forward_rows, mixing
        )
        d_rows, d_first, d_second = mode_backward(
            backward_first_pre, backward_second, arrived, forward_rows, inverse_rows, mixing
        )
        sent_back = lax.all_to_all(d_rows, "wide", split_axis=2, concat_axis=1, tiled=True)
        col_grad, mode_data, active, d_first, d_second = (
            sent_back,
            backward_mode_data,
            backward_active,
            d_first,
            d_second,
        )
        mix_in_part, mix_in_bias_part = block_grads(mode_data, d_first, onehot_full)
        mix_out_part, mix_out_bias_part = block_grads(active, d_second, onehot_full)
        col_grad = col_grad.reshape(item_count, NB, KW, rows_dev, 2, BS)
        normed_grad = jnp.einsum(
            "wpk,ickrpb->irwcb", forward_cols, col_grad, preferred_element_type=jnp.float32
        )
        normed_grad = normed_grad.reshape(item_count, rows_dev, W, D) + mid_grad
        unused, first_norm_pull = jax.vjp(
            layer_norm, layer_input, norm_gain[depth_index, 0], norm_shift[depth_index, 0]
        )
        input_part, gain_first, shift_first = first_norm_pull(normed_grad)
        upstream = mid_grad + input_part
        collected[depth_index] = (
            jnp.stack([gain_first, gain_second]),
            jnp.stack([shift_first, shift_second]),
            mix_in_part,
            mix_in_bias_part,
            mix_out_part,
            mix_out_bias_part,
            w_in_part,
            b_in_part,
            w_out_part,
            b_out_part,
        )
    stacked = [
        jnp.stack([collected[depth_index][slot] for depth_index in range(LAYERS)])
        for slot in range(10)
    ]
    small_grads = lax.psum(
        (stacked[0], stacked[1], stacked[3], stacked[5], stacked[7], stacked[9]), ("wide", "rep")
    )
    large_grads = (stacked[2], stacked[4], stacked[6], stacked[8])
    pieces = (
        lax.psum_scatter(large_grads[0], "wide", scatter_dimension=1, tiled=True),
        lax.psum_scatter(large_grads[1], "wide", scatter_dimension=1, tiled=True),
        lax.psum_scatter(large_grads[2], "wide", scatter_dimension=1, tiled=True),
        lax.psum_scatter(large_grads[3], "wide", scatter_dimension=2, tiled=True),
    )
    pieces = (
        lax.psum(pieces[0].astype(jnp.bfloat16), "rep").astype(jnp.float32),
        lax.psum(pieces[1].astype(jnp.bfloat16), "rep").astype(jnp.float32),
        lax.psum(pieces[2].astype(jnp.bfloat16), "rep").astype(jnp.float32),
        lax.psum(pieces[3].astype(jnp.bfloat16), "rep").astype(jnp.float32),
    )
    return (
        current,
        upstream,
        small_grads[0],
        small_grads[1],
        pieces[0],
        small_grads[2],
        pieces[1],
        small_grads[3],
        pieces[2],
        small_grads[4],
        pieces[3],
        small_grads[5],
    )


def solution(mesh):
    placed = (
        P("rep", "wide", None, None),
        P("rep", "wide", None, None),
        P(),
        P(),
        P(),
        P(),
        P(),
        P(),
        P(),
        P(),
        P(),
        P(),
    )
    return jax.shard_map(
        body,
        mesh=mesh,
        in_specs=placed,
        out_specs=(
            P("rep", "wide", None, None),
            P("rep", "wide", None, None),
            P(),
            P(),
            P(None, "wide", None),
            P(),
            P(None, "wide", None),
            P(),
            P(None, "wide", None),
            P(),
            P(None, None, "wide"),
            P(),
        ),
        check_vma=False,
    )
```

profile of v0, /device:TPU:0, one launch (start us, length us, event | category | flops | bytes accessed | tf_op | source)
XLA Modules:
  0.0 3952.7 jit_solution(1615715404601827696)
XLA Ops:
  27.4 21.2 reshape.758
  60.5 30.8 copy.254
  91.3 27.0 reshape.834
  130.1 179.0 %all-to-all-done = bf16[16,256,8,128]{3,2,0,1:T(8,128)(2,1)} async-done(((bf16[16,256,8,128]{3,2,0,1:T(8,128)(2,1)}), bf16[16,256,8,128]{3,2,0,1:T(8,128)(2,1)}, u32[]{:S(2)}, u32[]{:S(2)}) %all-to-all-start) | async-done | bytes 8388640 | tf_op jit(solution)/shard_map/all_to_all | solution.py:196
  318.3 27.8 reshape.759
  425.0 18.7 copy.135
  450.3 180.8 %all-to-all-done.1 = bf16[16,32,64,128]{3,1,0,2:T(8,128)(2,1)} async-done(((bf16[16,32,64,128]{3,1,0,2:T(8,128)(2,1)}), bf16[16,32,64,128]{3,1,0,2:T(8,128)(2,1)}, u32[]{:S(2)}, u32[]{:S(2)}) %all-to-all-start.1) | async-done | bytes 8388640 | tf_op jit(solution)/shard_map/all_to_all | solution.py:200
  631.1 27.8 reshape.835
  658.9 16.6 fusion.57
  675.5 32.0 copy.139
  707.5 27.6 reshape.762
  750.3 41.1 %multiply_convert_fusion.1 = (bf16[16,8,64,2048]{3,2,1,0:T(8,128)(2,1)}, f32[16,8,64,2048]{3,2,1,0:T(8,128)}) fusion(f32[2048]{0:T(1024)S(1)} %bitcast.611, bf16[2,512,2048]{2,1,0:T(8,128)(2,1)} %param.20, f32[16,8,64,512]{3,2,1,0:T(8,128)S(1)} %get-tuple-element.89, f32[512]{0:T(512)S(1)} %bitcast.620, f32[512]{0:T(512)S(1)} %bitcast.593, ...), kind=kOutput, calls=%fused_computation.21 | convolution fusion | flops 17368612864 | bytes 119615488 | tf_op jit(solution)/shard_map/irwd,df->irwf/dot_general | solution.py:213
  791.4 28.5 fusion.278
  835.6 21.2 reshape.763
  868.3 30.8 copy.266
  899.1 27.0 reshape.836
  933.9 179.7 %all-to-all-done.2 = bf16[16,256,8,128]{3,2,0,1:T(8,128)(2,1)} async-done(((bf16[16,256,8,128]{3,2,0,1:T(8,128)(2,1)}), bf16[16,256,8,128]{3,2,0,1:T(8,128)(2,1)}, u32[]{:S(2)}, u32[]{:S(2)}) %all-to-all-start.2) | async-done | bytes 8388640 | tf_op jit(solution)/shard_map/all_to_all | solution.py:196
  1122.8 27.9 reshape.764
  1229.2 18.7 copy.152
  1247.9 187.7 %all_to_all.130 = bf16[16,32,64,128]{3,1,0,2:T(8,128)(2,1)} all-to-all(bf16[16,32,64,128]{3,1,0,2:T(8,128)(2,1)} %copy.152), channel_id=1, replica_groups=mesh['wide'=8,'rep'=4] {'wide'}, dimensions={2} | all-to-all | bytes 16777216 | tf_op jit(solution)/shard_map/all_to_all | solution.py:200
  1435.6 27.8 reshape.837
  1463.4 16.6 fusion.60
  1480.0 32.0 copy.156
  1512.0 27.7 reshape.767
  1555.7 41.0 %multiply_convert_fusion = (bf16[16,8,64,2048]{3,2,1,0:T(8,128)(2,1)}, f32[16,8,64,2048]{3,2,1,0:T(8,128)}) fusion(f32[2048]{0:T(1024)S(1)} %bitcast.613, bf16[2,512,2048]{2,1,0:T(8,128)(2,1)} %param.20, f32[16,8,64,512]{3,2,1,0:T(8,128)S(1)} %get-tuple-element.87, f32[512]{0:T(512)S(1)} %bitcast.622, f32[512]{0:T(512)S(1)} %bitcast.588, ...), kind=kOutput, calls=%fused_computation.20 | convolution fusion | flops 17368612864 | bytes 119615488 | tf_op jit(solution)/shard_map/irwd,df->irwf/dot_general | solution.py:213
  1596.7 64.0 %convert_reduce_fusion = (f32[2048]{0:T(1024)}, bf16[16,8,64,2048]{3,2,1,0:T(8,128)(2,1)}) fusion(f32[16,8,64,2048]{3,2,1,0:T(8,128)} %get-tuple-element.144, f32[2048]{0:T(1024)S(1)} %bitcast.614, bf16[2,2048,512]{2,1,0:T(8,128)(2,1)} %param.22, f32[16,8,64,512]{3,2,1,0:T(8,128)} %param.13), kind=kOutput, calls=%fused_computation.18 | convolution fusion | flops 17569937408 | bytes 119554048 | tf_op jit(solution)/shard_map/irwd,fd->irwf/dot_general | solution.py:258
  1660.7 29.3 fusion.265
  1703.6 31.9 fusion.268
  1735.5 21.2 reshape.768
  1768.3 24.9 copy.280
  1793.1 26.9 reshape.838
  1820.1 186.7 %all_to_all.131 = bf16[16,256,8,128]{3,2,0,1:T(8,128)(2,1)} all-to-all(bf16[16,256,8,128]{3,2,0,1:T(8,128)(2,1)} %reshape.838), channel_id=1, replica_groups=mesh['wide'=8,'rep'=4] {'wide'}, dimensions={1} | all-to-all | bytes 16777216 | tf_op jit(solution)/shard_map/all_to_all | solution.py:281
  2015.9 27.9 reshape.769
  2057.7 28.6 copy.163
  2150.6 18.8 copy.168
  2169.4 187.2 %all_to_all.132 = bf16[16,32,64,128]{3,1,0,2:T(8,128)(2,1)} all-to-all(bf16[16,32,64,128]{3,1,0,2:T(8,128)(2,1)} %copy.168), channel_id=1, replica_groups=mesh['wide'=8,'rep'=4] {'wide'}, dimensions={2} | all-to-all | bytes 16777216 | tf_op jit(solution)/shard_map/all_to_all | solution.py:288
  2356.6 27.8 reshape.839
  2384.4 16.6 fusion.63
  2401.0 32.0 copy.172
  2433.0 27.7 reshape.773
  2460.7 25.4 fusion.264
  2500.1 17.5 convert_reduce_fusion.4
  2517.7 63.3 %convert_reduce_fusion.1 = (f32[2048]{0:T(1024)}, bf16[16,8,64,2048]{3,2,1,0:T(8,128)(2,1)}) fusion(f32[16,8,64,2048]{3,2,1,0:T(8,128)} %get-tuple-element.138, f32[2048]{0:T(1024)S(1)} %bitcast.612, bf16[16,8,64,512]{3,2,1,0:T(8,128)(2,1)} %get-tuple-element.75, bf16[2,2048,512]{2,1,0:T(8,128)(2,1)} %param.22), kind=kOutput, calls=%fused_computation.19 | convolution fusion | flops 17565743104 | bytes 111165440 | tf_op jit(solution)/shard_map/irwd,fd->irwf/dot_general | solution.py:258
  2581.0 29.4 fusion.263
  2624.1 34.9 fusion.267
  2658.9 21.2 reshape.774
  2691.6 24.6 copy.298
  2716.2 27.1 reshape.840
  2748.4 26.0 convolution_bitcast_fusion.2
  2786.1 144.1 %all-to-all-done.6 = bf16[16,256,8,128]{3,2,0,1:T(8,128)(2,1)} async-done(((bf16[16,256,8,128]{3,2,0,1:T(8,128)(2,1)}), bf16[16,256,8,128]{3,2,0,1:T(8,128)(2,1)}, u32[]{:S(2)}, u32[]{:S(2)}) %all-to-all-start.6) | async-done | bytes 8388640 | tf_op jit(solution)/shard_map/all_to_all | solution.py:281
  2939.3 27.8 reshape.775
  2981.0 28.6 copy.179
  3059.0 25.7 convolution_bitcast_fusion.3
  3119.6 18.8 copy.184
  3144.7 26.6 convolution_bitcast_fusion
  3171.4 28.5 add_add_fusion.8
  3200.2 21.5 convolution_bitcast_fusion.1
  3239.6 438.1 %all-reduce.11 = bf16[2,2048,512]{1,0,2:T(2,128)(2,1)} all-reduce(f32[2,2048,512]{1,0,2:T(2,128)} %copy.199), channel_id=5, replica_groups=mesh['wide'=8,'rep'=4] {'wide'}, use_global_device_ids=true, to_apply=%region_41.42.clone | all-reduce | flops 2097152 | bytes 12582912
  3685.4 30.9 all-reduce.8.cloned.1.call-done
  3719.1 36.3 all-reduce.10.cloned.1.call-done
  3759.7 27.8 reshape.841
  3804.0 32.0 copy.188
  3836.1 27.6 reshape.779
  3904.5 41.2 %all-reduce.1 = (f32[2,2,512]{2,1,0:T(2,128)}, f32[2,2,512]{2,1,0:T(2,128)}, f32[2,8,128]{2,1,0:T(8,128)}, f32[2,8,128]{2,1,0:T(8,128)}, f32[2,2048]{1,0:T(2,128)}, /*index=5*/f32[2,512]{1,0:T(2,128)}) all-reduce(f32[2,2,512]{2,1,0:T(2,128)S(1)} %pad_maximum_fusion.9, ...), channel_id=1, replica_groups=mesh['wide'=8,'rep'=4] {'wide','rep'}, use_global_device_ids=true, to_apply=%region_20.21 | all-reduce | flops 13312 | bytes 106496 | tf_op jit(solution)/shard_map/psum | solution.py:324
  (488 shorter events, 662.4 us)
Async XLA Ops:
  91.3 35.1 copy-start.74
  118.3 190.8 %all-to-all-start = ((bf16[16,256,8,128]{3,2,0,1:T(8,128)(2,1)}), bf16[16,256,8,128]{3,2,0,1:T(8,128)(2,1)}, u32[]{:S(2)}, u32[]{:S(2)}) async-start(bf16[16,256,8,128]{3,2,0,1:T(8,128)(2,1)} %reshape.834), calls=%async_computation | async-start | bytes 16777216 | tf_op jit(solution)/shard_map/all_to_all | solution.py:196
  126.2 288.1 %copy-start.58 = (bf16[64,1,32,2]{0,2,3,1:T(8,128)(2,1)}, bf16[64,1,32,2]{0,2,3,1:T(8,128)(2,1)S(1)}, u32[]{:S(2)}) copy-start(bf16[64,1,32,2]{0,2,3,1:T(8,128)(2,1)S(1)} %get-tuple-element.121) | copy-start | bytes 24580
  126.2 288.1 %copy-start.62 = (bf16[64,1,32,2]{0,2,3,1:T(8,128)(2,1)}, bf16[64,1,32,2]{0,2,3,1:T(8,128)(2,1)S(1)}, u32[]{:S(2)}) copy-start(bf16[64,1,32,2]{0,2,3,1:T(8,128)(2,1)S(1)} %get-tuple-element.122) | copy-start | bytes 24580
  126.4 219.7 %copy-start.76 = (bf16[32,1,64,2]{2,0,3,1:T(8,128)(2,1)}, bf16[32,1,64,2]{2,0,3,1:T(8,128)(2,1)S(1)}, u32[]{:S(2)}) copy-start(bf16[32,1,64,2]{2,0,3,1:T(8,128)(2,1)S(1)} %get-tuple-element.123) | copy-start | bytes 24580
  126.4 219.7 %copy-start.80 = (bf16[32,1,64,2]{2,0,3,1:T(8,128)(2,1)}, bf16[32,1,64,2]{2,0,3,1:T(8,128)(2,1)S(1)}, u32[]{:S(2)}) copy-start(bf16[32,1,64,2]{2,0,3,1:T(8,128)(2,1)S(1)} %get-tuple-element.124) | copy-start | bytes 24580
  128.0 257.0 %copy-start.4 = (bf16[32,128,128,1]{2,0,1,3:T(8,128)(2,1)}, bf16[32,128,128,1]{2,0,1,3:T(8,128)(2,1)S(1)}, u32[]{:S(2)}) copy-start(bf16[32,128,128,1]{2,0,1,3:T(8,128)(2,1)S(1)} %maximum_bitcast_fusion.1) | copy-start | bytes 3145732
  129.6 258.8 %copy-start.31 = (bf16[32,128,128,1]{2,0,1,3:T(8,128)(2,1)}, bf16[32,128,128,1]{2,0,1,3:T(8,128)(2,1)S(1)}, u32[]{:S(2)}) copy-start(bf16[32,128,128,1]{2,0,1,3:T(8,128)(2,1)S(1)} %maximum_bitcast_fusion) | copy-start | bytes 3145732
  129.9 258.6 %copy-start.110 = (f32[32,128]{1,0:T(8,128)}, f32[32,128]{1,0:T(8,128)S(1)}, u32[]{:S(2)}) copy-start(f32[32,128]{1,0:T(8,128)S(1)} %fusion.224) | copy-start | bytes 49156
  130.1 258.4 %copy-start.94 = (f32[32,128]{1,0:T(8,128)}, f32[32,128]{1,0:T(8,128)S(1)}, u32[]{:S(2)}) copy-start(f32[32,128]{1,0:T(8,128)S(1)} %fusion.222) | copy-start | bytes 49156
  443.8 187.3 %all-to-all-start.1 = ((bf16[16,32,64,128]{3,1,0,2:T(8,128)(2,1)}), bf16[16,32,64,128]{3,1,0,2:T(8,128)(2,1)}, u32[]{:S(2)}, u32[]{:S(2)}) async-start(bf16[16,32,64,128]{3,1,0,2:T(8,128)(2,1)} %copy.135), calls=%async_computation.1 | async-start | bytes 16777216 | tf_op jit(solution)/shard_map/all_to_all | solution.py:200
  449.0 226.4 %copy-start.70 = (bf16[2,32,64,1,1,1]{2,1,0,5,4,3:T(8,128)(2,1)}, bf16[2,32,64,1,1,1]{2,1,0,5,4,3:T(8,128)(2,1)S(1)}, u32[]{:S(2)}) copy-start(bf16[2,32,64,1,1,1]{2,1,0,5,4,3:T(8,128)(2,1)S(1)} %fusion.198) | copy-start | bytes 24580
  450.3 300.0 %copy-start.129 = (f32[1,2048]{1,0:T(1,128)}, f32[1,2048]{1,0:T(1,128)S(1)}, u32[]{:S(2)}) copy-start(f32[1,2048]{1,0:T(1,128)S(1)} %get-tuple-element.112) | copy-start | bytes 24580
  746.5 44.9 %copy-start.2 = (f32[16,8,64,512]{3,2,1,0:T(8,128)}, f32[16,8,64,512]{3,2,1,0:T(8,128)S(1)}, u32[]{:S(2)}) copy-start(f32[16,8,64,512]{3,2,1,0:T(8,128)S(1)} %get-tuple-element.89) | copy-start | bytes 50331652
  746.5 44.9 %copy-start.35 = (f32[16,8,64]{2,1,0:T(8,128)}, f32[16,8,64]{2,1,0:T(8,128)S(1)}, u32[]{:S(2)}) copy-start(f32[16,8,64]{2,1,0:T(8,128)S(1)} %broadcast_multiply_fusion.2) | copy-start | bytes 98308
  750.3 41.2 %copy-start.51 = (f32[16,8,64]{2,1,0:T(8,128)}, f32[16,8,64]{2,1,0:T(8,128)S(1)}, u32[]{:S(2)}) copy-start(f32[16,8,64]{2,1,0:T(8,128)S(1)} %fusion.177) | copy-start | bytes 98308
  899.1 32.5 copy-start.56
  899.1 32.5 copy-start.85
  926.1 187.5 %all-to-all-start.2 = ((bf16[16,256,8,128]{3,2,0,1:T(8,128)(2,1)}), bf16[16,256,8,128]{3,2,0,1:T(8,128)(2,1)}, u32[]{:S(2)}, u32[]{:S(2)}) async-start(bf16[16,256,8,128]{3,2,0,1:T(8,128)(2,1)} %reshape.836), calls=%async_computation.2 | async-start | bytes 16777216 | tf_op jit(solution)/shard_map/all_to_all | solution.py:196
  932.5 257.0 %copy-start.6 = (bf16[32,128,128,1]{2,0,1,3:T(8,128)(2,1)}, bf16[32,128,128,1]{2,0,1,3:T(8,128)(2,1)S(1)}, u32[]{:S(2)}) copy-start(bf16[32,128,128,1]{2,0,1,3:T(8,128)(2,1)S(1)} %maximum_bitcast_fusion.3) | copy-start | bytes 3145732
  933.5 259.5 %copy-start.33 = (bf16[32,128,128,1]{2,0,1,3:T(8,128)(2,1)}, bf16[32,128,128,1]{2,0,1,3:T(8,128)(2,1)S(1)}, u32[]{:S(2)}) copy-start(bf16[32,128,128,1]{2,0,1,3:T(8,128)(2,1)S(1)} %maximum_bitcast_fusion.2) | copy-start | bytes 3145732
  933.7 259.3 %copy-start.113 = (f32[32,128]{1,0:T(8,128)}, f32[32,128]{1,0:T(8,128)S(1)}, u32[]{:S(2)}) copy-start(f32[32,128]{1,0:T(8,128)S(1)} %fusion.220) | copy-start | bytes 49156
  933.9 259.1 %copy-start.98 = (f32[32,128]{1,0:T(8,128)}, f32[32,128]{1,0:T(8,128)S(1)}, u32[]{:S(2)}) copy-start(f32[32,128]{1,0:T(8,128)S(1)} %fusion.218) | copy-start | bytes 49156
  1122.8 27.9 copy-start.77
  1122.8 27.9 copy-start.81
  1551.9 44.8 %copy-start.1 = (f32[16,8,64,512]{3,2,1,0:T(8,128)}, f32[16,8,64,512]{3,2,1,0:T(8,128)S(1)}, u32[]{:S(2)}) copy-start(f32[16,8,64,512]{3,2,1,0:T(8,128)S(1)} %get-tuple-element.87) | copy-start | bytes 50331652
  1552.0 151.6 %copy-start.29 = (f32[16,8,64]{2,1,0:T(8,128)}, f32[16,8,64]{2,1,0:T(8,128)S(1)}, u32[]{:S(2)}) copy-start(f32[16,8,64]{2,1,0:T(8,128)S(1)} %broadcast_multiply_fusion) | copy-start | bytes 98308
  1555.7 41.0 %copy-start.40 = (f32[16,8,64]{2,1,0:T(8,128)}, f32[16,8,64]{2,1,0:T(8,128)S(1)}, u32[]{:S(2)}) copy-start(f32[16,8,64]{2,1,0:T(8,128)S(1)} %fusion.179) | copy-start | bytes 98308
  1596.7 64.0 %copy-start.140 = (bf16[2,512,2048]{2,1,0:T(8,128)(2,1)S(1)}, bf16[2,512,2048]{2,1,0:T(8,128)(2,1)}, u32[]{:S(2)}) copy-start(bf16[2,512,2048]{2,1,0:T(8,128)(2,1)} %param.20) | copy-start | bytes 12582916
  1660.7 29.3 copy-start.50
  1660.7 29.4 copy-start.41
  2015.9 27.9 copy-start.60
  2015.9 27.9 copy-start.64
  2460.7 39.4 slice-start
  2460.7 39.4 slice-start.1
  2460.7 39.4 slice-start.2
  2517.7 63.3 %copy-start.36 = (f32[16,8,64]{2,1,0:T(8,128)S(1)}, f32[16,8,64]{2,1,0:T(8,128)}, u32[]{:S(2)}) copy-start(f32[16,8,64]{2,1,0:T(8,128)} %copy-done.35) | copy-start | bytes 98308
  2517.7 63.3 %copy-start.103 = (f32[1,1,512]{2,1,0:T(1,128)S(1)}, f32[1,1,512]{2,1,0:T(1,128)}, u32[]{:S(2)}) copy-start(f32[1,1,512]{2,1,0:T(1,128)} %get-tuple-element.114) | copy-start | bytes 6148
  2517.7 63.3 %copy-start.141 = (bf16[2,512,2048]{2,1,0:T(8,128)(2,1)S(1)}, bf16[2,512,2048]{2,1,0:T(8,128)(2,1)}, u32[]{:S(2)}) copy-start(bf16[2,512,2048]{2,1,0:T(8,128)(2,1)} %param.20) | copy-start | bytes 12582916
  2581.0 29.4 copy-start.46
  2581.0 29.5 copy-start.52
  2716.2 32.2 copy-start.30
  2716.2 32.2 copy-start.42
  2716.2 32.2 copy-start.101
  2716.2 32.2 copy-start.139
  2743.3 186.9 %all-to-all-start.6 = ((bf16[16,256,8,128]{3,2,0,1:T(8,128)(2,1)}), bf16[16,256,8,128]{3,2,0,1:T(8,128)(2,1)}, u32[]{:S(2)}, u32[]{:S(2)}) async-start(bf16[16,256,8,128]{3,2,0,1:T(8,128)(2,1)} %reshape.840), calls=%async_computation.6 | async-start | bytes 16777216 | tf_op jit(solution)/shard_map/all_to_all | solution.py:281
  2748.3 931.6 %reduce-scatter.6.cloned.1.call-start = ((), (), s32[]{:S(2)}) async-start(), calls=%async_computation.12 | async-start | bytes 589824 | tf_op jit(solution)/shard_map/reduce_scatter | solution.py:330
  2939.3 27.8 copy-start.65
  3051.2 630.2 %reduce-scatter.4.cloned.1.call-start = ((), (), s32[]{:S(2)}) async-start(), calls=%async_computation.11 | async-start | bytes 589824 | tf_op jit(solution)/shard_map/reduce_scatter | solution.py:329
  3058.9 624.1 %reduce-scatter.8.cloned.1.call-start = ((), (), s32[]{:S(2)}) async-start(), calls=%async_computation.13 | async-start | bytes 9437184 | tf_op jit(solution)/shard_map/reduce_scatter | solution.py:331
  3138.4 621.3 %all-to-all-start.7 = ((bf16[16,32,64,128]{3,1,0,2:T(8,128)(2,1)}), bf16[16,32,64,128]{3,1,0,2:T(8,128)(2,1)}, u32[]{:S(2)}, u32[]{:S(2)}) async-start(bf16[16,32,64,128]{3,1,0,2:T(8,128)(2,1)} %copy.184), calls=%async_computation.7 | async-start | bytes 16777216 | tf_op jit(solution)/shard_map/all_to_all | solution.py:288
  3143.4 572.9 %all-reduce.8.cloned.1.call-start = ((), (), s32[]{:S(2)}) async-start(), calls=%async_computation.14 | async-start | bytes 131072 | tf_op jit(solution)/shard_map/psum | solution.py:335
  3144.7 55.4 %slice-start.12 = ((s8[8388608]{0:T(1024)(128)(4,1)}), s8[4194304]{0:T(1024)(128)(4,1)S(1)}, s32[]{:S(2)}) async-start(s8[8388608]{0:T(1024)(128)(4,1)} %bitcast.567), calls=%async_computation.28 | async-start | bytes 8388608
  3171.4 28.5 copy-start.96
  3171.4 28.6 copy-start.112
  3171.4 28.7 slice-start.13
  3226.1 456.8 %copy-start.119 = (f32[512]{0:T(512)S(1)}, f32[512]{0:T(512)}, u32[]{:S(2)}) copy-start(f32[512]{0:T(512)} %get-tuple-element.52) | copy-start | bytes 6148
  3226.1 456.8 %copy-start.121 = (f32[512]{0:T(512)S(1)}, f32[512]{0:T(512)}, u32[]{:S(2)}) copy-start(f32[512]{0:T(512)} %get-tuple-element.50) | copy-start | bytes 6148
  3226.1 459.0 %copy-start.117 = (f32[512]{0:T(512)S(1)}, f32[512]{0:T(512)}, u32[]{:S(2)}) copy-start(f32[512]{0:T(512)} %get-tuple-element.90) | copy-start | bytes 6148
  3226.1 459.0 %copy-start.120 = (f32[512]{0:T(512)S(1)}, f32[512]{0:T(512)}, u32[]{:S(2)}) copy-start(f32[512]{0:T(512)} %get-tuple-element.74) | copy-start | bytes 6148
  3226.1 459.0 %copy-start.97 = (f32[32,128]{1,0:T(8,128)S(1)}, f32[32,128]{1,0:T(8,128)}, u32[]{:S(2)}) copy-start(f32[32,128]{1,0:T(8,128)} %get-tuple-element.76) | copy-start | bytes 49156
  3226.1 459.1 %copy-start.116 = (f32[32,128]{1,0:T(8,128)S(1)}, f32[32,128]{1,0:T(8,128)}, u32[]{:S(2)}) copy-start(f32[32,128]{1,0:T(8,128)} %get-tuple-element.149) | copy-start | bytes 49156
  3677.7 109.8 %copy-start.69 = (bf16[64,2,32]{0,2,1:T(8,128)(2,1)S(1)}, bf16[64,2,32]{0,2,1:T(8,128)(2,1)}, u32[]{:S(2)}) copy-start(bf16[64,2,32]{0,2,1:T(8,128)(2,1)} %copy-done.66) | copy-start | bytes 24580
  3682.9 72.5 %all-reduce.10.cloned.1.call-start = ((), (), s32[]{:S(2)}) async-start(), calls=%async_computation.15 | async-start | bytes 2097152 | tf_op jit(solution)/shard_map/psum | solution.py:338
  (103 other events, 1483.3 us)
Sparse Core Ops, SparseCore 0:
  3051.3 61.0 reduce-scatter.5
  3116.6 209.7 reduce-scatter.3
  3330.0 331.4 reduce-scatter.7
  3683.0 33.2 all-reduce.7
  3719.2 36.1 all-reduce.9
where the time goes:
time: 3980 us; the launch traced here: 3950 us
  local copies, waits for them, and re-layouts  1120 us (28%)
  blocking collectives  1040 us (26%)
  waiting for transfers between devices  751 us (19%)
  matrix products  703 us (18%)
  other arithmetic  294 us (7%)
    unnamed x1, blocking collectives  438 us
    all_to_all x2, waiting for transfers between devices, body(): lax.all_to_all(spectra, 'wide', split_axis=1, concat_axis=2, tiled=True)  359 us
    all_to_all x1, blocking collectives, body(): lax.all_to_all(mode_inverse(second, inverse_rows), 'wide', split_axis=2,...  188 us
    all_to_all x1, blocking collectives, body(): lax.all_to_all(d_rows, 'wide', split_axis=2, concat_axis=1, tiled=True)  187 us
    all_to_all x1, blocking collectives, body(): lax.all_to_all(back_grad, 'wide', split_axis=1, concat_axis=2, tiled=True)  187 us
    all_to_all x1, waiting for transfers between devices, body(): lax.all_to_all(mode_inverse(second, inverse_rows), 'wide', split_axis=2,...  181 us
    all_to_all x1, waiting for transfers between devices, body(): lax.all_to_all(back_grad, 'wide', split_axis=1, concat_axis=2, tiled=True)  144 us
    dot_general x2, matrix products, body(): jnp.einsum('irwd,fd->irwf', branch_grad, w_out[depth_index], preferred_el...  127 us
  transfers between devices with their start and end apart: 10, of which 6 were waited for; matrix products, arithmetic and copies ran while one was open for 6% of the time, Pallas kernels for 0%

commit v1 on v0

--- a/solution.py
+++ b/solution.py
@@ -1,8 +1,13 @@
+import functools
 import math
 
 import jax
 import jax.numpy as jnp
+import ml_dtypes
+import numpy as np
 from jax import lax
+from jax.experimental import pallas as pl
+from jax.experimental.pallas import tpu as pltpu
 from jax.sharding import PartitionSpec as P
 
 D = 512
@@ -353,6 +358,623 @@
     )
 
 
+BF = jnp.bfloat16
+F32 = jnp.float32
+FF = 2048
+GROUPS = 4
+GELU_A = math.sqrt(2.0 / math.pi)
+GELU_B = GELU_A * 0.044715
+HB = 16
+KB = 8
+TT = 512
+FC = 512
+VMEM = 58 * 1024 * 1024
+
+
+def plain_tables():
+    def low(table):
+        return table.astype(np.float32).astype(ml_dtypes.bfloat16).astype(np.float64)
+
+    index = np.arange(64)
+    col_phase = 2.0 * np.pi * ((index[:, None] * np.arange(KW)[None, :]) % W) / W
+    forward_cols = np.stack([np.cos(col_phase), -np.sin(col_phase)], axis=1) / math.sqrt(W)
+    doubling = np.where(np.arange(KW) == 0, 1.0, 2.0)[:, None]
+    inverse_cols = (
+        np.stack([np.cos(col_phase).T * doubling, -np.sin(col_phase).T * doubling], axis=0)
+        / math.sqrt(W)
+    )
+    modes = np.arange(KH)
+    row_freq = np.where(modes < KH // 2, modes, H - KH + modes)
+    row_phase = 2.0 * np.pi * ((row_freq[:, None] * index[None, :]) % H) / H
+    cosine = np.cos(row_phase) / math.sqrt(H)
+    sine = np.sin(row_phase) / math.sqrt(H)
+    forward_rows = np.stack([np.stack([cosine, sine], -1), np.stack([-sine, cosine], -1)], 1)
+    inverse_rows = np.stack(
+        [np.stack([cosine.T, -sine.T], -1), np.stack([sine.T, cosine.T], -1)], 1
+    )
+    return [low(table) for table in (forward_cols, inverse_cols, forward_rows, inverse_rows)]
+
+
+def matrix_tables():
+    forward_cols, inverse_cols, forward_rows, inverse_rows = plain_tables()
+    eye = np.eye(8)
+    into = np.einsum("wpk,gh->kpghw", forward_cols, eye).reshape(512, 512)
+    outof = np.einsum("pkw,gh->gwkph", inverse_cols, eye).reshape(512, 512)
+    pair = np.eye(2)
+    rows_in = np.einsum("jphq,ab->apjbqh", forward_rows, pair).reshape(128, 256)
+    rows_out = np.einsum("hpjq,ab->aphbqj", inverse_rows, pair).reshape(256, 128)
+    return [
+        jnp.asarray(np.ascontiguousarray(table).astype(ml_dtypes.bfloat16))
+        for table in (into, outof, rows_in, rows_out, outof.T, into.T, rows_out.T, rows_in.T)
+    ]
+
+
+def big_matrices(weight):
+    four = weight.reshape(GROUPS, 2, BS, 2, BS)
+    eye = jnp.eye(2, dtype=weight.dtype)
+    real = (four[:, :, :, 0][:, :, :, None, :] * eye[None, :, None, :, None]).reshape(
+        GROUPS, 128, 128
+    )
+    imag = (four[:, :, :, 1][:, :, :, None, :] * eye[None, :, None, :, None]).reshape(
+        GROUPS, 128, 128
+    )
+    upper = jnp.concatenate([real, imag], -1)
+    lower = jnp.concatenate([-imag, real], -1)
+    return jnp.concatenate([upper, lower], 1)
+
+
+def big_bias(bias):
+    return bias.reshape(GROUPS, 2, 2, BS).transpose(0, 2, 1, 3).reshape(GROUPS, 1, 256)
+
+
+def small_matrix(big):
+    parts = big.reshape(GROUPS, 2, 2, BS, 2, 2, BS)
+    kept = jnp.stack([parts[:, :, c, :, :, c] for c in range(2)], 1)
+    real = kept[:, :, 0, :, 0] + kept[:, :, 1, :, 1]
+    imag = kept[:, :, 0, :, 1] - kept[:, :, 1, :, 0]
+    return jnp.concatenate([real, imag], -1).reshape(D, 2 * BS)
+
+
+def small_bias(big):
+    summed = jnp.sum(big, axis=1)
+    return summed.reshape(GROUPS, 2, 2, BS).transpose(0, 2, 1, 3).reshape(NB, 2 * BS)
+
+
+def mm(left, right):
+    return jnp.dot(left, right, preferred_element_type=F32)
+
+
+def normalize(values):
+    center = values - jnp.mean(values, axis=-1, keepdims=True)
+    spread = jnp.mean(center * center, axis=-1, keepdims=True)
+    scale = lax.rsqrt(spread + EPSILON)
+    return center * scale, scale
+
+
+def normalize_back(grad, unit, scale, gain_row):
+    inner = grad * gain_row
+    return scale * (
+        inner
+        - jnp.mean(inner, axis=-1, keepdims=True)
+        - unit * jnp.mean(inner * unit, axis=-1, keepdims=True)
+    )
+
+
+def folded(values):
+    return jnp.sum(values.reshape(values.shape[0] // 8, 8, values.shape[1]), axis=0)
+
+
+def gelu_of(v):
+    return 0.5 * v * (1.0 + jnp.tanh(v * (GELU_A + GELU_B * (v * v))))
+
+
+def gelu_and_slope(v):
+    square = v * v
+    bend = jnp.tanh(v * (GELU_A + GELU_B * square))
+    half = 0.5 * (1.0 + bend)
+    slope = half + 0.5 * v * (1.0 - bend * bend) * (GELU_A + 3.0 * GELU_B * square)
+    return v * half, slope
+
+
+def flat(block):
+    return block.reshape(-1, block.shape[-1])
+
+
+def cols_in(table, rows, store, at):
+    halves = [mm(table, rows[half * 512 : (half + 1) * 512]).reshape(64, 8, D) for half in range(2)]
+    store[:, pl.ds(at, HB), :] = jnp.concatenate(halves, axis=1).astype(BF)
+
+
+def cols_out(table, store, at):
+    block = store[:, pl.ds(at, HB), :].astype(F32)
+    return jnp.concatenate(
+        [
+            mm(table, block[:, half * 8 : half * 8 + 8].reshape(512, D).astype(BF))
+            for half in range(2)
+        ],
+        axis=0,
+    )
+
+
+def lanes_of(rows, group):
+    lanes = slice(group * 128, group * 128 + 128)
+    return jnp.concatenate(
+        [rows[:, :32, lanes].reshape(KB * 32, 128), rows[:, 32:, lanes].reshape(KB * 32, 128)],
+        axis=1,
+    )
+
+
+def put_lanes(store, group, values):
+    lanes = slice(group * 128, group * 128 + 128)
+    store[:, :32, lanes] = values[:, :128].reshape(KB, 32, 128)
+    store[:, 32:, lanes] = values[:, 128:].reshape(KB, 32, 128)
+
+
+def spectral_forward_kernel(
+    x_ref, gain, shift, into, outof, rows_in, rows_out, w1, b1, w2, b2, mid_ref, spec_ref, cols, mixed
+):
+    step = pl.program_id(1)
+    n_rows, n_freq = H // HB, KW // KB
+
+    @pl.when(step < n_rows)
+    def _():
+        unit, _ = normalize(flat(x_ref[...]).astype(F32))
+        normed = unit * gain[...] + shift[...]
+        cols_in(into[...], normed.astype(BF), cols, pl.multiple_of(step * HB, HB))
+
+    @pl.when((step >= n_rows) & (step < n_rows + n_freq))
+    def _():
+        first_plane = (step - n_rows) * (2 * KB)
+        for two in range(KB // 2):
+            planes = cols[pl.ds(first_plane + 4 * two, 4)]
+            spec_ref[0, 2 * two : 2 * two + 2] = (
+                mm(rows_in[...], planes.reshape(256, D)).astype(BF).reshape(2, 64, D)
+            )
+        modes = spec_ref[0]
+        for group in range(GROUPS):
+            first = mm(lanes_of(modes, group), w1[group]) + b1[group]
+            second = mm(gelu_of(first).astype(BF), w2[group]) + b2[group]
+            shrunk = second - THRESHOLD * jnp.tanh(second * (1.0 / THRESHOLD))
+            put_lanes(mixed, group, shrunk.astype(BF))
+        for two in range(KB // 2):
+            planes = mixed[2 * two : 2 * two + 2].reshape(128, D)
+            cols[pl.ds(first_plane + 4 * two, 4)] = (
+                mm(rows_out[...], planes).astype(BF).reshape(4, 64, D)
+            )
+
+    @pl.when(step >= n_rows + n_freq)
+    def _():
+        block = step - n_rows - n_freq
+        x = flat(x_ref[...]).astype(F32)
+        unit, _ = normalize(x)
+        normed = unit * gain[...] + shift[...]
+        filtered = cols_out(outof[...], cols, pl.multiple_of(block * HB, HB))
+        mid_ref[...] = (x + filtered + normed).astype(mid_ref.dtype).reshape(mid_ref.shape)
+
+
+def spectral_backward_kernel(
+    x_ref, grad_ref, spec_ref, gain, outof_t, into_t, rows_out_t, rows_in_t,
+    w1, b1, w2, b2, w1_t, w2_t,
+    new_ref, dw1, db1, dw2, db2, dgain, dshift, cols, mixed, kept,
+):
+    step = pl.program_id(0)
+    n_rows, n_freq = H // HB, KW // KB
+
+    @pl.when(step == 0)
+    def _():
+        for ref in (dw1, db1, dw2, db2, dgain, dshift):
+            ref[...] = jnp.zeros_like(ref)
+
+    @pl.when(step < n_rows)
+    def _():
+        cols_in(outof_t[...], flat(grad_ref[...]), cols, pl.multiple_of(step * HB, HB))
+
+    @pl.when((step >= n_rows) & (step < n_rows + n_freq))
+    def _():
+        first_plane = (step - n_rows) * (2 * KB)
+        for two in range(KB // 2):
+            planes = cols[pl.ds(first_plane + 4 * two, 4)]
+            kept[2 * two : 2 * two + 2] = mm(rows_out_t[...], planes.reshape(256, D)).reshape(
+                2, 64, D
+            )
+        modes = spec_ref[0]
+        grads = kept[...]
+        for group in range(GROUPS):
+            mode = lanes_of(modes, group)
+            first = mm(mode, w1[group]) + b1[group]
+            active, slope = gelu_and_slope(first)
+            active = active.astype(BF)
+            second = mm(active, w2[group]) + b2[group]
+            bend = jnp.tanh(second * (1.0 / THRESHOLD))
+            d_second = bend * bend * lanes_of(grads, group)
+            db2[group] += folded(d_second)
+            d_second = d_second.astype(BF)
+            dw2[group] += mm(active.T, d_second)
+            d_first = slope * mm(d_second, w2_t[group])
+            db1[group] += folded(d_first)
+            d_first = d_first.astype(BF)
+            dw1[group] += mm(mode.T, d_first)
+            put_lanes(mixed, group, mm(d_first, w1_t[group]).astype(BF))
+        for two in range(KB // 2):
+            planes = mixed[2 * two : 2 * two + 2].reshape(128, D)
+            cols[pl.ds(first_plane + 4 * two, 4)] = (
+                mm(rows_in_t[...], planes).astype(BF).reshape(4, 64, D)
+            )
+
+    @pl.when(step >= n_rows + n_freq)
+    def _():
+        block = step - n_rows - n_freq
+        unit, scale = normalize(flat(x_ref[...]).astype(F32))
+        mid_grad = flat(grad_ref[...]).astype(F32)
+        grad = cols_out(into_t[...], cols, pl.multiple_of(block * HB, HB)) + mid_grad
+        dgain[...] += folded(grad * unit)
+        dshift[...] += folded(grad)
+        new = mid_grad + normalize_back(grad, unit, scale, gain[...])
+        new_ref[...] = new.astype(new_ref.dtype).reshape(new_ref.shape)
+
+
+def feed_forward_kernel(mid_ref, gain, shift, w_in, b_in, w_out, b_out, out_ref, pre_ref):
+    middle = flat(mid_ref[...]).astype(F32)
+    unit, _ = normalize(middle)
+    lowered = (unit * gain[...] + shift[...]).astype(BF)
+    total = middle + b_out[...]
+    for part in range(FF // FC):
+        at = slice(part * FC, part * FC + FC)
+        pre = mm(lowered, w_in[:, at]) + b_in[:, at]
+        pre_ref[0, :, at] = pre.astype(BF)
+        total += mm(gelu_of(pre).astype(BF), w_out[at, :])
+    out_ref[...] = total.astype(out_ref.dtype).reshape(out_ref.shape)
+
+
+def feed_backward_kernel(with_start, *refs):
+    (g_ref, mid_ref, pre_ref, gain, shift, w_out_t, w_in_t), refs = refs[:7], refs[7:]
+    if with_start:
+        (start_in, start_out), refs = refs[:2], refs[2:]
+    mid_grad_ref, dw_in, dw_out, db_in, db_out, dgain, dshift = refs
+    step = pl.program_id(0)
+
+    @pl.when(step == 0)
+    def _():
+        for ref in (db_in, db_out, dgain, dshift):
+            ref[...] = jnp.zeros_like(ref)
+        if with_start:
+            dw_in[...] = start_in[...]
+            dw_out[...] = start_out[...]
+        else:
+            dw_in[...] = jnp.zeros_like(dw_in)
+            dw_out[...] = jnp.zeros_like(dw_out)
+
+    upstream = flat(g_ref[...])
+    unit, scale = normalize(flat(mid_ref[...]).astype(F32))
+    lowered = (unit * gain[...] + shift[...]).astype(BF)
+    db_out[...] += folded(upstream.astype(F32))
+    upstream_t = upstream.T
+    lowered_t = lowered.T
+    low_grad = jnp.zeros((TT, D), F32)
+    for part in range(FF // FC):
+        at = slice(part * FC, part * FC + FC)
+        active, slope = gelu_and_slope(pre_ref[0, :, at].astype(F32))
+        dw_out[:, at] += mm(upstream_t, active.astype(BF))
+        pre_grad = slope * mm(upstream, w_out_t[:, at])
+        db_in[:, at] += folded(pre_grad)
+        pre_grad = pre_grad.astype(BF)
+        dw_in[:, at] += mm(lowered_t, pre_grad)
+        low_grad += mm(pre_grad, w_in_t[at, :])
+    dgain[...] += folded(low_grad * unit)
+    dshift[...] += folded(low_grad)
+    new = upstream.astype(F32) + normalize_back(low_grad, unit, scale, gain[...])
+    mid_grad_ref[...] = new.astype(mid_grad_ref.dtype).reshape(mid_grad_ref.shape)
+
+
+def whole(array, grid_rank):
+    zeros = (0,) * array.ndim
+    return pl.BlockSpec(array.shape, lambda *_: zeros, pipeline_mode=pl.Buffered(1))
+
+
+def rows_spec(shape, rows, item_of, block_of):
+    if len(shape) == 3:
+        return pl.BlockSpec((1, rows * W, D), lambda *at: (item_of(*at), block_of(*at), 0))
+    own = shape[2]
+    if own <= rows:
+        return pl.BlockSpec(
+            (rows // own, 1, own, W, D), lambda *at: (block_of(*at), item_of(*at), 0, 0, 0)
+        )
+    parts = own // rows
+    return pl.BlockSpec(
+        (1, 1, rows, W, D),
+        lambda *at: (block_of(*at) // parts, item_of(*at), block_of(*at) % parts, 0, 0),
+    )
+
+
+def params(rank):
+    return pltpu.CompilerParams(
+        dimension_semantics=("arbitrary",) * rank, vmem_limit_bytes=VMEM
+    )
+
+
+N_ROWS, N_FREQ = H // HB, KW // KB
+SPECTRAL_STEPS = 2 * N_ROWS + N_FREQ
+
+
+def both_ends(step):
+    return jnp.where(
+        step < N_ROWS, step, jnp.where(step < N_ROWS + N_FREQ, 0, step - N_ROWS - N_FREQ)
+    )
+
+
+def last_end(step):
+    return jnp.maximum(step - N_ROWS - N_FREQ, 0)
+
+
+def middle_part(step):
+    return jnp.clip(step - N_ROWS, 0, N_FREQ - 1)
+
+
+def spectral_forward(x, items, gain, shift, tables, mix):
+    small = (gain, shift, *tables[:4], *mix[:4])
+    return pl.pallas_call(
+        spectral_forward_kernel,
+        grid=(items, SPECTRAL_STEPS),
+        in_specs=[rows_spec(x.shape, HB, lambda i, s: i, lambda i, s: both_ends(s))]
+        + [whole(array, 2) for array in small],
+        out_specs=[
+            pl.BlockSpec((1, HB * W, D), lambda i, s: (i, last_end(s), 0)),
+            pl.BlockSpec((1, KB, 64, D), lambda i, s: (i, middle_part(s), 0, 0)),
+        ],
+        out_shape=[
+            jax.ShapeDtypeStruct((items, H * W, D), BF),
+            jax.ShapeDtypeStruct((items, KW, 64, D), BF),
+        ],
+        scratch_shapes=[pltpu.VMEM((64, 64, D), BF), pltpu.VMEM((KB, 64, D), BF)],
+        compiler_params=params(2),
+        cost_estimate=pl.CostEstimate(
+            flops=items * 12_000_000_000, bytes_accessed=items * 14_000_000, transcendentals=0
+        ),
+        name="spectral_forward",
+    )(x, *small)
+
+
+def spectral_backward(x, item_x, grad, spec, item, gain, tables, mix, out_shape):
+    small = (gain, *tables[4:], *mix)
+    rows = functools.partial(rows_spec, rows=HB)
+    sums = [(GROUPS, 256, 256), (GROUPS, 8, 256)] * 2 + [(8, D)] * 2
+    return pl.pallas_call(
+        spectral_backward_kernel,
+        grid=(SPECTRAL_STEPS,),
+        in_specs=[
+            rows_spec(x.shape, HB, lambda s: item_x, both_ends),
+            rows_spec(grad.shape, HB, lambda s: 0, both_ends),
+            pl.BlockSpec((1, KB, 64, D), lambda s: (item, middle_part(s), 0, 0)),
+        ]
+        + [whole(array, 1) for array in small],
+        out_specs=[rows_spec(out_shape, HB, lambda s: 0, last_end)]
+        + [pl.BlockSpec(dims, lambda s, rank=len(dims): (0,) * rank) for dims in sums],
+        out_shape=[jax.ShapeDtypeStruct(out_shape, BF)]
+        + [jax.ShapeDtypeStruct(dims, F32) for dims in sums],
+        scratch_shapes=[
+            pltpu.VMEM((64, 64, D), BF),
+            pltpu.VMEM((KB, 64, D), BF),
+            pltpu.VMEM((KB, 64, D), F32),
+        ],
+        compiler_params=params(1),
+        cost_estimate=pl.CostEstimate(
+            flops=20_000_000_000, bytes_accessed=20_000_000, transcendentals=0
+        ),
+        name="spectral_backward",
+    )(x, grad, spec, *small)
+
+
+def feed_forward(middle, gain, shift, w_in, b_in, w_out, b_out, out_shape):
+    items = middle.shape[0]
+    small = (gain, shift, w_in, b_in, w_out, b_out)
+    rows = TT // W
+    return pl.pallas_call(
+        feed_forward_kernel,
+        grid=(items, H * W // TT),
+        in_specs=[pl.BlockSpec((1, TT, D), lambda i, s: (i, s, 0))]
+        + [whole(array, 2) for array in small],
+        out_specs=[
+            rows_spec(out_shape, rows, lambda i, s: i, lambda i, s: s),
+            pl.BlockSpec((1, TT, FF), lambda i, s: (i, s, 0)),
+        ],
+        out_shape=[
+            jax.ShapeDtypeStruct(out_shape, BF),
+            jax.ShapeDtypeStruct((items, H * W, FF), BF),
+        ],
+        compiler_params=params(2),
+        cost_estimate=pl.CostEstimate(
+            flops=items * 20_000_000_000, bytes_accessed=items * 25_000_000, transcendentals=0
+        ),
+        name="feed_forward",
+    )(middle, *small)
+
+
+def feed_backward(g, item_g, middle, pre, item, gain, shift, w_out_t, w_in_t, start):
+    small = (gain, shift, w_out_t, w_in_t) + start
+    rows = TT // W
+    sums = [(D, FF), (D, FF), (8, FF), (8, D), (8, D), (8, D)]
+    return pl.pallas_call(
+        functools.partial(feed_backward_kernel, len(start) > 0),
+        grid=(H * W // TT,),
+        in_specs=[
+            rows_spec(g.shape, rows, lambda s: item_g, lambda s: s),
+            pl.BlockSpec((1, TT, D), lambda s: (item, s, 0)),
+            pl.BlockSpec((1, TT, FF), lambda s: (item, s, 0)),
+        ]
+        + [whole(array, 1) for array in small],
+        out_specs=[pl.BlockSpec((1, TT, D), lambda s: (0, s, 0))]
+        + [pl.BlockSpec(dims, lambda s: (0, 0)) for dims in sums],
+        out_shape=[jax.ShapeDtypeStruct((1, H * W, D), BF)]
+        + [jax.ShapeDtypeStruct(dims, F32) for dims in sums],
+        compiler_params=params(1),
+        cost_estimate=pl.CostEstimate(
+            flops=45_000_000_000, bytes_accessed=60_000_000, transcendentals=0
+        ),
+        name="feed_backward",
+    )(g, middle, pre, *small)
+
+
+def exchange(array):
+    return lax.all_to_all(array, "wide", split_axis=0, concat_axis=0, tiled=True)
+
+
+def after(array, other):
+    return lax.optimization_barrier((array, other))[0]
+
+
+def traded(kept, sent, axis_name, bit):
+    size = lax.axis_size(axis_name)
+    arrived = lax.ppermute(sent.astype(BF), axis_name, [(i, i ^ (1 << bit)) for i in range(size)])
+    return kept.astype(F32) + arrived.astype(F32)
+
+
+def own_bit(axis_name, bit):
+    return (lax.axis_index(axis_name) >> bit) & 1
+
+
+def reversed_bits(value, bits):
+    return sum(((value >> bit) & 1) << (bits - 1 - bit) for bit in range(bits))
+
+
+def summed_shard(array):
+    rep_bits = lax.axis_size("rep").bit_length() - 1
+    wide_bits = lax.axis_size("wide").bit_length() - 1
+    shard = array.shape[0] >> wide_bits
+    for bit in range(rep_bits):
+        mine, half = own_bit("rep", bit), array.shape[1] // 2
+        array = traded(
+            lax.dynamic_slice_in_dim(array, mine * half, half, 1),
+            lax.dynamic_slice_in_dim(array, (1 - mine) * half, half, 1),
+            "rep",
+            bit,
+        )
+    columns = array.shape[1]
+    for bit in range(wide_bits):
+        mine = own_bit("wide", bit)
+        blocks = array.reshape(-1, 2, shard, columns)
+        array = traded(
+            lax.dynamic_slice_in_dim(blocks, mine, 1, 1),
+            lax.dynamic_slice_in_dim(blocks, 1 - mine, 1, 1),
+            "wide",
+            bit,
+        )
+    gathered = lax.all_gather(array.reshape(shard, columns).astype(BF), "rep")
+    return jnp.concatenate(
+        [gathered[reversed_bits(block, rep_bits)] for block in range(1 << rep_bits)], axis=1
+    ).astype(F32)
+
+
+def whole_items(
+    tokens, cotangent, norm_gain, norm_shift, mix_in, mix_in_bias, mix_out, mix_out_bias,
+    w_in, b_in, w_out, b_out,
+):
+    wide = lax.axis_size("wide")
+    rows = tokens.shape[1]
+    items = tokens.shape[0] // wide
+    abroad = (wide, items, rows, W, D)
+    arrived = exchange(tokens.reshape(abroad))
+    upstream = exchange(after(cotangent.astype(BF).reshape(abroad), arrived))
+    tables = matrix_tables()
+    first_mats = [big_matrices(mix_in[layer]) for layer in range(LAYERS)]
+    second_mats = [big_matrices(mix_out[layer]) for layer in range(LAYERS)]
+    mixes = [
+        (
+            first_mats[layer],
+            big_bias(mix_in_bias[layer]),
+            second_mats[layer],
+            big_bias(mix_out_bias[layer]),
+            first_mats[layer].transpose(0, 2, 1),
+            second_mats[layer].transpose(0, 2, 1),
+        )
+        for layer in range(LAYERS)
+    ]
+
+    def row(array, *at):
+        return array[at].reshape(1, -1)
+
+    current = arrived
+    stored = []
+    for layer in range(LAYERS):
+        middle, spec = spectral_forward(
+            current, items, row(norm_gain, layer, 0), row(norm_shift, layer, 0), tables, mixes[layer]
+        )
+        following, pre = feed_forward(
+            middle, row(norm_gain, layer, 1), row(norm_shift, layer, 1), w_in[layer],
+            row(b_in, layer), w_out[layer], row(b_out, layer),
+            abroad if layer == LAYERS - 1 else (items, H * W, D),
+        )
+        stored.append((current, middle, spec, pre))
+        current = following
+    output = exchange(current).reshape(tokens.shape).astype(F32)
+
+    sums = [None] * LAYERS
+    matrices = [()] * LAYERS
+    returned = []
+    for item in range(items):
+        grad, item_grad = upstream, item
+        for layer in reversed(range(LAYERS)):
+            layer_input, middle, spec, pre = stored[layer]
+            mid_grad, dw_in, dw_out, *ff_sums = feed_backward(
+                grad, item_grad, middle, pre, item, row(norm_gain, layer, 1),
+                row(norm_shift, layer, 1), w_out[layer].T, w_in[layer].T, matrices[layer],
+            )
+            matrices[layer] = (dw_in, dw_out)
+            grad, *mix_sums = spectral_backward(
+                layer_input, item, mid_grad, spec, item, row(norm_gain, layer, 0), tables,
+                mixes[layer], (1, H * W, D) if layer else (wide, 1, rows, W, D),
+            )
+            item_grad = 0
+            own = ff_sums + mix_sums
+            sums[layer] = own if item == 0 else [a + b for a, b in zip(sums[layer], own)]
+        returned.append(exchange(grad))
+    input_grad = jnp.concatenate(returned, axis=1).reshape(tokens.shape).astype(F32)
+
+    shards = []
+    for layer in reversed(range(LAYERS)):
+        parts = list(matrices[layer])
+        if layer == 0:
+            for slot in (4, 6):
+                parts += [small_matrix(sums[each][slot]) for each in range(LAYERS)]
+        shards.append(summed_shard(jnp.concatenate(parts, axis=1)))
+    shards.reverse()
+    w_in_grad = jnp.stack([shard[:, :FF] for shard in shards])
+    w_out_grad = jnp.stack([shard[:, FF : 2 * FF].T for shard in shards])
+    mix_grads = shards[0][:, 2 * FF :].reshape(-1, 2, LAYERS, 2 * BS).transpose(1, 2, 0, 3)
+
+    def of_both(slot, change):
+        return jnp.stack([change(sums[layer][slot]) for layer in range(LAYERS)])
+
+    def line(array):
+        return jnp.sum(array, axis=0)
+
+    gain_grad, shift_grad, in_bias, out_bias, b_in_grad, b_out_grad = lax.psum(
+        (
+            jnp.stack([of_both(8, line), of_both(2, line)], axis=1),
+            jnp.stack([of_both(9, line), of_both(3, line)], axis=1),
+            of_both(5, small_bias),
+            of_both(7, small_bias),
+            of_both(0, line),
+            of_both(1, line),
+        ),
+        ("wide", "rep"),
+    )
+    return (
+        output, input_grad, gain_grad, shift_grad, mix_grads[0], in_bias, mix_grads[1], out_bias,
+        w_in_grad, b_in_grad, w_out_grad, b_out_grad,
+    )
+
+
+def power_of_two(number):
+    return number > 0 and number & (number - 1) == 0
+
+
+def any_size(tokens, *others):
+    wide, rep = lax.axis_size("wide"), lax.axis_size("rep")
+    if tokens.shape[0] % wide == 0 and power_of_two(wide) and power_of_two(rep) and wide <= 16:
+        return whole_items(tokens, *others)
+    return body(tokens, *others)
+
+
 def solution(mesh):
     placed = (
         P("rep", "wide", None, None),
@@ -369,7 +991,7 @@
         P(),
     )
     return jax.shard_map(
-        body,
+        any_size,
         mesh=mesh,
         in_specs=placed,
         out_specs=(

time: 3980 us -> 1090 us (0.27)
  local copies, waits for them, and re-layouts: 1120 us -> 81.1 us
  blocking collectives: 1040 us -> 129 us
  matrix products: 703 us -> 0 us
  Pallas kernels: 0 us -> 527 us
  waiting for transfers between devices: 751 us -> 244 us
  other arithmetic: 294 us -> 61.1 us
    dot_general x56 -> x0, matrix products: 703 us -> none  [the longest x2 127 us: body(): jnp.einsum('irwd,fd->irwf', branch_grad, w_out[depth_index], preferred_el...]
    all_to_all x3 -> x0, blocking collectives: 562 us -> none  [the longest x1 188 us: body(): lax.all_to_all(mode_inverse(second, inverse_rows), 'wide', split_axis=2,...]
    pallas_call x0 -> x12, Pallas kernels: none -> 527 us  [the longest x4 238 us: feed_backward(): pl.pallas_call(functools.partial(feed_backward_kernel, len(start) > 0), g...]
    reshape x22 -> x14, local copies, waits for them, and re-layouts: 510 us -> 8.12 us  [the longest x4 4.95 us: small_matrix(): parts = big.reshape(GROUPS, 2, 2, BS, 2, 2, BS)]
    all_to_all x5, waiting for transfers between devices: 684 us -> 196 us  [exchange(): lax.all_to_all(array, 'wide', split_axis=0, concat_axis=0, tiled=True)]
    unnamed x1 -> x0, blocking collectives: 438 us -> none
    convert_element_type x17 -> x10, local copies, waits for them, and re-layouts: 351 us -> 7.34 us  [traded(): sent.astype(BF)]
    transpose x6 -> x4, local copies, waits for them, and re-layouts: 185 us -> 0.03 us  [small_bias(): summed.reshape(GROUPS, 2, 2, BS).transpose(0, 2, 1, 3).reshape(NB, 2 * BS)]
  transfers between devices with their start and end apart: 10 -> 15, of which waited for: 6 -> 7; matrix products, arithmetic and copies ran while one was open for 6% -> 11% of each run, Pallas kernels for 0% -> 49%
where the time goes in v1:
time: 1090 us; the launch traced here: 1080 us
  Pallas kernels  527 us (48%)
  waiting for transfers between devices  244 us (22%)
  blocking collectives  129 us (12%)
  local copies, waits for them, and re-layouts  81.1 us (7%)
  other arithmetic  61.1 us (6%)
  starting transfers between devices  38.1 us (3%)
    pallas_call x4, Pallas kernels, feed_backward(): pl.pallas_call(functools.partial(feed_backward_kernel, len(start) > 0), g...  238 us
    all_to_all x5, waiting for transfers between devices, exchange(): lax.all_to_all(array, 'wide', split_axis=0, concat_axis=0, tiled=True)  196 us
    pallas_call x4, Pallas kernels, spectral_backward(): pl.pallas_call(spectral_backward_kernel, grid=(SPECTRAL_STEPS,), in_specs...  115 us
    psum x1, blocking collectives, whole_items(): lax.psum((jnp.stack([of_both(8, line), of_both(2, line)], axis=1), jnp.st...  114 us
    pallas_call x2, Pallas kernels, feed_forward(): pl.pallas_call(feed_forward_kernel, grid=(items, H * W // TT), in_specs=[...  105 us
    pallas_call x2, Pallas kernels, spectral_forward(): pl.pallas_call(spectral_forward_kernel, grid=(items, SPECTRAL_STEPS), in_...  69.3 us
    ppermute x10, waiting for transfers between devices, traded(): lax.ppermute(sent.astype(BF), axis_name, [(i, i ^ 1 << bit) for i in rang...  47.9 us
    all_to_all x5, starting transfers between devices, exchange(): lax.all_to_all(array, 'wide', split_axis=0, concat_axis=0, tiled=True)  30 us
  transfers between devices with their start and end apart: 15, of which 7 were waited for; matrix products, arithmetic and copies ran while one was open for 11% of the time, Pallas kernels for 49%

profile of v1, /device:TPU:0, one launch (start us, length us, event | category | flops | bytes accessed | tf_op | source)
XLA Modules:
  0.0 1082.6 jit_solution(13612149743267250435)
XLA Ops:
  0.7 7.4 all-to-all-start
  14.6 1.2 fusion.22
  17.8 9.1 convert_element_type.138
  26.9 164.3 %all-to-all-done.x_ref = bf16[8,2,8,64,512]{4,3,2,1,0:T(8,128)(2,1)} async-done(((bf16[8,2,8,64,512]{4,3,2,1,0:T(8,128)(2,1)}), bf16[8,2,8,64,512]{4,3,2,1,0:T(8,128)(2,1)}, u32[]{:S(2)}, u32[]{:S(2)}) %all-to-all-start) | async-done | bytes 8388640 | tf_op jit(solution)/shard_map/all_to_all | solution.py:818
  191.2 5.3 all-to-all-start.2
  198.1 1.2 fusion.20
  199.3 1.0 copy.187.w1
  202.8 5.3 fusion.29
  208.1 3.9 copy.229
  212.1 6.1 fusion.28
  218.2 3.9 copy.228
  222.1 2.4 copy.227
  224.5 4.0 copy.226
  230.3 34.6 %spectral_forward.2 = (bf16[2,4096,512]{2,1,0:T(8,128)(2,1)}, bf16[2,32,64,512]{3,2,1,0:T(8,128)(2,1)}) custom-call(bf16[8,2,8,64,512]{4,3,2,1,0:T(8,128)(2,1)} %all-to-all-done.x_ref, f32[1,512]{1,0:T(1,128)} %get-tuple-element.281.gain, f32[1,512]{1,0:T(1,128)} %get-tuple-element.264.shift, bf16[512,512]{1,0:T(8,128)(2,1)} %constant.49.clone.into, ...), custom_call_target="tpu_custom_call" | custom-call | flops 24000000000 | bytes 28000000 | tf_op jit(solution)/shard_map/spectral_forward/pallas_call | solution.py:715
  264.9 52.6 %feed_forward.2 = (bf16[2,4096,512]{2,1,0:T(8,128)(2,1)}, bf16[2,4096,2048]{2,1,0:T(8,128)(2,1)}) custom-call(bf16[2,4096,512]{2,1,0:T(8,128)(2,1)} %get-tuple-element.77.mid_ref.refs_1_, f32[1,512]{1,0:T(1,128)} %get-tuple-element.282.gain.refs_3_, f32[1,512]{1,0:T(1,128)} %get-tuple-element.263.shift.refs_4_, bf16[512,2048]{1,0:T(8,128)(2,1)} %get-tuple-element.193.w_in, ...), custom_call_target="tpu_custom_call" | custom-call | flops 40000000000 | bytes 50000000 | tf_op jit(solution)/shard_map/feed_forward/pallas_call | solution.py:771
  317.5 34.7 %spectral_forward.3 = (bf16[2,4096,512]{2,1,0:T(8,128)(2,1)}, bf16[2,32,64,512]{3,2,1,0:T(8,128)(2,1)}) custom-call(bf16[2,4096,512]{2,1,0:T(8,128)(2,1)} %get-tuple-element.78.x_ref, f32[1,512]{1,0:T(1,128)} %get-tuple-element.280.gain, f32[1,512]{1,0:T(1,128)} %get-tuple-element.265.shift, bf16[512,512]{1,0:T(8,128)(2,1)} %constant.49.clone.into, ...), custom_call_target="tpu_custom_call" | custom-call | flops 24000000000 | bytes 28000000 | tf_op jit(solution)/shard_map/spectral_forward/pallas_call | solution.py:715
  352.2 52.6 %feed_forward.3 = (bf16[8,2,8,64,512]{4,3,2,1,0:T(8,128)(2,1)}, bf16[2,4096,2048]{2,1,0:T(8,128)(2,1)}) custom-call(bf16[2,4096,512]{2,1,0:T(8,128)(2,1)} %get-tuple-element.79.mid_ref.refs_1_, f32[1,512]{1,0:T(1,128)} %get-tuple-element.283.gain.refs_3_, f32[1,512]{1,0:T(1,128)} %get-tuple-element.262.shift.refs_4_, ...), custom_call_target="tpu_custom_call" | custom-call | flops 40000000000 | bytes 50000000 | tf_op jit(solution)/shard_map/feed_forward/pallas_call | solution.py:771
  404.9 6.4 all-to-all-start.1
  411.3 58.1 %feed_backward.4 = (bf16[1,4096,512]{2,1,0:T(8,128)(2,1)}, f32[512,2048]{1,0:T(8,128)}, f32[512,2048]{1,0:T(8,128)}, f32[8,2048]{1,0:T(8,128)}, f32[8,512]{1,0:T...) custom-call(bf16[8,2,8,64,512]{4,3,2,1,0:T(8,128)(2,1)} %all-to-all-done.2.refs_0_, ...), custom_call_target="tpu_custom_call" | custom-call | flops 44999999488 | bytes 60000000 | tf_op jit(solution)/shard_map/feed_backward/pallas_call | solution.py:796
  469.4 28.5 %spectral_backward.4 = (bf16[1,4096,512]{2,1,0:T(8,128)(2,1)}, f32[4,256,256]{2,1,0:T(8,128)}, f32[4,8,256]{2,1,0:T(8,128)}, f32[4,256,256]{2,1,0:T(8,128)}, f32...) custom-call(bf16[2,4096,512]{2,1,0:T(8,128)(2,1)} %get-tuple-element.78.x_ref, ...), custom_call_target="tpu_custom_call" | custom-call | flops 20000000000 | bytes 20000000 | tf_op jit(solution)/shard_map/spectral_backward/pallas_call | solution.py:741
  498.0 60.7 %feed_backward.6 = (bf16[1,4096,512]{2,1,0:T(8,128)(2,1)}, f32[512,2048]{1,0:T(8,128)}, f32[512,2048]{1,0:T(8,128)}, f32[8,2048]{1,0:T(8,128)}, f32[8,512]{1,0:T...) custom-call(bf16[8,2,8,64,512]{4,3,2,1,0:T(8,128)(2,1)} %all-to-all-done.2.refs_0_, ...), custom_call_target="tpu_custom_call" | custom-call | flops 44999999488 | bytes 60000000 | tf_op jit(solution)/shard_map/feed_backward/pallas_call | solution.py:796
  558.7 28.8 %spectral_backward.6 = (bf16[1,4096,512]{2,1,0:T(8,128)(2,1)}, f32[4,256,256]{2,1,0:T(8,128)}, f32[4,8,256]{2,1,0:T(8,128)}, f32[4,256,256]{2,1,0:T(8,128)}, f32...) custom-call(bf16[2,4096,512]{2,1,0:T(8,128)(2,1)} %get-tuple-element.78.x_ref, ...), custom_call_target="tpu_custom_call" | custom-call | flops 20000000000 | bytes 20000000 | tf_op jit(solution)/shard_map/spectral_backward/pallas_call | solution.py:741
  587.5 1.4 add.198
  588.9 1.2 reshape.198
  590.1 1.0 fusion.30
  592.9 58.2 %feed_backward.5 = (bf16[1,4096,512]{2,1,0:T(8,128)(2,1)}, f32[512,2048]{1,0:T(8,128)}, f32[512,2048]{1,0:T(8,128)}, f32[8,2048]{1,0:T(8,128)}, f32[8,512]{1,0:T...) custom-call(bf16[1,4096,512]{2,1,0:T(8,128)(2,1)} %get-tuple-element.85.refs_0_, ...), custom_call_target="tpu_custom_call" | custom-call | flops 44999999488 | bytes 60000000 | tf_op jit(solution)/shard_map/feed_backward/pallas_call | solution.py:796
  651.1 28.8 %spectral_backward.5 = (bf16[8,1,8,64,512]{4,3,2,1,0:T(8,128)(2,1)}, f32[4,256,256]{2,1,0:T(8,128)}, f32[4,8,256]{2,1,0:T(8,128)}, f32[4,256,256]{2,1,0:T(8,128)...) custom-call(bf16[8,2,8,64,512]{4,3,2,1,0:T(8,128)(2,1)} %all-to-all-done.x_ref, ...), custom_call_target="tpu_custom_call" | custom-call | flops 20000000000 | bytes 20000000 | tf_op jit(solution)/shard_map/spectral_backward/pallas_call | solution.py:741
  679.9 60.5 %feed_backward.7 = (bf16[1,4096,512]{2,1,0:T(8,128)(2,1)}, f32[512,2048]{1,0:T(8,128)}, f32[512,2048]{1,0:T(8,128)}, f32[8,2048]{1,0:T(8,128)}, f32[8,512]{1,0:T...) custom-call(bf16[1,4096,512]{2,1,0:T(8,128)(2,1)} %get-tuple-element.93.refs_0_, ...), custom_call_target="tpu_custom_call" | custom-call | flops 44999999488 | bytes 60000000 | tf_op jit(solution)/shard_map/feed_backward/pallas_call | solution.py:796
  740.4 28.7 %spectral_backward.7 = (bf16[8,1,8,64,512]{4,3,2,1,0:T(8,128)(2,1)}, f32[4,256,256]{2,1,0:T(8,128)}, f32[4,8,256]{2,1,0:T(8,128)}, f32[4,256,256]{2,1,0:T(8,128)...) custom-call(bf16[8,2,8,64,512]{4,3,2,1,0:T(8,128)(2,1)} %all-to-all-done.x_ref, ...), custom_call_target="tpu_custom_call" | custom-call | flops 20000000000 | bytes 20000000 | tf_op jit(solution)/shard_map/spectral_backward/pallas_call | solution.py:741
  769.1 1.4 add.195
  770.5 1.2 reshape.197
  772.7 1.0 fusion.9
  774.7 1.2 reshape.196
  776.0 1.0 fusion.32
  778.8 1.2 reshape.195
  782.3 10.9 %concatenate.73 = f32[512,4608]{1,0:T(8,128)} concatenate(f32[512,2048]{1,0:T(8,128)} %get-tuple-element.114, f32[512,2048]{1,0:T(8,128)} %get-tuple-element.115, f32[512,64]{1,0:T(8,128)S(1)} %bitcast.211, f32[512,64]{1,0:T(8,128)S(1)} %bitcast.212, f32[512,64]{1,0:T(8,128)S(1)} %bitcast.216, f32[512,64]{1,0:T(8,128)S(1)} %bitcast.215, f32[512,64]{1,0:T(8,128)S(1)} %bitcast.209, ...), dimensions={1} | concatenate | bytes 18874368 | tf_op jit(solution)/shard_map/concatenate | solution.py:938
  793.2 6.0 all-to-all-start.3
  799.2 4.1 dynamic-slice_convert_fusion
  803.8 1.7 copy-done.2
  806.0 3.3 copy-done.1
  809.6 1.8 dynamic-slice_convert_fusion.1
  813.3 12.2 %bitcast_convert_fusion.1 = f32[16,8,64,512]{3,2,1,0:T(8,128)} fusion(bf16[8,2,8,64,512]{4,3,2,1,0:T(8,128)(2,1)} %all-to-all-done.1), kind=kLoop, calls=%fused_computation.2 | loop fusion | flops 4194304 | bytes 25165824 | tf_op jit(solution)/shard_map/convert_element_type | solution.py:908
  825.5 3.6 convert_add_fusion.1
  829.2 1.6 collective-permute-start.6
  830.9 2.4 convert_add_fusion
  834.0 21.4 %collective-permute-done.6 = bf16[512,1024]{1,0:T(8,128)(2,1)S(1)} collective-permute-done((bf16[512,1024]{1,0:T(8,128)(2,1)S(1)}, bf16[512,1024]{1,0:T(8,128)(2,1)S(1)}, u32[]{:S(2)}, u32[]{:S(2)}) %collective-permute-start.6) | collective-permute-done | bytes 1048608 | tf_op jit(solution)/shard_map/ppermute | solution.py:827
  856.5 2.0 collective-permute-start.7
  858.5 31.9 %all-to-all-done.3 = bf16[8,1,8,64,512]{4,3,2,1,0:T(8,128)(2,1)} async-done(((bf16[8,1,8,64,512]{4,3,2,1,0:T(8,128)(2,1)}), bf16[8,1,8,64,512]{4,3,2,1,0:T(8,128)(2,1)}, u32[]{:S(2)}, u32[]{:S(2)}) %all-to-all-start.3) | async-done | bytes 4194336 | tf_op jit(solution)/shard_map/all_to_all | solution.py:818
  890.5 4.9 all-to-all-start.4
  895.5 113.5 %all-reduce = (f32[2,2,512]{2,0,1:T(2,128)S(1)}, f32[2,2,512]{2,0,1:T(2,128)S(1)}, f32[2,8,128]{2,1,0:T(8,128)}, f32[2,8,128]{2,1,0:T(8,128)}, f32[2,2048]{1,0:T(2,128)}, /*index=5*/f32[2,512]{1,0:T(2,128)}) all-reduce(f32[2,2,512]{2,0,1:T(2,128)S(1)} %pad_maximum_fusion.11, ...), channel_id=1, replica_groups=mesh['wide'=8,'rep'=4] {'wide','rep'}, use_global_device_ids=true, to_apply=%region_4.0 | all-reduce | flops 13312 | bytes 106496 | tf_op jit(solution)/shard_map/psum | solution.py:950
  1010.3 1.2 convert_add_fusion.5
  1011.6 2.2 convert_add_fusion.2
  1013.8 4.9 collective-permute-done.8
  1018.8 1.2 collective-permute-start.9
  1020.1 1.4 collective-permute-start.2
  1021.4 4.5 collective-permute-done.9
  1026.0 8.1 all-gather.1
  1035.2 8.5 collective-permute-done.3
  1044.0 8.6 collective-permute-done.4
  1052.6 7.2 all-gather
  1060.7 1.0 pad_maximum_fusion.2
  1061.7 1.0 pad_maximum_fusion.1
  1062.8 7.6 pad_maximum_fusion
  1070.3 12.0 %bitcast_convert_fusion = f32[16,8,64,512]{3,2,1,0:T(8,128)} fusion(bf16[8,2,8,64,512]{4,3,2,1,0:T(8,128)(2,1)} %pad_maximum_fusion), kind=kLoop, calls=%fused_computation.1 | loop fusion | flops 4194304 | bytes 25165824 | tf_op jit(solution)/shard_map/convert_element_type | solution.py:930
  (267 shorter events, 30.2 us)
Async XLA Ops:
  0.6 7.4 copy-start.15
  0.7 190.6 %all-to-all-start = ((bf16[8,2,8,64,512]{4,3,2,1,0:T(8,128)(2,1)}), bf16[8,2,8,64,512]{4,3,2,1,0:T(8,128)(2,1)}, u32[]{:S(2)}, u32[]{:S(2)}) async-start(bf16[8,2,8,64,512]{4,3,2,1,0:T(8,128)(2,1)} %bitcast.184), calls=%async_computation | async-start | bytes 16777216 | tf_op jit(solution)/shard_map/all_to_all | solution.py:818
  191.2 5.3 copy-start.50
  191.2 6.1 copy-start.51
  191.2 213.7 %all-to-all-start.2 = ((bf16[8,2,8,64,512]{4,3,2,1,0:T(8,128)(2,1)}), bf16[8,2,8,64,512]{4,3,2,1,0:T(8,128)(2,1)}, u32[]{:S(2)}, u32[]{:S(2)}) async-start(bf16[8,2,8,64,512]{4,3,2,1,0:T(8,128)(2,1)} %bitcast.181), calls=%async_computation.2 | async-start | bytes 16777216 | tf_op jit(solution)/shard_map/all_to_all | solution.py:818
  222.1 6.4 copy-start.54
  222.1 7.0 copy-start.52
  222.1 7.0 copy-start.53
  222.1 7.6 copy-start.29
  404.9 388.3 %all-to-all-start.1 = ((bf16[8,2,8,64,512]{4,3,2,1,0:T(8,128)(2,1)}), bf16[8,2,8,64,512]{4,3,2,1,0:T(8,128)(2,1)}, u32[]{:S(2)}, u32[]{:S(2)}) async-start(bf16[8,2,8,64,512]{4,3,2,1,0:T(8,128)(2,1)} %get-tuple-element.80), calls=%async_computation.1 | async-start | bytes 16777216 | tf_op jit(solution)/shard_map/all_to_all | solution.py:818
  558.7 28.8 %copy-start.14 = (f32[4,256,256]{2,1,0:T(8,128)S(1)}, f32[4,256,256]{2,1,0:T(8,128)}, u32[]{:S(2)}) copy-start(f32[4,256,256]{2,1,0:T(8,128)} %get-tuple-element.122) | copy-start | bytes 3145732
  740.4 28.7 %copy-start.13 = (f32[4,256,256]{2,1,0:T(8,128)S(1)}, f32[4,256,256]{2,1,0:T(8,128)}, u32[]{:S(2)}) copy-start(f32[4,256,256]{2,1,0:T(8,128)} %get-tuple-element.120) | copy-start | bytes 3145732
  771.7 2.9 copy-start.9
  771.7 2.8 copy-start.10
  775.9 2.8 copy-start.11
  775.9 2.7 copy-start.12
  793.2 97.3 %all-to-all-start.3 = ((bf16[8,1,8,64,512]{4,3,2,1,0:T(8,128)(2,1)}), bf16[8,1,8,64,512]{4,3,2,1,0:T(8,128)(2,1)}, u32[]{:S(2)}, u32[]{:S(2)}) async-start(bf16[8,1,8,64,512]{4,3,2,1,0:T(8,128)(2,1)} %get-tuple-element.89), calls=%async_computation.3 | async-start | bytes 8388608 | tf_op jit(solution)/shard_map/all_to_all | solution.py:818
  799.2 4.2 copy-start.3
  803.3 27.5 %collective-permute-start = (bf16[512,2304]{1,0:T(8,128)(2,1)}, bf16[512,2304]{1,0:T(8,128)(2,1)}, u32[]{:S(2)}, u32[]{:S(2)}) collective-permute-start(bf16[512,2304]{1,0:T(8,128)(2,1)} %dynamic-slice_convert_fusion), channel_id=1, source_target_pairs={{0,1},{1,0},{2,3},{3,2},{4,5},{5,4},{6,7},{7,6},{8,9},{9,8},{10,11... | collective-permute-start | bytes 7077896 | tf_op jit(solution)/shard_map/ppermute | solution.py:827
  806.0 3.3 copy-start.1
  809.3 2.8 copy-start.22
  809.3 2.8 copy-start.24
  809.3 3.0 copy-start.25
  809.4 3.0 copy-start.27
  809.4 3.2 copy-start.21
  809.4 3.2 copy-start.23
  809.4 3.4 copy-start.48
  809.4 3.4 copy-start.49
  809.4 3.4 copy-start.38
  809.4 3.4 copy-start.41
  809.4 3.4 copy-start.45
  809.4 3.4 copy-start.46
  809.4 3.4 copy-start.35
  809.5 3.4 copy-start.36
  809.5 3.5 copy-start.44
  809.5 3.5 copy-start.47
  809.5 3.5 copy-start.34
  809.5 3.5 copy-start.37
  809.5 3.6 copy-start.40
  809.5 3.6 copy-start.43
  809.5 3.6 copy-start.31
  809.5 3.6 copy-start.33
  809.5 3.6 copy-start.39
  809.6 3.6 copy-start.42
  809.6 3.6 copy-start.30
  809.6 3.6 copy-start.32
  809.6 3.6 copy-start.19
  809.6 3.6 copy-start.20
  811.4 14.1 %collective-permute-start.5 = (bf16[512,2048]{1,0:T(8,128)(2,1)}, bf16[512,2048]{1,0:T(8,128)(2,1)}, u32[]{:S(2)}, u32[]{:S(2)}) collective-permute-start(bf16[512,2048]{1,0:T(8,128)(2,1)} %dynamic-slice_convert_fusion.1), channel_id=1, source_target_pairs={{0,1},{1,0},{2,3},{3,2},{4,5},{5,4},{6,7},{7,6},{8,9},{9,8},{10,11... | collective-permute-start | bytes 6291464 | tf_op jit(solution)/shard_map/ppermute | solution.py:827
  813.3 17.5 %slice-start = ((s8[9437184]{0:T(1024)(128)(4,1)}), s8[4194304]{0:T(1024)(128)(4,1)S(1)}, s32[]{:S(2)}) async-start(s8[9437184]{0:T(1024)(128)(4,1)} %bitcast.182), calls=%async_computation.5 | async-start | bytes 8388608
  813.3 17.5 %slice-start.1 = ((s8[9437184]{0:T(1024)(128)(4,1)}), s8[1048576]{0:T(1024)(128)(4,1)S(1)}, s32[]{:S(2)}) async-start(s8[9437184]{0:T(1024)(128)(4,1)} %bitcast.182), calls=%async_computation.6 | async-start | bytes 2097152
  825.5 5.4 slice-start.2
  829.2 26.1 %collective-permute-start.6 = (bf16[512,1024]{1,0:T(8,128)(2,1)S(1)}, bf16[512,1024]{1,0:T(8,128)(2,1)S(1)}, u32[]{:S(2)}, u32[]{:S(2)}) collective-permute-start(bf16[512,1024]{1,0:T(8,128)(2,1)S(1)} %dynamic-slice_convert_fusion.3), channel_id=1, source_target_pairs={{0,2},{1,3},{2,0},{3,1},{4,6},{5,7},{6,4},{7,5},{8,10},{9,11},{10,... | collective-permute-start | bytes 3145736 | tf_op jit(solution)/shard_map/ppermute | solution.py:827
  833.2 23.3 %copy-start = (f32[512,2304]{1,0:T(8,128)}, f32[512,2304]{1,0:T(8,128)S(1)}, u32[]{:S(2)}) copy-start(f32[512,2304]{1,0:T(8,128)S(1)} %convert_add_fusion) | copy-start | bytes 14155780
  833.4 178.2 %collective-permute-start.1 = (bf16[512,1152]{1,0:T(8,128)(2,1)S(1)}, bf16[512,1152]{1,0:T(8,128)(2,1)}, u32[]{:S(2)}, u32[]{:S(2)}) collective-permute-start(bf16[512,1152]{1,0:T(8,128)(2,1)S(1)} %dynamic-slice_convert_fusion.2), channel_id=1, source_target_pairs={{0,2},{1,3},{2,0},{3,1},{4,6},{5,7},{6,4},{7,5},{8,10},{9,11},{10,... | collective-permute-start | bytes 3538952 | tf_op jit(solution)/shard_map/ppermute | solution.py:827
  856.5 153.7 %collective-permute-start.7 = (bf16[4,1,64,1024]{3,2,1,0:T(8,128)(2,1)}, bf16[4,1,64,1024]{3,2,1,0:T(8,128)(2,1)}, u32[]{:S(2)}, u32[]{:S(2)}) collective-permute-start(bf16[4,1,64,1024]{3,2,1,0:T(8,128)(2,1)} %dynamic-slice_convert_fusion.5), channel_id=1, source_target_pairs={{0,4},{4,0},{8,12},{12,8},{16,20},{20,16},{24,28},{28,24},{1,5},{5... | collective-permute-start | bytes 1572872 | tf_op jit(solution)/shard_map/ppermute | solution.py:827
  890.5 5.0 copy-start.17
  890.5 5.0 copy-start.18
  890.5 172.3 %all-to-all-start.4 = ((bf16[8,1,8,64,512]{4,3,2,1,0:T(8,128)(2,1)}), bf16[8,1,8,64,512]{4,3,2,1,0:T(8,128)(2,1)}, u32[]{:S(2)}, u32[]{:S(2)}) async-start(bf16[8,1,8,64,512]{4,3,2,1,0:T(8,128)(2,1)} %get-tuple-element.97), calls=%async_computation.4 | async-start | bytes 8388608 | tf_op jit(solution)/shard_map/all_to_all | solution.py:818
  1011.5 7.2 collective-permute-start.8
  1018.8 7.2 collective-permute-start.9
  1020.1 14.1 %collective-permute-start.2 = (bf16[4,1,64,1152]{3,2,1,0:T(8,128)(2,1)S(1)}, bf16[4,1,64,1152]{3,2,1,0:T(8,128)(2,1)S(1)}, u32[]{:S(2)}, u32[]{:S(2)}) collective-permute-start(bf16[4,1,64,1152]{3,2,1,0:T(8,128)(2,1)S(1)} %dynamic-slice_convert_fusion.4), channel_id=1, source_target_pairs={{0,4},{4,0},{8,12},{12,8},{16,20},{20,16},{24,28},{28,24},{1,5},{5... | collective-permute-start | bytes 1769480 | tf_op jit(solution)/shard_map/ppermute | solution.py:827
  1034.4 9.3 collective-permute-start.3
  1043.8 8.7 collective-permute-start.4
  (9 other events, 19.2 us)

commit v2 on v1

--- a/solution.py
+++ b/solution.py
@@ -365,9 +365,9 @@
 GELU_A = math.sqrt(2.0 / math.pi)
 GELU_B = GELU_A * 0.044715
 HB = 16
-KB = 8
+KB = 16
 TT = 512
-FC = 512
+FC = 1024
 VMEM = 58 * 1024 * 1024
 
 
@@ -427,21 +427,17 @@
     return bias.reshape(GROUPS, 2, 2, BS).transpose(0, 2, 1, 3).reshape(GROUPS, 1, 256)
 
 
-def small_matrix(big):
-    parts = big.reshape(GROUPS, 2, 2, BS, 2, 2, BS)
-    kept = jnp.stack([parts[:, :, c, :, :, c] for c in range(2)], 1)
-    real = kept[:, :, 0, :, 0] + kept[:, :, 1, :, 1]
-    imag = kept[:, :, 0, :, 1] - kept[:, :, 1, :, 0]
-    return jnp.concatenate([real, imag], -1).reshape(D, 2 * BS)
-
-
-def small_bias(big):
-    summed = jnp.sum(big, axis=1)
-    return summed.reshape(GROUPS, 2, 2, BS).transpose(0, 2, 1, 3).reshape(NB, 2 * BS)
+def small_bias(line):
+    parts = line.reshape(-1, GROUPS, 2, 2, BS).transpose(0, 1, 3, 2, 4)
+    return parts.reshape(-1, NB, 2 * BS)
 
 
 def mm(left, right):
     return jnp.dot(left, right, preferred_element_type=F32)
+
+
+def mm_t(left, right):
+    return lax.dot_general(left, right, (((1,), (1,)), ((), ())), preferred_element_type=F32)
 
 
 def normalize(values):
@@ -474,10 +470,6 @@
     half = 0.5 * (1.0 + bend)
     slope = half + 0.5 * v * (1.0 - bend * bend) * (GELU_A + 3.0 * GELU_B * square)
     return v * half, slope
-
-
-def flat(block):
-    return block.reshape(-1, block.shape[-1])
 
 
 def cols_in(table, rows, store, at):
@@ -511,14 +503,17 @@
 
 
 def spectral_forward_kernel(
-    x_ref, gain, shift, into, outof, rows_in, rows_out, w1, b1, w2, b2, mid_ref, spec_ref, cols, mixed
+    x_ref, gain, shift, into, outof, rows_in, rows_out, w1, b1, w2, b2, mid_ref, spec_ref,
+    cols, mixed, held,
 ):
-    step = pl.program_id(1)
+    step = pl.program_id(0)
     n_rows, n_freq = H // HB, KW // KB
 
     @pl.when(step < n_rows)
     def _():
-        unit, _ = normalize(flat(x_ref[...]).astype(F32))
+        x = lines_of(x_ref)
+        held[step] = x
+        unit, _ = normalize(x.astype(F32))
         normed = unit * gain[...] + shift[...]
         cols_in(into[...], normed.astype(BF), cols, pl.multiple_of(step * HB, HB))
 
@@ -527,10 +522,10 @@
         first_plane = (step - n_rows) * (2 * KB)
         for two in range(KB // 2):
             planes = cols[pl.ds(first_plane + 4 * two, 4)]
-            spec_ref[0, 2 * two : 2 * two + 2] = (
+            spec_ref[2 * two : 2 * two + 2] = (
                 mm(rows_in[...], planes.reshape(256, D)).astype(BF).reshape(2, 64, D)
             )
-        modes = spec_ref[0]
+        modes = spec_ref[...]
         for group in range(GROUPS):
             first = mm(lanes_of(modes, group), w1[group]) + b1[group]
             second = mm(gelu_of(first).astype(BF), w2[group]) + b2[group]
@@ -545,29 +540,48 @@
     @pl.when(step >= n_rows + n_freq)
     def _():
         block = step - n_rows - n_freq
-        x = flat(x_ref[...]).astype(F32)
+        x = held[block].astype(F32)
         unit, _ = normalize(x)
         normed = unit * gain[...] + shift[...]
         filtered = cols_out(outof[...], cols, pl.multiple_of(block * HB, HB))
-        mid_ref[...] = (x + filtered + normed).astype(mid_ref.dtype).reshape(mid_ref.shape)
-
-
-def spectral_backward_kernel(
-    x_ref, grad_ref, spec_ref, gain, outof_t, into_t, rows_out_t, rows_in_t,
-    w1, b1, w2, b2, w1_t, w2_t,
-    new_ref, dw1, db1, dw2, db2, dgain, dshift, cols, mixed, kept,
-):
+        mid_ref[...] = (x + filtered + normed).astype(mid_ref.dtype)
+
+
+def compact(big):
+    low_lanes = lax.broadcasted_iota(jnp.int32, (BS, 128), 1) < BS
+    parts = []
+    for c in range(2):
+        real_rows, imag_rows = slice(c * BS, c * BS + BS), slice(128 + c * BS, 128 + c * BS + BS)
+        real = big[real_rows, :128] + big[imag_rows, 128:]
+        imag = big[real_rows, 128:] - big[imag_rows, :128]
+        if c == 0:
+            parts.append(jnp.where(low_lanes, real, pltpu.roll(imag, BS, 1)))
+        else:
+            parts.append(jnp.where(low_lanes, pltpu.roll(real, BS, 1), imag))
+    return jnp.concatenate(parts, axis=0)
+
+
+def spectral_backward_kernel(with_start, *refs):
+    (
+        x_ref, grad_ref, spec_ref, gain, outof_t, into_t, rows_out_t, rows_in_t,
+        w1, b1, w2, b2, w1_t, w2_t,
+    ), refs = refs[:14], refs[14:]
+    starts, refs = refs[:2] if with_start else (), refs[2:] if with_start else refs
+    new_ref, blocks, lines, dw1, dw2, cols, mixed, kept, held = refs
     step = pl.program_id(0)
     n_rows, n_freq = H // HB, KW // KB
 
     @pl.when(step == 0)
     def _():
-        for ref in (dw1, db1, dw2, db2, dgain, dshift):
+        lines[...] = starts[1][...] if with_start else jnp.zeros_like(lines)
+        for ref in (dw1, dw2):
             ref[...] = jnp.zeros_like(ref)
 
     @pl.when(step < n_rows)
     def _():
-        cols_in(outof_t[...], flat(grad_ref[...]), cols, pl.multiple_of(step * HB, HB))
+        grad = grad_ref[...]
+        held[step] = grad
+        cols_in(outof_t[...], grad, cols, pl.multiple_of(step * HB, HB))
 
     @pl.when((step >= n_rows) & (step < n_rows + n_freq))
     def _():
@@ -577,7 +591,7 @@
             kept[2 * two : 2 * two + 2] = mm(rows_out_t[...], planes.reshape(256, D)).reshape(
                 2, 64, D
             )
-        modes = spec_ref[0]
+        modes = spec_ref[...]
         grads = kept[...]
         for group in range(GROUPS):
             mode = lanes_of(modes, group)
@@ -587,11 +601,12 @@
             second = mm(active, w2[group]) + b2[group]
             bend = jnp.tanh(second * (1.0 / THRESHOLD))
             d_second = bend * bend * lanes_of(grads, group)
-            db2[group] += folded(d_second)
+            at = slice(group * 256, group * 256 + 256)
+            lines[:, 1024 + group * 256 : 1280 + group * 256] += folded(d_second)
             d_second = d_second.astype(BF)
             dw2[group] += mm(active.T, d_second)
             d_first = slope * mm(d_second, w2_t[group])
-            db1[group] += folded(d_first)
+            lines[:, at] += folded(d_first)
             d_first = d_first.astype(BF)
             dw1[group] += mm(mode.T, d_first)
             put_lanes(mixed, group, mm(d_first, w1_t[group]).astype(BF))
@@ -601,105 +616,116 @@
                 mm(rows_in_t[...], planes).astype(BF).reshape(4, 64, D)
             )
 
+    @pl.when(step == n_rows + n_freq)
+    def _():
+        for group in range(GROUPS):
+            at = slice(group * 128, group * 128 + 128)
+            for slot, ref in enumerate((dw1, dw2)):
+                lanes = slice(slot * 128, slot * 128 + 128)
+                block = compact(ref[group])
+                blocks[at, lanes] = block + starts[0][at, lanes] if with_start else block
+
     @pl.when(step >= n_rows + n_freq)
     def _():
         block = step - n_rows - n_freq
-        unit, scale = normalize(flat(x_ref[...]).astype(F32))
-        mid_grad = flat(grad_ref[...]).astype(F32)
+        unit, scale = normalize(lines_of(x_ref).astype(F32))
+        mid_grad = held[block].astype(F32)
         grad = cols_out(into_t[...], cols, pl.multiple_of(block * HB, HB)) + mid_grad
-        dgain[...] += folded(grad * unit)
-        dshift[...] += folded(grad)
+        lines[:, 2048:2560] += folded(grad * unit)
+        lines[:, 2560:3072] += folded(grad)
         new = mid_grad + normalize_back(grad, unit, scale, gain[...])
-        new_ref[...] = new.astype(new_ref.dtype).reshape(new_ref.shape)
-
-
-def feed_forward_kernel(mid_ref, gain, shift, w_in, b_in, w_out, b_out, out_ref, pre_ref):
-    middle = flat(mid_ref[...]).astype(F32)
+        new_ref[...] = new.astype(new_ref.dtype)
+
+
+def feed_forward_kernel(mid_ref, gain, shift, w_in, b_in, w_out, b_out, *refs):
+    out_ref, pre_ref = refs[-2:]
+    middle = mid_ref[...].astype(F32)
     unit, _ = normalize(middle)
     lowered = (unit * gain[...] + shift[...]).astype(BF)
     total = middle + b_out[...]
     for part in range(FF // FC):
         at = slice(part * FC, part * FC + FC)
         pre = mm(lowered, w_in[:, at]) + b_in[:, at]
-        pre_ref[0, :, at] = pre.astype(BF)
-        total += mm(gelu_of(pre).astype(BF), w_out[at, :])
-    out_ref[...] = total.astype(out_ref.dtype).reshape(out_ref.shape)
+        pre = pre.astype(BF)
+        pre_ref[:, at] = pre
+        total += mm(gelu_of(pre), w_out[at, :])
+    out_ref[...] = total.astype(out_ref.dtype)
 
 
 def feed_backward_kernel(with_start, *refs):
-    (g_ref, mid_ref, pre_ref, gain, shift, w_out_t, w_in_t), refs = refs[:7], refs[7:]
+    (g_ref, mid_ref, pre_ref, gain, shift, w_out, w_in), refs = refs[:7], refs[7:]
     if with_start:
-        (start_in, start_out), refs = refs[:2], refs[2:]
-    mid_grad_ref, dw_in, dw_out, db_in, db_out, dgain, dshift = refs
+        (start_far, start_lines, mid_grad_ref, sent, lines, dw, start, arrival) = refs
+        copy = pltpu.make_async_copy(start_far, start, arrival)
+    else:
+        mid_grad_ref, dw, lines = refs
     step = pl.program_id(0)
 
     @pl.when(step == 0)
     def _():
-        for ref in (db_in, db_out, dgain, dshift):
-            ref[...] = jnp.zeros_like(ref)
+        lines[...] = start_lines[...] if with_start else jnp.zeros_like(lines)
+        dw[...] = jnp.zeros_like(dw)
         if with_start:
-            dw_in[...] = start_in[...]
-            dw_out[...] = start_out[...]
-        else:
-            dw_in[...] = jnp.zeros_like(dw_in)
-            dw_out[...] = jnp.zeros_like(dw_out)
-
-    upstream = flat(g_ref[...])
-    unit, scale = normalize(flat(mid_ref[...]).astype(F32))
+            copy.start()
+
+    upstream = lines_of(g_ref)
+    unit, scale = normalize(mid_ref[...].astype(F32))
     lowered = (unit * gain[...] + shift[...]).astype(BF)
-    db_out[...] += folded(upstream.astype(F32))
+    lines[:, FF : FF + D] += folded(upstream.astype(F32))
     upstream_t = upstream.T
     lowered_t = lowered.T
     low_grad = jnp.zeros((TT, D), F32)
     for part in range(FF // FC):
         at = slice(part * FC, part * FC + FC)
-        active, slope = gelu_and_slope(pre_ref[0, :, at].astype(F32))
-        dw_out[:, at] += mm(upstream_t, active.astype(BF))
-        pre_grad = slope * mm(upstream, w_out_t[:, at])
-        db_in[:, at] += folded(pre_grad)
-        pre_grad = pre_grad.astype(BF)
-        dw_in[:, at] += mm(lowered_t, pre_grad)
-        low_grad += mm(pre_grad, w_in_t[at, :])
-    dgain[...] += folded(low_grad * unit)
-    dshift[...] += folded(low_grad)
+        active, slope = gelu_and_slope(pre_ref[:, at])
+        dw[:, FF + part * FC : FF + part * FC + FC] += mm(upstream_t, active)
+        pre_grad = slope * mm_t(upstream, w_out[at, :]).astype(BF)
+        lines[:, at] += folded(pre_grad.astype(F32))
+        dw[:, at] += mm(lowered_t, pre_grad)
+        low_grad += mm_t(pre_grad, w_in[:, at])
+    lines[:, FF + D : FF + 2 * D] += folded(low_grad * unit)
+    lines[:, FF + 2 * D : FF + 3 * D] += folded(low_grad)
     new = upstream.astype(F32) + normalize_back(low_grad, unit, scale, gain[...])
-    mid_grad_ref[...] = new.astype(mid_grad_ref.dtype).reshape(mid_grad_ref.shape)
-
-
-def whole(array, grid_rank):
+    mid_grad_ref[...] = new.astype(mid_grad_ref.dtype)
+    if with_start:
+
+        @pl.when(step == H * W // TT - 1)
+        def _():
+            copy.wait()
+            sent[...] = (dw[...] + start[...]).astype(BF)
+
+
+def whole(array):
     zeros = (0,) * array.ndim
     return pl.BlockSpec(array.shape, lambda *_: zeros, pipeline_mode=pl.Buffered(1))
 
 
-def rows_spec(shape, rows, item_of, block_of):
-    if len(shape) == 3:
-        return pl.BlockSpec((1, rows * W, D), lambda *at: (item_of(*at), block_of(*at), 0))
-    own = shape[2]
-    if own <= rows:
-        return pl.BlockSpec(
-            (rows // own, 1, own, W, D), lambda *at: (block_of(*at), item_of(*at), 0, 0, 0)
-        )
-    parts = own // rows
-    return pl.BlockSpec(
-        (1, 1, rows, W, D),
-        lambda *at: (block_of(*at) // parts, item_of(*at), block_of(*at) % parts, 0, 0),
-    )
-
-
-def params(rank):
-    return pltpu.CompilerParams(
-        dimension_semantics=("arbitrary",) * rank, vmem_limit_bytes=VMEM
-    )
+def of_layer(array, layer):
+    at = (layer,) + (0,) * (array.ndim - 1)
+    return pl.BlockSpec((None, *array.shape[1:]), lambda *_: at, pipeline_mode=pl.Buffered(1))
+
+
+def rows_spec(rows, block_of, array=None, kind=None):
+    if kind is None:
+        return pl.BlockSpec((rows * W, D), lambda s: (block_of(s), 0))
+    own = array.shape[2]
+    return pl.BlockSpec((rows * W // own, None, own, D), lambda s: (block_of(s), kind, 0, 0))
+
+
+def lines_of(ref):
+    return ref[...].reshape(-1, D)
+
+
+PARAMS = pltpu.CompilerParams(dimension_semantics=("arbitrary",), vmem_limit_bytes=VMEM)
+COST = pl.CostEstimate(flops=1_000_000, bytes_accessed=1_000_000, transcendentals=0)
 
 
 N_ROWS, N_FREQ = H // HB, KW // KB
 SPECTRAL_STEPS = 2 * N_ROWS + N_FREQ
 
 
-def both_ends(step):
-    return jnp.where(
-        step < N_ROWS, step, jnp.where(step < N_ROWS + N_FREQ, 0, step - N_ROWS - N_FREQ)
-    )
+def first_end(step):
+    return jnp.minimum(step, N_ROWS - 1)
 
 
 def last_end(step):
@@ -710,108 +736,151 @@
     return jnp.clip(step - N_ROWS, 0, N_FREQ - 1)
 
 
-def spectral_forward(x, items, gain, shift, tables, mix):
+def spectral_forward(x, kind, gain, shift, tables, mix):
     small = (gain, shift, *tables[:4], *mix[:4])
     return pl.pallas_call(
         spectral_forward_kernel,
-        grid=(items, SPECTRAL_STEPS),
-        in_specs=[rows_spec(x.shape, HB, lambda i, s: i, lambda i, s: both_ends(s))]
-        + [whole(array, 2) for array in small],
+        grid=(SPECTRAL_STEPS,),
+        in_specs=[rows_spec(HB, first_end, x, kind)] + [whole(array) for array in small],
         out_specs=[
-            pl.BlockSpec((1, HB * W, D), lambda i, s: (i, last_end(s), 0)),
-            pl.BlockSpec((1, KB, 64, D), lambda i, s: (i, middle_part(s), 0, 0)),
+            rows_spec(HB, last_end),
+            pl.BlockSpec((KB, 64, D), lambda s: (middle_part(s), 0, 0)),
         ],
         out_shape=[
-            jax.ShapeDtypeStruct((items, H * W, D), BF),
-            jax.ShapeDtypeStruct((items, KW, 64, D), BF),
+            jax.ShapeDtypeStruct((H * W, D), BF),
+            jax.ShapeDtypeStruct((KW, 64, D), BF),
         ],
-        scratch_shapes=[pltpu.VMEM((64, 64, D), BF), pltpu.VMEM((KB, 64, D), BF)],
-        compiler_params=params(2),
-        cost_estimate=pl.CostEstimate(
-            flops=items * 12_000_000_000, bytes_accessed=items * 14_000_000, transcendentals=0
-        ),
-        name="spectral_forward",
-    )(x, *small)
-
-
-def spectral_backward(x, item_x, grad, spec, item, gain, tables, mix, out_shape):
-    small = (gain, *tables[4:], *mix)
-    rows = functools.partial(rows_spec, rows=HB)
-    sums = [(GROUPS, 256, 256), (GROUPS, 8, 256)] * 2 + [(8, D)] * 2
-    return pl.pallas_call(
-        spectral_backward_kernel,
-        grid=(SPECTRAL_STEPS,),
-        in_specs=[
-            rows_spec(x.shape, HB, lambda s: item_x, both_ends),
-            rows_spec(grad.shape, HB, lambda s: 0, both_ends),
-            pl.BlockSpec((1, KB, 64, D), lambda s: (item, middle_part(s), 0, 0)),
-        ]
-        + [whole(array, 1) for array in small],
-        out_specs=[rows_spec(out_shape, HB, lambda s: 0, last_end)]
-        + [pl.BlockSpec(dims, lambda s, rank=len(dims): (0,) * rank) for dims in sums],
-        out_shape=[jax.ShapeDtypeStruct(out_shape, BF)]
-        + [jax.ShapeDtypeStruct(dims, F32) for dims in sums],
         scratch_shapes=[
             pltpu.VMEM((64, 64, D), BF),
             pltpu.VMEM((KB, 64, D), BF),
+            pltpu.VMEM((N_ROWS, HB * W, D), BF),
+        ],
+        compiler_params=PARAMS,
+        cost_estimate=COST,
+        name="spectral_forward",
+    )(x, *small)
+
+
+def spectral_backward(x, kind, grad, spec, gain, tables, mix, start):
+    small = (gain, *tables[4:], *mix, *start)
+    sums = [(D, 256), (8, 3072)]
+    return pl.pallas_call(
+        functools.partial(spectral_backward_kernel, len(start) > 0),
+        grid=(SPECTRAL_STEPS,),
+        in_specs=[
+            rows_spec(HB, last_end, x, kind),
+            rows_spec(HB, first_end),
+            pl.BlockSpec((KB, 64, D), lambda s: (middle_part(s), 0, 0)),
+        ]
+        + [whole(array) for array in small],
+        out_specs=[rows_spec(HB, last_end)] + [pl.BlockSpec(dims, lambda s: (0, 0)) for dims in sums],
+        out_shape=[jax.ShapeDtypeStruct((H * W, D), BF)]
+        + [jax.ShapeDtypeStruct(dims, F32) for dims in sums],
+        scratch_shapes=[
+            pltpu.VMEM((GROUPS, 256, 256), F32),
+            pltpu.VMEM((GROUPS, 256, 256), F32),
+            pltpu.VMEM((64, 64, D), BF),
+            pltpu.VMEM((KB, 64, D), BF),
             pltpu.VMEM((KB, 64, D), F32),
+            pltpu.VMEM((N_ROWS, HB * W, D), BF),
         ],
-        compiler_params=params(1),
-        cost_estimate=pl.CostEstimate(
-            flops=20_000_000_000, bytes_accessed=20_000_000, transcendentals=0
-        ),
+        compiler_params=PARAMS,
+        cost_estimate=COST,
         name="spectral_backward",
     )(x, grad, spec, *small)
 
 
-def feed_forward(middle, gain, shift, w_in, b_in, w_out, b_out, out_shape):
-    items = middle.shape[0]
-    small = (gain, shift, w_in, b_in, w_out, b_out)
-    rows = TT // W
+def feed_forward(middle, layer, gain, shift, w_in, b_in, w_out, b_out, abroad=None, onto=None):
+    rows = rows_spec(TT // W, lambda s: s)
+    shape = jax.ShapeDtypeStruct((H * W, D), BF)
+    if abroad is not None:
+        receivers, chunks, own, chunk = abroad
+        shape = jax.ShapeDtypeStruct((receivers, chunks, own * W, D), BF)
+        rows = pl.BlockSpec((None, None, TT, D), lambda s: (s, chunk, 0, 0))
+    more = [] if onto is None else [onto]
     return pl.pallas_call(
         feed_forward_kernel,
-        grid=(items, H * W // TT),
-        in_specs=[pl.BlockSpec((1, TT, D), lambda i, s: (i, s, 0))]
-        + [whole(array, 2) for array in small],
-        out_specs=[
-            rows_spec(out_shape, rows, lambda i, s: i, lambda i, s: s),
-            pl.BlockSpec((1, TT, FF), lambda i, s: (i, s, 0)),
-        ],
-        out_shape=[
-            jax.ShapeDtypeStruct(out_shape, BF),
-            jax.ShapeDtypeStruct((items, H * W, FF), BF),
-        ],
-        compiler_params=params(2),
-        cost_estimate=pl.CostEstimate(
-            flops=items * 20_000_000_000, bytes_accessed=items * 25_000_000, transcendentals=0
-        ),
+        grid=(H * W // TT,),
+        in_specs=[
+            rows_spec(TT // W, lambda s: s),
+            whole(gain),
+            whole(shift),
+            of_layer(w_in, layer),
+            whole(b_in),
+            of_layer(w_out, layer),
+            whole(b_out),
+        ]
+        + [pl.BlockSpec(memory_space=pl.ANY) for _ in more],
+        out_specs=[rows, pl.BlockSpec((TT, FF), lambda s: (s, 0))],
+        out_shape=[shape, jax.ShapeDtypeStruct((H * W, FF), BF)],
+        input_output_aliases={7: 0} if more else {},
+        compiler_params=PARAMS,
+        cost_estimate=COST,
         name="feed_forward",
-    )(middle, *small)
-
-
-def feed_backward(g, item_g, middle, pre, item, gain, shift, w_out_t, w_in_t, start):
-    small = (gain, shift, w_out_t, w_in_t) + start
-    rows = TT // W
-    sums = [(D, FF), (D, FF), (8, FF), (8, D), (8, D), (8, D)]
+    )(middle, gain, shift, w_in, b_in, w_out, b_out, *more)
+
+
+def start_of(fb):
+    return (fb[1], fb[2])
+
+
+def feed_backward(g, kind, middle, pre, layer, gain, shift, w_out, w_in, start):
+    sums = [(D, 2 * FF), (8, FF + 3 * D)]
     return pl.pallas_call(
         functools.partial(feed_backward_kernel, len(start) > 0),
         grid=(H * W // TT,),
         in_specs=[
-            rows_spec(g.shape, rows, lambda s: item_g, lambda s: s),
-            pl.BlockSpec((1, TT, D), lambda s: (item, s, 0)),
-            pl.BlockSpec((1, TT, FF), lambda s: (item, s, 0)),
+            rows_spec(TT // W, lambda s: s, g, kind),
+            rows_spec(TT // W, lambda s: s),
+            pl.BlockSpec((TT, FF), lambda s: (s, 0)),
+            whole(gain),
+            whole(shift),
+            of_layer(w_out, layer),
+            of_layer(w_in, layer),
         ]
-        + [whole(array, 1) for array in small],
-        out_specs=[pl.BlockSpec((1, TT, D), lambda s: (0, s, 0))]
+        + ([pl.BlockSpec(memory_space=pl.ANY), whole(start[1])] if start else []),
+        out_specs=[rows_spec(TT // W, lambda s: s)]
         + [pl.BlockSpec(dims, lambda s: (0, 0)) for dims in sums],
-        out_shape=[jax.ShapeDtypeStruct((1, H * W, D), BF)]
-        + [jax.ShapeDtypeStruct(dims, F32) for dims in sums],
-        compiler_params=params(1),
-        cost_estimate=pl.CostEstimate(
-            flops=45_000_000_000, bytes_accessed=60_000_000, transcendentals=0
+        out_shape=[
+            jax.ShapeDtypeStruct((H * W, D), BF),
+            jax.ShapeDtypeStruct(sums[0], BF if start else F32),
+            jax.ShapeDtypeStruct(sums[1], F32),
+        ],
+        scratch_shapes=[
+            pltpu.VMEM(sums[0], F32),
+            pltpu.VMEM(sums[0], F32),
+            pltpu.SemaphoreType.DMA,
+        ]
+        if start
+        else [],
+        compiler_params=PARAMS,
+        cost_estimate=COST,
+        name="feed_backward",
+    )(g, middle, pre, gain, shift, w_out, w_in, *start)
+
+
+def widen_kernel(part, *refs):
+    refs[-1][...] = part[...].astype(F32)
+
+
+def widened(part, chunk, chunks, onto):
+    items, parts = part.shape[:2]
+    block = (None, None, *part.shape[2:])
+    more = [] if onto is None else [onto]
+    return pl.pallas_call(
+        widen_kernel,
+        grid=(parts, items),
+        in_specs=[pl.BlockSpec(block, lambda p, s: (s, p, 0, 0, 0))]
+        + [pl.BlockSpec(memory_space=pl.ANY) for _ in more],
+        out_specs=pl.BlockSpec(block, lambda p, s: (chunk + p, s, 0, 0, 0)),
+        out_shape=jax.ShapeDtypeStruct((chunks, items, *part.shape[2:]), F32),
+        input_output_aliases={1: 0} if more else {},
+        compiler_params=pltpu.CompilerParams(
+            dimension_semantics=("arbitrary", "arbitrary"), vmem_limit_bytes=VMEM
         ),
-        name="feed_backward",
-    )(g, middle, pre, *small)
+        cost_estimate=COST,
+        name="widen",
+    )(part, *more)
 
 
 def exchange(array):
@@ -822,46 +891,62 @@
     return lax.optimization_barrier((array, other))[0]
 
 
-def traded(kept, sent, axis_name, bit):
+def swapped(array, axis_name, far):
     size = lax.axis_size(axis_name)
-    arrived = lax.ppermute(sent.astype(BF), axis_name, [(i, i ^ (1 << bit)) for i in range(size)])
-    return kept.astype(F32) + arrived.astype(F32)
-
-
-def own_bit(axis_name, bit):
-    return (lax.axis_index(axis_name) >> bit) & 1
+    return lax.ppermute(array, axis_name, [(i, i ^ far) for i in range(size)])
+
+
+def tree_sum(parts):
+    parts = [part.astype(F32) for part in parts]
+    while len(parts) > 1:
+        parts = [parts[at] + parts[at + 1] for at in range(0, len(parts), 2)]
+    return parts[0]
+
+
+def share(array, index, size, axis):
+    return lax.dynamic_slice_in_dim(array, index * size, size, axis)
+
+
+def own_half(array, axis_name, bit, axis):
+    mine, half = (lax.axis_index(axis_name) >> bit) & 1, array.shape[axis] // 2
+    other = share(array, 1 - mine, half, axis).astype(BF)
+    return tree_sum([share(array, mine, half, axis), swapped(other, axis_name, 1 << bit)])
+
+
+def own_rows(array, bits, parts):
+    for bit in bits:
+        blocks = array.reshape(parts // 2, 2, -1, array.shape[1])
+        array = own_half(blocks, "wide", bit, 1).reshape(-1, array.shape[1])
+        parts //= 2
+    return array
+
+
+def wide_step(blocks, packed, bit, wide):
+    mine = (lax.axis_index("wide") >> bit) & 1
+    halves = blocks.reshape(wide >> (bit + 1), 2, -1, 128)
+    own, other = (share(halves, at, 1, 1).reshape(-1, 128) for at in (mine, 1 - mine))
+    arrived = swapped(jnp.concatenate([other, packed]), "wide", 1 << bit)
+    return own + arrived[: own.shape[0]], packed + arrived[own.shape[0] :]
 
 
 def reversed_bits(value, bits):
     return sum(((value >> bit) & 1) << (bits - 1 - bit) for bit in range(bits))
 
 
-def summed_shard(array):
-    rep_bits = lax.axis_size("rep").bit_length() - 1
-    wide_bits = lax.axis_size("wide").bit_length() - 1
-    shard = array.shape[0] >> wide_bits
-    for bit in range(rep_bits):
-        mine, half = own_bit("rep", bit), array.shape[1] // 2
-        array = traded(
-            lax.dynamic_slice_in_dim(array, mine * half, half, 1),
-            lax.dynamic_slice_in_dim(array, (1 - mine) * half, half, 1),
-            "rep",
-            bit,
-        )
-    columns = array.shape[1]
-    for bit in range(wide_bits):
-        mine = own_bit("wide", bit)
-        blocks = array.reshape(-1, 2, shard, columns)
-        array = traded(
-            lax.dynamic_slice_in_dim(blocks, mine, 1, 1),
-            lax.dynamic_slice_in_dim(blocks, 1 - mine, 1, 1),
-            "wide",
-            bit,
-        )
-    gathered = lax.all_gather(array.reshape(shard, columns).astype(BF), "rep")
-    return jnp.concatenate(
-        [gathered[reversed_bits(block, rep_bits)] for block in range(1 << rep_bits)], axis=1
-    ).astype(F32)
+def gathered(array):
+    me = lax.axis_index("rep")
+    parts = [array]
+    for bit in reversed(range(lax.axis_size("rep").bit_length() - 1)):
+        mine = ((me >> bit) & 1) == 0
+        others = [swapped(part, "rep", 1 << bit) for part in (jnp.concatenate(parts, axis=1),)][0]
+        others = jnp.split(others, len(parts), axis=1)
+        parts = [
+            jnp.where(mine == (side == 0), part, other)
+            for side in range(2)
+            for part, other in zip(parts, others)
+        ]
+    bits = lax.axis_size("rep").bit_length() - 1
+    return [parts[reversed_bits(index, bits)] for index in range(len(parts))]
 
 
 def whole_items(
@@ -869,98 +954,186 @@
     w_in, b_in, w_out, b_out,
 ):
     wide = lax.axis_size("wide")
-    rows = tokens.shape[1]
-    items = tokens.shape[0] // wide
-    abroad = (wide, items, rows, W, D)
-    arrived = exchange(tokens.reshape(abroad))
-    upstream = exchange(after(cotangent.astype(BF).reshape(abroad), arrived))
+    chunks = tokens.shape[0] // wide
+    abroad = (wide, *tokens.shape[1:])
+
+    def rows_by_layer(array):
+        return [array[layer].reshape(-1, 1, array.shape[-1]) for layer in range(LAYERS)]
+
+    lines = [
+        [[line for line in group] for group in rows_by_layer(array)]
+        for array in (norm_gain, norm_shift, b_in, b_out)
+    ]
+
     tables = matrix_tables()
-    first_mats = [big_matrices(mix_in[layer]) for layer in range(LAYERS)]
-    second_mats = [big_matrices(mix_out[layer]) for layer in range(LAYERS)]
-    mixes = [
+    mixes = []
+    for layer in range(LAYERS):
+        first_mats, second_mats = big_matrices(mix_in[layer]), big_matrices(mix_out[layer])
+        mixes.append(
+            (
+                first_mats,
+                big_bias(mix_in_bias[layer]),
+                second_mats,
+                big_bias(mix_out_bias[layer]),
+                first_mats.transpose(0, 2, 1),
+                second_mats.transpose(0, 2, 1),
+            )
+        )
+
+    stored = {}
+    feed_sums = [()] * LAYERS
+    mix_sums = [()] * LAYERS
+    tie = lax.optimization_barrier
+
+    def rows_of(array, chunk):
+        return array[chunk * wide : chunk * wide + wide].astype(BF)
+
+    def forward(chunk, current, kind, onto):
+        for layer in range(LAYERS):
+            middle, spec = spectral_forward(
+                current, kind, gains[layer][0], shifts[layer][0], tables, mixes[layer]
+            )
+            last = layer == LAYERS - 1
+            following, pre = feed_forward(
+                middle, layer, gains[layer][1], shifts[layer][1], w_in,
+                in_biases[layer][0], w_out, out_biases[layer][0],
+                abroad=(wide, chunks, tokens.shape[1], chunk) if last else None,
+                onto=onto if last else None,
+            )
+            stored[layer, chunk] = (current, kind, middle, spec, pre)
+            current, kind = following, None
+        return current
+
+    def backward_feed(chunk, layer, grad, kind=None):
+        _, _, middle, _, pre = stored[layer, chunk]
+        mid_grad, *feed_sums[layer] = feed_backward(
+            grad, kind, middle, pre, layer, gains[layer][1], shifts[layer][1], w_out, w_in,
+            feed_sums[layer],
+        )
+        return mid_grad
+
+    def backward_spectral(chunk, layer, mid_grad):
+        layer_input, kind, _, spec, _ = stored[layer, chunk]
+        grad, *mix_sums[layer] = spectral_backward(
+            layer_input, kind, mid_grad, spec, gains[layer][0], tables, mixes[layer], mix_sums[layer]
+        )
+        return grad
+
+    def backward(chunk, layer, grad):
+        return backward_spectral(chunk, layer, backward_feed(chunk, layer, grad))
+
+    def as_item(array):
+        return array.reshape(H * W, D)
+
+    def one_part(array):
+        return array.reshape(wide, 1, *tokens.shape[1:])
+
+    def both(first, second):
+        return jnp.stack([first, second], axis=1).reshape(wide, 2, -1, D)
+
+    sent, tokens_here, cotangent_here = tie((rows_of(tokens, 0), tokens, cotangent))
+    arrived = exchange(sent)
+    arrived, mixes, lines, sent, later = tie(
         (
-            first_mats[layer],
-            big_bias(mix_in_bias[layer]),
-            second_mats[layer],
-            big_bias(mix_out_bias[layer]),
-            first_mats[layer].transpose(0, 2, 1),
-            second_mats[layer].transpose(0, 2, 1),
-        )
-        for layer in range(LAYERS)
+            arrived,
+            mixes,
+            lines,
+            rows_of(cotangent_here, 0),
+            both(rows_of(tokens_here, 1), rows_of(cotangent_here, 1)),
+        )
+    )
+    gains, shifts, in_biases, out_biases = lines
+    upstream = exchange(sent)
+    output = forward(0, as_item(arrived), None, None)
+
+    upstream, output, later = tie((upstream, output, later))
+    arrived = exchange(later)
+    grad = backward(0, 1, as_item(upstream))
+    grad = backward(0, 0, grad)
+
+    grad, arrived, output = tie((grad, arrived, output))
+    returned = exchange(grad.reshape(abroad))
+    output = forward(1, arrived, 0, output)
+
+    returned, output, arrived = tie((returned, output, arrived))
+    delivered = exchange(output)
+    mid_grad = backward_feed(1, 1, arrived, 1)
+    grad = backward_spectral(1, 1, mid_grad)
+    last_sum, grad = tie((own_half(feed_sums[1][0], "rep", 0, 1), grad))
+    mid_grad = backward_feed(1, 0, grad)
+    last_sum = own_half(last_sum, "rep", 1, 1)
+    first_sum = own_half(after(feed_sums[0][0], last_sum), "rep", 0, 1)
+    mid_grad, last_sum, first_sum = tie((mid_grad, last_sum, first_sum))
+    grad = backward_spectral(1, 0, mid_grad)
+    last_sum = own_rows(last_sum, [0], wide)
+    first_sum = own_half(first_sum, "rep", 1, 1)
+
+    delivered, grad, last_sum, first_sum, feed_sums, mix_sums = tie(
+        (delivered, grad, last_sum, first_sum, feed_sums, mix_sums)
+    )
+    input_grad = widened(one_part(returned), 0, chunks, None)
+    returned = exchange(grad.reshape(abroad))
+    output = widened(
+        delivered.reshape(wide, chunks, *tokens.shape[1:]), 0, chunks, None
+    ).reshape(tokens.shape)
+    packed = jnp.stack(
+        [
+            jnp.concatenate([jnp.sum(sums[layer][1], axis=0) for sums in (feed_sums, mix_sums)])
+            for layer in range(LAYERS)
+        ]
+    ).reshape(-1, 128)
+    blocks = jnp.concatenate([sums[0] for sums in mix_sums], axis=1)
+    rep, rep_at, wide_at = lax.axis_size("rep"), lax.axis_index("rep"), lax.axis_index("wide")
+    width = blocks.shape[1] // rep
+
+    def mixed_message(far):
+        return jnp.concatenate([share(blocks, rep_at ^ far, width, 1).reshape(-1, 128), packed])
+
+    summed = tree_sum(
+        [mixed_message(0)] + [swapped(mixed_message(far), "rep", far) for far in range(1, rep)]
+    )
+    blocks, packed = summed[: D * width // 128], summed[D * width // 128 :]
+    extra = (input_grad, output)
+    top = wide.bit_length() - 2
+    for bit in range(top):
+        if bit + 1 < top:
+            last_sum = own_rows(last_sum, [bit + 1], wide >> (bit + 1))
+        first_sum = own_rows(first_sum, [bit], wide >> bit)
+        if bit:
+            blocks, packed = wide_step(blocks, packed, bit - 1, wide)
+        last_sum, first_sum, blocks, packed, extra = tie(
+            (last_sum, first_sum, blocks, packed, extra)
+        )
+    blocks, packed = wide_step(blocks, packed, top - 1, wide)
+    blocks, packed = wide_step(blocks, packed, top, wide)
+    last_sum, first_sum = (own_rows(each, [top], wide >> top) for each in (last_sum, first_sum))
+    input_grad, output = extra
+    returned, output, packed, blocks, last_sum, first_sum = tie(
+        (returned, output, packed, blocks, last_sum, first_sum)
+    )
+    pieces = gathered(
+        jnp.concatenate([first_sum, last_sum, blocks.reshape(-1, width)], axis=1).astype(BF)
+    )
+    columns = first_sum.shape[1]
+    in_order = [pieces[reversed_bits(index, rep.bit_length() - 1)] for index in range(rep)]
+    matrices = [
+        jnp.concatenate([piece[:, at : at + columns] for piece in in_order], axis=1).astype(F32)
+        for at in (0, columns)
     ]
-
-    def row(array, *at):
-        return array[at].reshape(1, -1)
-
-    current = arrived
-    stored = []
-    for layer in range(LAYERS):
-        middle, spec = spectral_forward(
-            current, items, row(norm_gain, layer, 0), row(norm_shift, layer, 0), tables, mixes[layer]
-        )
-        following, pre = feed_forward(
-            middle, row(norm_gain, layer, 1), row(norm_shift, layer, 1), w_in[layer],
-            row(b_in, layer), w_out[layer], row(b_out, layer),
-            abroad if layer == LAYERS - 1 else (items, H * W, D),
-        )
-        stored.append((current, middle, spec, pre))
-        current = following
-    output = exchange(current).reshape(tokens.shape).astype(F32)
-
-    sums = [None] * LAYERS
-    matrices = [()] * LAYERS
-    returned = []
-    for item in range(items):
-        grad, item_grad = upstream, item
-        for layer in reversed(range(LAYERS)):
-            layer_input, middle, spec, pre = stored[layer]
-            mid_grad, dw_in, dw_out, *ff_sums = feed_backward(
-                grad, item_grad, middle, pre, item, row(norm_gain, layer, 1),
-                row(norm_shift, layer, 1), w_out[layer].T, w_in[layer].T, matrices[layer],
-            )
-            matrices[layer] = (dw_in, dw_out)
-            grad, *mix_sums = spectral_backward(
-                layer_input, item, mid_grad, spec, item, row(norm_gain, layer, 0), tables,
-                mixes[layer], (1, H * W, D) if layer else (wide, 1, rows, W, D),
-            )
-            item_grad = 0
-            own = ff_sums + mix_sums
-            sums[layer] = own if item == 0 else [a + b for a, b in zip(sums[layer], own)]
-        returned.append(exchange(grad))
-    input_grad = jnp.concatenate(returned, axis=1).reshape(tokens.shape).astype(F32)
-
-    shards = []
-    for layer in reversed(range(LAYERS)):
-        parts = list(matrices[layer])
-        if layer == 0:
-            for slot in (4, 6):
-                parts += [small_matrix(sums[each][slot]) for each in range(LAYERS)]
-        shards.append(summed_shard(jnp.concatenate(parts, axis=1)))
-    shards.reverse()
-    w_in_grad = jnp.stack([shard[:, :FF] for shard in shards])
-    w_out_grad = jnp.stack([shard[:, FF : 2 * FF].T for shard in shards])
-    mix_grads = shards[0][:, 2 * FF :].reshape(-1, 2, LAYERS, 2 * BS).transpose(1, 2, 0, 3)
-
-    def of_both(slot, change):
-        return jnp.stack([change(sums[layer][slot]) for layer in range(LAYERS)])
-
-    def line(array):
-        return jnp.sum(array, axis=0)
-
-    gain_grad, shift_grad, in_bias, out_bias, b_in_grad, b_out_grad = lax.psum(
-        (
-            jnp.stack([of_both(8, line), of_both(2, line)], axis=1),
-            jnp.stack([of_both(9, line), of_both(3, line)], axis=1),
-            of_both(5, small_bias),
-            of_both(7, small_bias),
-            of_both(0, line),
-            of_both(1, line),
-        ),
-        ("wide", "rep"),
+    blocks = jnp.concatenate([piece[:, 2 * columns :] for piece in pieces], axis=1).astype(F32)
+    w_in_grad = jnp.stack([matrix[:, :FF] for matrix in matrices])
+    w_out_grad = jnp.stack([matrix[:, FF:].T for matrix in matrices])
+    mix_grads = blocks.reshape(-1, LAYERS, 2, 2 * BS).transpose(2, 1, 0, 3)
+    packed = packed.reshape(LAYERS, -1)
+    input_grad = widened(one_part(returned), 1, chunks, input_grad).reshape(tokens.shape)
+
+    b_in_grad, b_out_grad, gain_two, shift_two, in_bias, out_bias, gain_one, shift_one = (
+        jnp.split(packed, np.cumsum([FF, D, D, D, 1024, 1024, D]), axis=1)
     )
     return (
-        output, input_grad, gain_grad, shift_grad, mix_grads[0], in_bias, mix_grads[1], out_bias,
-        w_in_grad, b_in_grad, w_out_grad, b_out_grad,
+        output, input_grad, jnp.stack([gain_one, gain_two], axis=1),
+        jnp.stack([shift_one, shift_two], axis=1), mix_grads[0], small_bias(in_bias),
+        mix_grads[1], small_bias(out_bias), w_in_grad, b_in_grad, w_out_grad, b_out_grad,
     )
 
 
@@ -970,7 +1143,7 @@
 
 def any_size(tokens, *others):
     wide, rep = lax.axis_size("wide"), lax.axis_size("rep")
-    if tokens.shape[0] % wide == 0 and power_of_two(wide) and power_of_two(rep) and wide <= 16:
+    if tokens.shape[0] == 2 * wide and tokens.shape[1] * W == TT and power_of_two(rep):
         return whole_items(tokens, *others)
     return body(tokens, *others)
 

time: 1090 us -> 828 us (0.76)
  blocking collectives: 129 us -> 0 us
  waiting for transfers between devices: 244 us -> 199 us
  Pallas kernels: 527 us -> 485 us
  local copies, waits for them, and re-layouts: 81.1 us -> 45.1 us
  other arithmetic: 61.1 us -> 38.7 us
  starting transfers between devices: 38.1 us -> 50.4 us
    psum x1 -> x0, blocking collectives: 114 us -> none  [whole_items(): lax.psum((jnp.stack([of_both(8, line), of_both(2, line)], axis=1), jnp.st...]
    all_to_all x5 -> x6, waiting for transfers between devices: 196 us -> 118 us  [exchange(): lax.all_to_all(array, 'wide', split_axis=0, concat_axis=0, tiled=True)]
    pallas_call x4, Pallas kernels: 238 us -> 198 us  [feed_backward(): pl.pallas_call(functools.partial(feed_backward_kernel, len(start) > 0), g...]
    convert_element_type x6 -> x2, other arithmetic: 33.4 us -> 0.14 us  [whole_items(): jnp.concatenate([piece[:, at:at + columns] for piece in in_order], axis=1)]
    ppermute x10 -> x18, waiting for transfers between devices: 47.9 us -> 81 us  [swapped(): return lax.ppermute(array, axis_name, [(i, i ^ far) for i in range(size)])]
    unnamed x127 -> x41, local copies, waits for them, and re-layouts: 24.6 us -> 7.11 us
    all_gather x2 -> x0, blocking collectives: 15.3 us -> none  [summed_shard(): gathered = lax.all_gather(array.reshape(shard, columns).astype(BF), 'rep')]
    another operation x13 -> x7, other arithmetic: 2.28 us -> 17.5 us  [the longest x2 1.15 us: whole_items(): w_out_grad = jnp.stack([shard[:, FF:2 * FF].T for shard in shards])]
  transfers between devices with their start and end apart: 15 -> 24, of which waited for: 7 -> 14; matrix products, arithmetic and copies ran while one was open for 11% -> 9% of each run, Pallas kernels for 49% -> 59%
where the time goes in v2:
time: 828 us; the launch traced here: 820 us
  Pallas kernels  485 us (59%)
  waiting for transfers between devices  199 us (24%)
  starting transfers between devices  50.4 us (6%)
  local copies, waits for them, and re-layouts  45.1 us (5%)
  other arithmetic  38.7 us (5%)
    pallas_call x4, Pallas kernels, feed_backward(): pl.pallas_call(functools.partial(feed_backward_kernel, len(start) > 0), g...  198 us
    all_to_all x6, waiting for transfers between devices, exchange(): lax.all_to_all(array, 'wide', split_axis=0, concat_axis=0, tiled=True)  118 us
    pallas_call x4, Pallas kernels, feed_forward(): pl.pallas_call(feed_forward_kernel, grid=(H * W // TT,), in_specs=[rows_s...  98.2 us
    pallas_call x4, Pallas kernels, spectral_backward(): pl.pallas_call(functools.partial(spectral_backward_kernel, len(start) > 0...  94.7 us
    ppermute x18, waiting for transfers between devices, swapped(): return lax.ppermute(array, axis_name, [(i, i ^ far) for i in range(size)])  81 us
    pallas_call x4, Pallas kernels, spectral_forward(): pl.pallas_call(spectral_forward_kernel, grid=(SPECTRAL_STEPS,), in_specs=...  66.7 us
    all_to_all x6, starting transfers between devices, exchange(): lax.all_to_all(array, 'wide', split_axis=0, concat_axis=0, tiled=True)  31.9 us
    pallas_call x3, Pallas kernels, widened(): pl.pallas_call(widen_kernel, grid=(parts, items), in_specs=[pl.BlockSpec(...  27.9 us
  transfers between devices with their start and end apart: 24, of which 14 were waited for; matrix products, arithmetic and copies ran while one was open for 9% of the time, Pallas kernels for 59%

profile of v2, /device:TPU:0, one launch (start us, length us, event | category | flops | bytes accessed | tf_op | source)
XLA Modules:
  0.0 820.2 jit_solution(12320734199316316454)
XLA Ops:
  0.6 4.7 slice.172
  5.3 7.4 all-to-all-start
  19.1 9.1 %convert.15 = bf16[16,8,64,512]{3,2,1,0:T(8,128)(2,1)} convert(f32[16,8,64,512]{3,2,1,0:T(8,128)} %param.21) | non-fusion elementwise | flops 4194304 | bytes 25165824 | tf_op jit(solution)/shard_map/convert.6
  32.1 1.1 fusion.2
  36.2 4.1 fusion.10
  40.7 6.3 pad_maximum_fusion
  46.9 59.1 %all-to-all-done = bf16[8,8,64,512]{3,2,1,0:T(8,128)(2,1)} async-done(((bf16[8,8,64,512]{3,2,1,0:T(8,128)(2,1)}), bf16[8,8,64,512]{3,2,1,0:T(8,128)(2,1)}, u32[]{:S(2)}, u32[]{:S(2)}) %all-to-all-start) | async-done | bytes 4194336 | tf_op jit(solution)/shard_map/all_to_all | solution.py:887
  106.0 4.7 all-to-all-start.1
  114.9 16.6 %spectral_forward.4 = (bf16[4096,512]{1,0:T(8,128)(2,1)}, bf16[32,64,512]{2,1,0:T(8,128)(2,1)}) custom-call(bf16[4096,512]{1,0:T(8,128)(2,1)} %bitcast.26.x_ref.refs_0_, f32[1,512]{1,0:T(1,128)} %get-tuple-element.129.gain.refs_3_, f32[1,512]{1,0:T(1,128)} %get-tuple-element.130.shift, bf16[512,512]{1,0:T(8,128)(2,1)} %constant.46.clone.into, ...), custom_call_target="tpu_custom_call" | custom-call | flops 1000000 | bytes 1000000 | tf_op jit(solution)/shard_map/spectral_forward/pallas_call | solution.py:741
  131.5 24.4 %feed_forward.4 = (bf16[4096,512]{1,0:T(8,128)(2,1)}, bf16[4096,2048]{1,0:T(8,128)(2,1)}) custom-call(bf16[4096,512]{1,0:T(8,128)(2,1)} %get-tuple-element.135.mid_ref.refs_1_, f32[1,512]{1,0:T(1,128)} %get-tuple-element.136.gain.refs_3_, f32[1,512]{1,0:T(1,128)} %get-tuple-element.137.shift.refs_4_, bf16[2,512,2048]{2,1,0:T(8,128)(2,1)} %refs_6_.11, ...), custom_call_target="tpu_custom_call" | custom-call | flops 1000000 | bytes 1000000 | tf_op jit(solution)/shard_map/feed_forward/pallas_call | solution.py:801
  155.9 16.7 %spectral_forward.5 = (bf16[4096,512]{1,0:T(8,128)(2,1)}, bf16[32,64,512]{2,1,0:T(8,128)(2,1)}) custom-call(bf16[4096,512]{1,0:T(8,128)(2,1)} %get-tuple-element.140.x_ref.refs_0_, f32[1,512]{1,0:T(1,128)} %get-tuple-element.142.gain.refs_3_, f32[1,512]{1,0:T(1,128)} %get-tuple-element.143.shift, bf16[512,512]{1,0:T(8,128)(2,1)} %constant.46.clone.into, ...), custom_call_target="tpu_custom_call" | custom-call | flops 1000000 | bytes 1000000 | tf_op jit(solution)/shard_map/spectral_forward/pallas_call | solution.py:741
  172.6 24.4 %feed_forward.5 = (bf16[8,2,512,512]{3,2,1,0:T(8,128)(2,1)}, bf16[4096,2048]{1,0:T(8,128)(2,1)}) custom-call(bf16[4096,512]{1,0:T(8,128)(2,1)} %get-tuple-element.148.mid_ref.refs_1_, f32[1,512]{1,0:T(1,128)} %get-tuple-element.149.gain.refs_3_, f32[1,512]{1,0:T(1,128)} %get-tuple-element.150.shift.refs_4_, bf16[2,512,2048]{2,1,0:T(8,128)(2,1)} %refs_6_.11, ...), custom_call_target="tpu_custom_call" | custom-call | flops 1000000 | bytes 1000000 | tf_op jit(solution)/shard_map/feed_forward/pallas_call | solution.py:801
  197.0 6.3 all-to-all-done.1
  203.3 5.4 all-to-all-start.2
  208.7 48.8 %feed_backward.4 = (bf16[4096,512]{1,0:T(8,128)(2,1)}, f32[512,4096]{1,0:T(8,128)}, f32[8,3584]{1,0:T(8,128)}) custom-call(bf16[4096,512]{1,0:T(8,128)(2,1)} %bitcast.27.refs_0_, bf16[4096,512]{1,0:T(8,128)(2,1)} %get-tuple-element.148.mid_ref.refs_1_, bf16[4096,2048]{1,0:T(8,128)(2,1)} %get-tuple-element.156.refs_2_, ...), custom_call_target="tpu_custom_call" | custom-call | flops 1000000 | bytes 1000000 | tf_op jit(solution)/shard_map/feed_backward/pallas_call | solution.py:829
  257.5 23.4 %spectral_backward.4 = (bf16[4096,512]{1,0:T(8,128)(2,1)}, f32[512,256]{1,0:T(8,128)}, f32[8,3072]{1,0:T(8,128)}) custom-call(bf16[4096,512]{1,0:T(8,128)(2,1)} %get-tuple-element.140.x_ref.refs_0_, bf16[4096,512]{1,0:T(8,128)(2,1)} %get-tuple-element.157.refs_1_, bf16[32,64,512]{2,1,0:T(8,128)(2,1)} %get-tuple-element.158.refs_2_, ...), custom_call_target="tpu_custom_call" | custom-call | flops 1000000 | bytes 1000000 | tf_op jit(solution)/shard_map/spectral_backward/pallas_call | solution.py:767
  280.9 49.1 %feed_backward.5 = (bf16[4096,512]{1,0:T(8,128)(2,1)}, f32[512,4096]{1,0:T(8,128)}, f32[8,3584]{1,0:T(8,128)}) custom-call(bf16[4096,512]{1,0:T(8,128)(2,1)} %get-tuple-element.161.refs_0_, bf16[4096,512]{1,0:T(8,128)(2,1)} %get-tuple-element.135.mid_ref.refs_1_, bf16[4096,2048]{1,0:T(8,128)(2,1)} %get-tuple-element.162.refs_2_, ...), custom_call_target="tpu_custom_call" | custom-call | flops 1000000 | bytes 1000000 | tf_op jit(solution)/shard_map/feed_backward/pallas_call | solution.py:829
  330.0 23.5 %spectral_backward.5 = (bf16[4096,512]{1,0:T(8,128)(2,1)}, f32[512,256]{1,0:T(8,128)}, f32[8,3072]{1,0:T(8,128)}) custom-call(bf16[4096,512]{1,0:T(8,128)(2,1)} %bitcast.26.x_ref.refs_0_, bf16[4096,512]{1,0:T(8,128)(2,1)} %get-tuple-element.163.refs_1_, bf16[32,64,512]{2,1,0:T(8,128)(2,1)} %get-tuple-element.164.refs_2_, ...), custom_call_target="tpu_custom_call" | custom-call | flops 1000000 | bytes 1000000 | tf_op jit(solution)/shard_map/spectral_backward/pallas_call | solution.py:767
  353.5 37.2 %all-to-all-done.2.x_ref.refs_0_ = bf16[8,2,512,512]{3,2,1,0:T(8,128)(2,1)} async-done(((bf16[8,2,512,512]{3,2,1,0:T(8,128)(2,1)}), bf16[8,2,512,512]{3,2,1,0:T(8,128)(2,1)}, u32[]{:S(2)}, u32[]{:S(2)}) %all-to-all-start.2) | async-done | bytes 8388640 | tf_op jit(solution)/shard_map/all_to_all | solution.py:887
  390.7 4.8 all-to-all-start.3
  395.4 16.8 %spectral_forward.6 = (bf16[4096,512]{1,0:T(8,128)(2,1)}, bf16[32,64,512]{2,1,0:T(8,128)(2,1)}) custom-call(bf16[8,2,512,512]{3,2,1,0:T(8,128)(2,1)} %all-to-all-done.2.x_ref.refs_0_, f32[1,512]{1,0:T(1,128)} %get-tuple-element.129.gain.refs_3_, f32[1,512]{1,0:T(1,128)} %get-tuple-element.130.shift, bf16[512,512]{1,0:T(8,128)(2,1)} %constant.46.clone.into, ...), custom_call_target="tpu_custom_call" | custom-call | flops 1000000 | bytes 1000000 | tf_op jit(solution)/shard_map/spectral_forward/pallas_call | solution.py:741
  412.3 24.5 %feed_forward.6 = (bf16[4096,512]{1,0:T(8,128)(2,1)}, bf16[4096,2048]{1,0:T(8,128)(2,1)}) custom-call(bf16[4096,512]{1,0:T(8,128)(2,1)} %get-tuple-element.172.mid_ref.refs_1_, f32[1,512]{1,0:T(1,128)} %get-tuple-element.136.gain.refs_3_, f32[1,512]{1,0:T(1,128)} %get-tuple-element.137.shift.refs_4_, bf16[2,512,2048]{2,1,0:T(8,128)(2,1)} %refs_6_.11, ...), custom_call_target="tpu_custom_call" | custom-call | flops 1000000 | bytes 1000000 | tf_op jit(solution)/shard_map/feed_forward/pallas_call | solution.py:801
  436.7 16.6 %spectral_forward.7 = (bf16[4096,512]{1,0:T(8,128)(2,1)}, bf16[32,64,512]{2,1,0:T(8,128)(2,1)}) custom-call(bf16[4096,512]{1,0:T(8,128)(2,1)} %get-tuple-element.173.x_ref.refs_0_, f32[1,512]{1,0:T(1,128)} %get-tuple-element.142.gain.refs_3_, f32[1,512]{1,0:T(1,128)} %get-tuple-element.143.shift, bf16[512,512]{1,0:T(8,128)(2,1)} %constant.46.clone.into, ...), custom_call_target="tpu_custom_call" | custom-call | flops 1000000 | bytes 1000000 | tf_op jit(solution)/shard_map/spectral_forward/pallas_call | solution.py:741
  453.3 24.9 %feed_forward.7 = (bf16[8,2,512,512]{3,2,1,0:T(8,128)(2,1)}, bf16[4096,2048]{1,0:T(8,128)(2,1)}) custom-call(bf16[4096,512]{1,0:T(8,128)(2,1)} %get-tuple-element.174.mid_ref.refs_1_, f32[1,512]{1,0:T(1,128)} %get-tuple-element.149.gain.refs_3_, f32[1,512]{1,0:T(1,128)} %get-tuple-element.150.shift.refs_4_, ...), custom_call_target="tpu_custom_call", output_to_operand_aliasing={{0}: (7, {})} | custom-call | flops 1000000 | bytes 1000000 | tf_op jit(solution)/shard_map/feed_forward/pallas_call | solution.py:801
  478.2 10.0 %all-to-all-done.3 = bf16[8,8,64,512]{3,2,1,0:T(8,128)(2,1)} async-done(((bf16[8,8,64,512]{3,2,1,0:T(8,128)(2,1)}), bf16[8,8,64,512]{3,2,1,0:T(8,128)(2,1)}, u32[]{:S(2)}, u32[]{:S(2)}) %all-to-all-start.3) | async-done | bytes 4194336 | tf_op jit(solution)/shard_map/all_to_all | solution.py:887
  488.2 5.0 all-to-all-start.4
  493.2 49.8 %feed_backward.6 = (bf16[4096,512]{1,0:T(8,128)(2,1)}, bf16[512,4096]{1,0:T(8,128)(2,1)}, f32[8,3584]{1,0:T(8,128)}) custom-call(bf16[8,2,512,512]{3,2,1,0:T(8,128)(2,1)} %all-to-all-done.2.x_ref.refs_0_, bf16[4096,512]{1,0:T(8,128)(2,1)} %get-tuple-element.174.mid_ref.refs_1_, bf16[4096,2048]{1,0:T(8,128)(2,1)} %get-tuple-element.179.refs_2_, ...), custom_call_target="tpu_custom_call" | custom-call | flops 1000000 | bytes 1000000 | tf_op jit(solution)/shard_map/feed_backward/pallas_call | solution.py:829
  543.0 3.2 constant_dynamic-slice_fusion.9
  546.2 23.9 %spectral_backward.6 = (bf16[4096,512]{1,0:T(8,128)(2,1)}, f32[512,256]{1,0:T(8,128)}, f32[8,3072]{1,0:T(8,128)}) custom-call(bf16[4096,512]{1,0:T(8,128)(2,1)} %get-tuple-element.173.x_ref.refs_0_, bf16[4096,512]{1,0:T(8,128)(2,1)} %get-tuple-element.183.refs_1_, bf16[32,64,512]{2,1,0:T(8,128)(2,1)} %get-tuple-element.184.refs_2_, ...), custom_call_target="tpu_custom_call" | custom-call | flops 1000000 | bytes 1000000 | tf_op jit(solution)/shard_map/spectral_backward/pallas_call | solution.py:767
  570.0 2.4 convert_add_fusion.1
  572.5 2.0 copy-done.3
  574.7 1.6 collective-permute-start.1
  576.2 50.1 %feed_backward.7 = (bf16[4096,512]{1,0:T(8,128)(2,1)}, bf16[512,4096]{1,0:T(8,128)(2,1)}, f32[8,3584]{1,0:T(8,128)}) custom-call(bf16[4096,512]{1,0:T(8,128)(2,1)} %get-tuple-element.188.refs_0_, bf16[4096,512]{1,0:T(8,128)(2,1)} %get-tuple-element.172.mid_ref.refs_1_, bf16[4096,2048]{1,0:T(8,128)(2,1)} %get-tuple-element.189.refs_2_, ...), custom_call_target="tpu_custom_call" | custom-call | flops 1000000 | bytes 1000000 | tf_op jit(solution)/shard_map/feed_backward/pallas_call | solution.py:829
  626.4 3.2 convert_add_fusion.3
  630.0 3.9 collective-permute-done.2
  634.8 2.0 copy-done.1
  636.8 1.1 dynamic-slice_convert_fusion
  638.4 1.3 dynamic-slice_convert_fusion.3
  639.7 1.9 collective-permute-start.3
  641.7 24.0 %spectral_backward.7 = (bf16[4096,512]{1,0:T(8,128)(2,1)}, f32[512,256]{1,0:T(8,128)}, f32[8,3072]{1,0:T(8,128)}) custom-call(bf16[8,2,512,512]{3,2,1,0:T(8,128)(2,1)} %all-to-all-done.2.x_ref.refs_0_, bf16[4096,512]{1,0:T(8,128)(2,1)} %get-tuple-element.196.refs_1_, bf16[32,64,512]{2,1,0:T(8,128)(2,1)} %get-tuple-element.197.refs_2_, ...), custom_call_target="tpu_custom_call" | custom-call | flops 1000000 | bytes 1000000 | tf_op jit(solution)/shard_map/spectral_backward/pallas_call | solution.py:767
  665.7 1.5 convert_add_fusion.5
  667.2 3.0 convert_add_fusion.2
  670.2 5.0 all-to-all-done.4
  675.2 4.7 all-to-all-start.5
  682.1 1.9 collective-permute-start.5
  687.3 1.5 collective-permute-start.8
  690.0 1.5 collective-permute-start.6
  691.5 7.3 widen.3.refs_0_
  698.8 13.4 %widen.4 = f32[2,8,8,64,512]{4,3,2,1,0:T(8,128)} custom-call(bf16[8,2,8,64,512]{4,3,2,1,0:T(8,128)(2,1)} %bitcast.37.part), custom_call_target="tpu_custom_call" | custom-call | flops 1000000 | bytes 1000000 | tf_op jit(solution)/shard_map/widen/pallas_call | solution.py:870
  712.2 41.1 %collective-permute-done.5 = bf16[2,1,64,1024]{3,2,0,1:T(8,128)(2,1)} collective-permute-done((bf16[2,1,64,1024]{3,2,0,1:T(8,128)(2,1)}, bf16[2,1,64,1024]{3,2,0,1:T(8,128)(2,1)}, u32[]{:S(2)}, u32[]{:S(2)}) %collective-permute-start.5) | collective-permute-done | bytes 262176 | tf_op jit(solution)/shard_map/ppermute | solution.py:896
  753.3 1.8 bitcast_add_fusion.1
  755.1 1.2 fusion.1
  756.4 1.2 convert_add_fusion.4
  757.7 1.6 collective-permute-start.11
  759.3 2.5 collective-permute-start.10
  761.9 2.2 collective-permute-done.11
  764.1 13.9 %collective-permute-done.10 = bf16[2,1,64,1024]{3,2,0,1:T(8,128)(2,1)S(1)} collective-permute-done((bf16[2,1,64,1024]{3,2,0,1:T(8,128)(2,1)S(1)}, bf16[2,1,64,1024]{3,2,0,1:T(8,128)(2,1)S(1)}, u32[]{:S(2)}, u32[]{:S(2)}) %collective-permute-start.10) | collective-permute-done | bytes 262176 | tf_op jit(solution)/shard_map/ppermute | solution.py:896
  778.3 2.9 collective-permute-start.15
  782.3 3.2 collective-permute-done.12
  785.7 7.1 collective-permute-done.15
  792.8 2.8 collective-permute-done.14
  796.9 1.6 collective-permute-start.16
  798.5 6.5 collective-permute-done.16
  809.2 7.3 widen.5
  (193 shorter events, 36.4 us)
Async XLA Ops:
  5.3 7.4 copy-start.8
  5.3 100.7 %all-to-all-start = ((bf16[8,8,64,512]{3,2,1,0:T(8,128)(2,1)}), bf16[8,8,64,512]{3,2,1,0:T(8,128)(2,1)}, u32[]{:S(2)}, u32[]{:S(2)}) async-start(bf16[8,8,64,512]{3,2,1,0:T(8,128)(2,1)} %slice.172), calls=%async_computation | async-start | bytes 8388608 | tf_op jit(solution)/shard_map/all_to_all | solution.py:887
  12.7 1.6 copy-start.9
  28.1 0.7 copy-start.14
  28.1 1.5 copy-start.15
  31.9 2.4 copy-start.18
  31.9 3.0 copy-start.16
  31.9 3.0 copy-start.17
  31.9 3.6 copy-start.13
  31.9 4.2 copy-start
  36.2 4.5 slice-start
  106.0 97.3 %all-to-all-start.1 = ((bf16[8,8,64,512]{3,2,1,0:T(8,128)(2,1)}), bf16[8,8,64,512]{3,2,1,0:T(8,128)(2,1)}, u32[]{:S(2)}, u32[]{:S(2)}) async-start(bf16[8,8,64,512]{3,2,1,0:T(8,128)(2,1)} %get-tuple-element.141), calls=%async_computation.1 | async-start | bytes 8388608 | tf_op jit(solution)/shard_map/all_to_all | solution.py:887
  203.3 187.4 %all-to-all-start.2 = ((bf16[8,2,512,512]{3,2,1,0:T(8,128)(2,1)}), bf16[8,2,512,512]{3,2,1,0:T(8,128)(2,1)}, u32[]{:S(2)}, u32[]{:S(2)}) async-start(bf16[8,2,512,512]{3,2,1,0:T(8,128)(2,1)} %pad_maximum_fusion), calls=%async_computation.2 | async-start | bytes 16777216 | tf_op jit(solution)/shard_map/all_to_all | solution.py:887
  390.7 97.5 %all-to-all-start.3 = ((bf16[8,8,64,512]{3,2,1,0:T(8,128)(2,1)}), bf16[8,8,64,512]{3,2,1,0:T(8,128)(2,1)}, u32[]{:S(2)}, u32[]{:S(2)}) async-start(bf16[8,8,64,512]{3,2,1,0:T(8,128)(2,1)} %bitcast.154), calls=%async_computation.3 | async-start | bytes 8388608 | tf_op jit(solution)/shard_map/all_to_all | solution.py:887
  488.2 187.0 %all-to-all-start.4 = ((bf16[8,2,512,512]{3,2,1,0:T(8,128)(2,1)}), bf16[8,2,512,512]{3,2,1,0:T(8,128)(2,1)}, u32[]{:S(2)}, u32[]{:S(2)}) async-start(bf16[8,2,512,512]{3,2,1,0:T(8,128)(2,1)} %get-tuple-element.177), calls=%async_computation.4 | async-start | bytes 16777216 | tf_op jit(solution)/shard_map/all_to_all | solution.py:887
  546.2 23.9 %collective-permute-start = (bf16[512,2048]{1,0:T(8,128)(2,1)}, bf16[512,2048]{1,0:T(8,128)(2,1)}, u32[]{:S(2)}, u32[]{:S(2)}) collective-permute-start(bf16[512,2048]{1,0:T(8,128)(2,1)} %constant_dynamic-slice_fusion.9), channel_id=1, source_target_pairs={{0,1},{1,0},{2,3},{3,2},{4,5},{5,4},{6,7},{7,6},{8,9},{9,8},{10,11... | collective-permute-start | bytes 6291464 | tf_op jit(solution)/shard_map/ppermute | solution.py:896
  546.2 23.9 %copy-start.6 = (bf16[512,4096]{1,0:T(8,128)(2,1)S(1)}, bf16[512,4096]{1,0:T(8,128)(2,1)}, u32[]{:S(2)}) copy-start(bf16[512,4096]{1,0:T(8,128)(2,1)} %get-tuple-element.182) | copy-start | bytes 12582916
  572.5 2.0 copy-start.3
  574.7 51.7 %collective-permute-start.1 = (bf16[512,1024]{1,0:T(8,128)(2,1)S(1)}, bf16[512,1024]{1,0:T(8,128)(2,1)}, u32[]{:S(2)}, u32[]{:S(2)}) collective-permute-start(bf16[512,1024]{1,0:T(8,128)(2,1)S(1)} %dynamic-slice_convert_fusion.1), channel_id=1, source_target_pairs={{0,2},{1,3},{2,0},{3,1},{4,6},{5,7},{6,4},{7,5},{8,10},{9,11},{10,... | collective-permute-start | bytes 3145736 | tf_op jit(solution)/shard_map/ppermute | solution.py:896
  576.2 50.2 %copy-start.4 = (f32[512,2048]{1,0:T(8,128)S(1)}, f32[512,2048]{1,0:T(8,128)}, u32[]{:S(2)}) copy-start(f32[512,2048]{1,0:T(8,128)} %copy-done.3) | copy-start | bytes 12582916
  626.4 3.2 copy-start.7
  629.7 4.2 collective-permute-start.2
  634.8 2.0 copy-start.1
  637.9 29.3 %collective-permute-start.4 = (bf16[512,1024]{1,0:T(8,128)(2,1)}, bf16[512,1024]{1,0:T(8,128)(2,1)}, u32[]{:S(2)}, u32[]{:S(2)}) collective-permute-start(bf16[512,1024]{1,0:T(8,128)(2,1)} %dynamic-slice_convert_fusion), channel_id=1, source_target_pairs={{0,2},{1,3},{2,0},{3,1},{4,6},{5,7},{6,4},{7,5},{8,10},{9,11},{10,... | collective-permute-start | bytes 3145736 | tf_op jit(solution)/shard_map/ppermute | solution.py:896
  639.7 26.0 %collective-permute-start.3 = (bf16[4,1,64,1024]{3,2,1,0:T(8,128)(2,1)S(1)}, bf16[4,1,64,1024]{3,2,1,0:T(8,128)(2,1)}, u32[]{:S(2)}, u32[]{:S(2)}) collective-permute-start(bf16[4,1,64,1024]{3,2,1,0:T(8,128)(2,1)S(1)} %dynamic-slice_convert_fusion.3), channel_id=1, source_target_pairs={{0,4},{4,0},{8,12},{12,8},{16,20},{20,16},{24,28},{28,24},{1,5},{5... | collective-permute-start | bytes 1572872 | tf_op jit(solution)/shard_map/ppermute | solution.py:896
  641.6 25.6 %copy-start.2 = (f32[512,2048]{1,0:T(8,128)S(1)}, f32[512,2048]{1,0:T(8,128)}, u32[]{:S(2)}) copy-start(f32[512,2048]{1,0:T(8,128)} %copy-done.1) | copy-start | bytes 12582916
  675.2 4.7 copy-start.11
  675.2 5.9 copy-start.10
  675.2 5.9 copy-start.12
  675.2 121.6 %all-to-all-start.5 = ((bf16[8,8,64,512]{3,2,1,0:T(8,128)(2,1)}), bf16[8,8,64,512]{3,2,1,0:T(8,128)(2,1)}, u32[]{:S(2)}, u32[]{:S(2)}) async-start(bf16[8,8,64,512]{3,2,1,0:T(8,128)(2,1)} %bitcast.153), calls=%async_computation.5 | async-start | bytes 8388608 | tf_op jit(solution)/shard_map/all_to_all | solution.py:887
  679.9 9.3 %copy-start.5 = (f32[512,1024]{1,0:T(8,128)S(1)}, f32[512,1024]{1,0:T(8,128)}, u32[]{:S(2)}) copy-start(f32[512,1024]{1,0:T(8,128)} %convert_add_fusion.2) | copy-start | bytes 6291460
  682.1 71.2 %collective-permute-start.5 = (bf16[2,1,64,1024]{3,2,0,1:T(8,128)(2,1)}, bf16[2,1,64,1024]{3,2,0,1:T(8,128)(2,1)}, u32[]{:S(2)}, u32[]{:S(2)}) collective-permute-start(bf16[2,1,64,1024]{3,2,0,1:T(8,128)(2,1)} %bitcast_convert_fusion.1), channel_id=1, source_target_pairs={{0,8},{4,12},{8,0},{12,4},{16,24},{20,28},{24,16},{28,20},{1,9},{5... | collective-permute-start | bytes 786440 | tf_op jit(solution)/shard_map/ppermute | solution.py:896
  687.3 67.8 %collective-permute-start.7 = (f32[616,128]{1,0:T(8,128)}, f32[616,128]{1,0:T(8,128)}, u32[]{:S(2)}, u32[]{:S(2)}) collective-permute-start(f32[616,128]{1,0:T(8,128)} %get-tuple-element.342), channel_id=1, source_target_pairs={{0,1},{1,0},{2,3},{3,2},{4,5},{5,4},{6,7},{7,6},{8,9},{9,8},{10,11... | collective-permute-start | bytes 946184 | tf_op jit(solution)/shard_map/ppermute | solution.py:896
  687.3 67.8 %collective-permute-start.8 = (f32[616,128]{1,0:T(8,128)}, f32[616,128]{1,0:T(8,128)}, u32[]{:S(2)}, u32[]{:S(2)}) collective-permute-start(f32[616,128]{1,0:T(8,128)} %get-tuple-element.343), channel_id=1, source_target_pairs={{0,2},{1,3},{2,0},{3,1},{4,6},{5,7},{6,4},{7,5},{8,10},{9,11},{10,... | collective-permute-start | bytes 946184 | tf_op jit(solution)/shard_map/ppermute | solution.py:896
  688.8 66.3 %collective-permute-start.9 = (f32[616,128]{1,0:T(8,128)}, f32[616,128]{1,0:T(8,128)}, u32[]{:S(2)}, u32[]{:S(2)}) collective-permute-start(f32[616,128]{1,0:T(8,128)} %get-tuple-element.341), channel_id=1, source_target_pairs={{0,3},{1,2},{2,1},{3,0},{4,7},{5,6},{6,5},{7,4},{8,11},{9,10},{10,... | collective-permute-start | bytes 946184 | tf_op jit(solution)/shard_map/ppermute | solution.py:896
  690.0 66.3 %collective-permute-start.6 = (bf16[4,1,64,1024]{3,2,1,0:T(8,128)(2,1)}, bf16[4,1,64,1024]{3,2,1,0:T(8,128)(2,1)}, u32[]{:S(2)}, u32[]{:S(2)}) collective-permute-start(bf16[4,1,64,1024]{3,2,1,0:T(8,128)(2,1)} %dynamic-slice_convert_fusion.2), channel_id=1, source_target_pairs={{0,4},{4,0},{8,12},{12,8},{16,20},{20,16},{24,28},{28,24},{1,5},{5... | collective-permute-start | bytes 1572872 | tf_op jit(solution)/shard_map/ppermute | solution.py:896
  757.7 6.4 collective-permute-start.11
  759.3 18.7 %collective-permute-start.10 = (bf16[2,1,64,1024]{3,2,0,1:T(8,128)(2,1)S(1)}, bf16[2,1,64,1024]{3,2,0,1:T(8,128)(2,1)S(1)}, u32[]{:S(2)}, u32[]{:S(2)}) collective-permute-start(bf16[2,1,64,1024]{3,2,0,1:T(8,128)(2,1)S(1)} %bitcast_convert_fusion), channel_id=1, source_target_pairs={{0,8},{4,12},{8,0},{12,4},{16,24},{20,28},{24,16},{28,20},{1,9},{5... | collective-permute-start | bytes 786440 | tf_op jit(solution)/shard_map/ppermute | solution.py:896
  778.1 7.4 collective-permute-start.12
  778.3 14.5 %collective-permute-start.15 = (bf16[1,1,64,1024]{3,2,1,0:T(8,128)(2,1)S(1)}, bf16[1,1,64,1024]{3,2,1,0:T(8,128)(2,1)S(1)}, u32[]{:S(2)}, u32[]{:S(2)}) collective-permute-start(bf16[1,1,64,1024]{3,2,1,0:T(8,128)(2,1)S(1)} %dynamic-slice_convert_fusion.4), channel_id=1, source_target_pairs={{0,16},{4,20},{8,24},{12,28},{16,0},{20,4},{24,8},{28,12},{1,17},{... | collective-permute-start | bytes 393224 | tf_op jit(solution)/shard_map/ppermute | solution.py:896
  782.1 13.4 %collective-permute-start.14 = (bf16[1,1,64,1024]{3,2,1,0:T(8,128)(2,1)S(1)}, bf16[1,1,64,1024]{3,2,1,0:T(8,128)(2,1)S(1)}, u32[]{:S(2)}, u32[]{:S(2)}) collective-permute-start(bf16[1,1,64,1024]{3,2,1,0:T(8,128)(2,1)S(1)} %dynamic-slice_convert_fusion.5), channel_id=1, source_target_pairs={{0,16},{4,20},{8,24},{12,28},{16,0},{20,4},{24,8},{28,12},{1,17},{... | collective-permute-start | bytes 393224 | tf_op jit(solution)/shard_map/ppermute | solution.py:896
  785.6 11.2 %collective-permute-start.13 = (f32[168,128]{1,0:T(8,128)S(1)}, f32[168,128]{1,0:T(8,128)S(1)}, u32[]{:S(2)}, u32[]{:S(2)}) collective-permute-start(f32[168,128]{1,0:T(8,128)S(1)} %pad_maximum_fusion.11), channel_id=1, source_target_pairs={{0,16},{4,20},{8,24},{12,28},{16,0},{20,4},{24,8},{28,12},{1,17},{... | collective-permute-start | bytes 258056 | tf_op jit(solution)/shard_map/ppermute | solution.py:896
  796.9 8.2 collective-permute-start.16
  805.2 11.3 %collective-permute-start.17 = (bf16[64,4352]{1,0:T(8,128)(2,1)S(1)}, bf16[64,4352]{1,0:T(8,128)(2,1)S(1)}, u32[]{:S(2)}, u32[]{:S(2)}) collective-permute-start(bf16[64,4352]{1,0:T(8,128)(2,1)S(1)} %pad_maximum_fusion.7), channel_id=1, source_target_pairs={{0,1},{1,0},{2,3},{3,2},{4,5},{5,4},{6,7},{7,6},{8,9},{9,8},{10,11... | collective-permute-start | bytes 1671176 | tf_op jit(solution)/shard_map/ppermute | solution.py:896

commit v3 on v2

--- a/solution.py
+++ b/solution.py
@@ -397,12 +397,14 @@
 
 def matrix_tables():
     forward_cols, inverse_cols, forward_rows, inverse_rows = plain_tables()
-    eye = np.eye(8)
-    into = np.einsum("wpk,gh->kpghw", forward_cols, eye).reshape(512, 512)
-    outof = np.einsum("pkw,gh->gwkph", inverse_cols, eye).reshape(512, 512)
+    eye = np.eye(4)
+    into = np.einsum("wpk,gh->kpghw", forward_cols, eye).reshape(256, 256)
+    outof = np.einsum("pkw,gh->gwkph", inverse_cols, eye).reshape(256, 256)
     pair = np.eye(2)
-    rows_in = np.einsum("jphq,ab->apjbqh", forward_rows, pair).reshape(128, 256)
-    rows_out = np.einsum("hpjq,ab->aphbqj", inverse_rows, pair).reshape(256, 128)
+    forward_rows = forward_rows.reshape(KH, 2, H // 4, 4, 2)
+    inverse_rows = inverse_rows.reshape(H // 4, 4, 2, KH, 2)
+    rows_in = np.einsum("jphsq,ab->apjbhqs", forward_rows, pair).reshape(128, 256)
+    rows_out = np.einsum("hspjq,ab->ahpsbqj", inverse_rows, pair).reshape(256, 128)
     return [
         jnp.asarray(np.ascontiguousarray(table).astype(ml_dtypes.bfloat16))
         for table in (into, outof, rows_in, rows_out, outof.T, into.T, rows_out.T, rows_in.T)
@@ -472,17 +474,21 @@
     return v * half, slope
 
 
-def cols_in(table, rows, store, at):
-    halves = [mm(table, rows[half * 512 : (half + 1) * 512]).reshape(64, 8, D) for half in range(2)]
-    store[:, pl.ds(at, HB), :] = jnp.concatenate(halves, axis=1).astype(BF)
-
-
-def cols_out(table, store, at):
-    block = store[:, pl.ds(at, HB), :].astype(F32)
+def cols_in(table, rows, store, block):
+    parts = [
+        mm(table, rows[at * 256 : at * 256 + 256]).reshape(KW, 8, D) for at in range(HB // 4)
+    ]
+    store[:, pl.ds(pl.multiple_of(block * 2 * HB, 2 * HB), 2 * HB), :] = jnp.concatenate(
+        parts, axis=1
+    ).astype(BF)
+
+
+def cols_out(table, store, block):
+    part = store[:, pl.ds(pl.multiple_of(block * 2 * HB, 2 * HB), 2 * HB), :].astype(F32)
     return jnp.concatenate(
         [
-            mm(table, block[:, half * 8 : half * 8 + 8].reshape(512, D).astype(BF))
-            for half in range(2)
+            mm(table, part[:, at * 8 : at * 8 + 8].reshape(256, D).astype(BF))
+            for at in range(HB // 4)
         ],
         axis=0,
     )
@@ -515,13 +521,13 @@
         held[step] = x
         unit, _ = normalize(x.astype(F32))
         normed = unit * gain[...] + shift[...]
-        cols_in(into[...], normed.astype(BF), cols, pl.multiple_of(step * HB, HB))
+        cols_in(into[...], normed.astype(BF), cols, step)
 
     @pl.when((step >= n_rows) & (step < n_rows + n_freq))
     def _():
-        first_plane = (step - n_rows) * (2 * KB)
+        first_plane = (step - n_rows) * KB
         for two in range(KB // 2):
-            planes = cols[pl.ds(first_plane + 4 * two, 4)]
+            planes = cols[pl.ds(first_plane + 2 * two, 2)]
             spec_ref[2 * two : 2 * two + 2] = (
                 mm(rows_in[...], planes.reshape(256, D)).astype(BF).reshape(2, 64, D)
             )
@@ -533,8 +539,8 @@
             put_lanes(mixed, group, shrunk.astype(BF))
         for two in range(KB // 2):
             planes = mixed[2 * two : 2 * two + 2].reshape(128, D)
-            cols[pl.ds(first_plane + 4 * two, 4)] = (
-                mm(rows_out[...], planes).astype(BF).reshape(4, 64, D)
+            cols[pl.ds(first_plane + 2 * two, 2)] = (
+                mm(rows_out[...], planes).astype(BF).reshape(2, 128, D)
             )
 
     @pl.when(step >= n_rows + n_freq)
@@ -543,7 +549,7 @@
         x = held[block].astype(F32)
         unit, _ = normalize(x)
         normed = unit * gain[...] + shift[...]
-        filtered = cols_out(outof[...], cols, pl.multiple_of(block * HB, HB))
+        filtered = cols_out(outof[...], cols, block)
         mid_ref[...] = (x + filtered + normed).astype(mid_ref.dtype)
 
 
@@ -581,13 +587,13 @@
     def _():
         grad = grad_ref[...]
         held[step] = grad
-        cols_in(outof_t[...], grad, cols, pl.multiple_of(step * HB, HB))
+        cols_in(outof_t[...], grad, cols, step)
 
     @pl.when((step >= n_rows) & (step < n_rows + n_freq))
     def _():
-        first_plane = (step - n_rows) * (2 * KB)
+        first_plane = (step - n_rows) * KB
         for two in range(KB // 2):
-            planes = cols[pl.ds(first_plane + 4 * two, 4)]
+            planes = cols[pl.ds(first_plane + 2 * two, 2)]
             kept[2 * two : 2 * two + 2] = mm(rows_out_t[...], planes.reshape(256, D)).reshape(
                 2, 64, D
             )
@@ -612,8 +618,8 @@
             put_lanes(mixed, group, mm(d_first, w1_t[group]).astype(BF))
         for two in range(KB // 2):
             planes = mixed[2 * two : 2 * two + 2].reshape(128, D)
-            cols[pl.ds(first_plane + 4 * two, 4)] = (
-                mm(rows_in_t[...], planes).astype(BF).reshape(4, 64, D)
+            cols[pl.ds(first_plane + 2 * two, 2)] = (
+                mm(rows_in_t[...], planes).astype(BF).reshape(2, 128, D)
             )
 
     @pl.when(step == n_rows + n_freq)
@@ -630,7 +636,7 @@
         block = step - n_rows - n_freq
         unit, scale = normalize(lines_of(x_ref).astype(F32))
         mid_grad = held[block].astype(F32)
-        grad = cols_out(into_t[...], cols, pl.multiple_of(block * HB, HB)) + mid_grad
+        grad = cols_out(into_t[...], cols, block) + mid_grad
         lines[:, 2048:2560] += folded(grad * unit)
         lines[:, 2560:3072] += folded(grad)
         new = mid_grad + normalize_back(grad, unit, scale, gain[...])
@@ -655,7 +661,7 @@
 def feed_backward_kernel(with_start, *refs):
     (g_ref, mid_ref, pre_ref, gain, shift, w_out, w_in), refs = refs[:7], refs[7:]
     if with_start:
-        (start_far, start_lines, mid_grad_ref, sent, lines, dw, start, arrival) = refs
+        (start_far, start_lines, side, mid_grad_ref, kept, sent, lines, dw, start, arrival) = refs
         copy = pltpu.make_async_copy(start_far, start, arrival)
     else:
         mid_grad_ref, dw, lines = refs
@@ -692,7 +698,9 @@
         @pl.when(step == H * W // TT - 1)
         def _():
             copy.wait()
-            sent[...] = (dw[...] + start[...]).astype(BF)
+            for ref, half in ((kept, side[0]), (sent, 1 - side[0])):
+                at = pl.ds(pl.multiple_of(half * FF, FF), FF)
+                ref[...] = (dw[:, at] + start[:, at]).astype(BF)
 
 
 def whole(array):
@@ -717,7 +725,12 @@
 
 
 PARAMS = pltpu.CompilerParams(dimension_semantics=("arbitrary",), vmem_limit_bytes=VMEM)
-COST = pl.CostEstimate(flops=1_000_000, bytes_accessed=1_000_000, transcendentals=0)
+
+
+def cost(microseconds):
+    return pl.CostEstimate(
+        flops=microseconds * 400_000_000, bytes_accessed=1_000_000, transcendentals=0
+    )
 
 
 N_ROWS, N_FREQ = H // HB, KW // KB
@@ -751,12 +764,12 @@
             jax.ShapeDtypeStruct((KW, 64, D), BF),
         ],
         scratch_shapes=[
-            pltpu.VMEM((64, 64, D), BF),
+            pltpu.VMEM((KW, 128, D), BF),
             pltpu.VMEM((KB, 64, D), BF),
             pltpu.VMEM((N_ROWS, HB * W, D), BF),
         ],
         compiler_params=PARAMS,
-        cost_estimate=COST,
+        cost_estimate=cost(16),
         name="spectral_forward",
     )(x, *small)
 
@@ -779,13 +792,13 @@
         scratch_shapes=[
             pltpu.VMEM((GROUPS, 256, 256), F32),
             pltpu.VMEM((GROUPS, 256, 256), F32),
-            pltpu.VMEM((64, 64, D), BF),
+            pltpu.VMEM((KW, 128, D), BF),
             pltpu.VMEM((KB, 64, D), BF),
             pltpu.VMEM((KB, 64, D), F32),
             pltpu.VMEM((N_ROWS, HB * W, D), BF),
         ],
         compiler_params=PARAMS,
-        cost_estimate=COST,
+        cost_estimate=cost(24),
         name="spectral_backward",
     )(x, grad, spec, *small)
 
@@ -815,17 +828,16 @@
         out_shape=[shape, jax.ShapeDtypeStruct((H * W, FF), BF)],
         input_output_aliases={7: 0} if more else {},
         compiler_params=PARAMS,
-        cost_estimate=COST,
+        cost_estimate=cost(24),
         name="feed_forward",
     )(middle, gain, shift, w_in, b_in, w_out, b_out, *more)
 
 
-def start_of(fb):
-    return (fb[1], fb[2])
-
-
-def feed_backward(g, kind, middle, pre, layer, gain, shift, w_out, w_in, start):
-    sums = [(D, 2 * FF), (8, FF + 3 * D)]
+def feed_backward(g, kind, middle, pre, layer, gain, shift, w_out, w_in, start, side):
+    matrices, lines = (D, 2 * FF), (8, FF + 3 * D)
+    halves = [(D, FF), (D, FF)]
+    sums = [(dims, BF) for dims in halves] if start else [(matrices, F32)]
+    sums.append((lines, F32))
     return pl.pallas_call(
         functools.partial(feed_backward_kernel, len(start) > 0),
         grid=(H * W // TT,),
@@ -838,25 +850,30 @@
             of_layer(w_out, layer),
             of_layer(w_in, layer),
         ]
-        + ([pl.BlockSpec(memory_space=pl.ANY), whole(start[1])] if start else []),
+        + (
+            [
+                pl.BlockSpec(memory_space=pl.ANY),
+                whole(start[1]),
+                pl.BlockSpec(memory_space=pltpu.SMEM),
+            ]
+            if start
+            else []
+        ),
         out_specs=[rows_spec(TT // W, lambda s: s)]
-        + [pl.BlockSpec(dims, lambda s: (0, 0)) for dims in sums],
-        out_shape=[
-            jax.ShapeDtypeStruct((H * W, D), BF),
-            jax.ShapeDtypeStruct(sums[0], BF if start else F32),
-            jax.ShapeDtypeStruct(sums[1], F32),
-        ],
+        + [pl.BlockSpec(dims, lambda s: (0, 0)) for dims, _ in sums],
+        out_shape=[jax.ShapeDtypeStruct((H * W, D), BF)]
+        + [jax.ShapeDtypeStruct(dims, kind_of) for dims, kind_of in sums],
         scratch_shapes=[
-            pltpu.VMEM(sums[0], F32),
-            pltpu.VMEM(sums[0], F32),
+            pltpu.VMEM(matrices, F32),
+            pltpu.VMEM(matrices, F32),
             pltpu.SemaphoreType.DMA,
         ]
         if start
         else [],
         compiler_params=PARAMS,
-        cost_estimate=COST,
+        cost_estimate=cost(49),
         name="feed_backward",
-    )(g, middle, pre, gain, shift, w_out, w_in, *start)
+    )(g, middle, pre, gain, shift, w_out, w_in, *start, *([side] if start else []))
 
 
 def widen_kernel(part, *refs):
@@ -878,7 +895,7 @@
         compiler_params=pltpu.CompilerParams(
             dimension_semantics=("arbitrary", "arbitrary"), vmem_limit_bytes=VMEM
         ),
-        cost_estimate=COST,
+        cost_estimate=cost(0),
         name="widen",
     )(part, *more)
 
@@ -896,57 +913,45 @@
     return lax.ppermute(array, axis_name, [(i, i ^ far) for i in range(size)])
 
 
-def tree_sum(parts):
-    parts = [part.astype(F32) for part in parts]
-    while len(parts) > 1:
-        parts = [parts[at] + parts[at + 1] for at in range(0, len(parts), 2)]
-    return parts[0]
-
-
 def share(array, index, size, axis):
     return lax.dynamic_slice_in_dim(array, index * size, size, axis)
 
 
-def own_half(array, axis_name, bit, axis):
-    mine, half = (lax.axis_index(axis_name) >> bit) & 1, array.shape[axis] // 2
-    other = share(array, 1 - mine, half, axis).astype(BF)
-    return tree_sum([share(array, mine, half, axis), swapped(other, axis_name, 1 << bit)])
-
-
-def own_rows(array, bits, parts):
-    for bit in bits:
-        blocks = array.reshape(parts // 2, 2, -1, array.shape[1])
-        array = own_half(blocks, "wide", bit, 1).reshape(-1, array.shape[1])
-        parts //= 2
-    return array
-
-
-def wide_step(blocks, packed, bit, wide):
-    mine = (lax.axis_index("wide") >> bit) & 1
-    halves = blocks.reshape(wide >> (bit + 1), 2, -1, 128)
-    own, other = (share(halves, at, 1, 1).reshape(-1, 128) for at in (mine, 1 - mine))
-    arrived = swapped(jnp.concatenate([other, packed]), "wide", 1 << bit)
-    return own + arrived[: own.shape[0]], packed + arrived[own.shape[0] :]
-
-
-def reversed_bits(value, bits):
-    return sum(((value >> bit) & 1) << (bits - 1 - bit) for bit in range(bits))
-
-
-def gathered(array):
-    me = lax.axis_index("rep")
-    parts = [array]
-    for bit in reversed(range(lax.axis_size("rep").bit_length() - 1)):
-        mine = ((me >> bit) & 1) == 0
-        others = [swapped(part, "rep", 1 << bit) for part in (jnp.concatenate(parts, axis=1),)][0]
-        others = jnp.split(others, len(parts), axis=1)
-        parts = [
-            jnp.where(mine == (side == 0), part, other)
-            for side in range(2)
-            for part, other in zip(parts, others)
-        ]
-    bits = lax.axis_size("rep").bit_length() - 1
-    return [parts[reversed_bits(index, bits)] for index in range(len(parts))]
+def own_bit(axis_name, bit):
+    return (lax.axis_index(axis_name) >> bit) & 1
+
+
+def halves(array, side, axis):
+    half = array.shape[axis] // 2
+    return share(array, side, half, axis), share(array, 1 - side, half, axis)
+
+
+def row_halves(array, bit, shard):
+    blocks = array.reshape(-1, 2, shard, array.shape[1])
+    return [half.reshape(-1, array.shape[1]) for half in halves(blocks, own_bit("wide", bit), 1)]
+
+
+def traded(kept, sent, axis_name, bit, behind=()):
+    arrived = swapped(sent.astype(BF), axis_name, 1 << bit)
+    return after(kept, behind).astype(F32) + arrived.astype(F32)
+
+
+def traded_with(kept, sent, extra, axis_name, bit, behind=()):
+    extra = extra.astype(BF)
+    message = jnp.concatenate([sent.astype(BF), extra.reshape(-1, sent.shape[1])], axis=0)
+    arrived = swapped(message, axis_name, 1 << bit).astype(F32)
+    rows = sent.shape[0]
+    return (
+        after(kept, behind).astype(F32) + arrived[:rows],
+        extra.astype(F32) + arrived[rows:].reshape(extra.shape),
+    )
+
+
+def side_by_side(own, other, bit):
+    first = own_bit("rep", bit) == 0
+    return jnp.concatenate(
+        [jnp.where(first, own, other), jnp.where(first, other, own)], axis=1
+    )
 
 
 def whole_items(
@@ -1008,7 +1013,7 @@
         _, _, middle, _, pre = stored[layer, chunk]
         mid_grad, *feed_sums[layer] = feed_backward(
             grad, kind, middle, pre, layer, gains[layer][1], shifts[layer][1], w_out, w_in,
-            feed_sums[layer],
+            feed_sums[layer], side,
         )
         return mid_grad
 
@@ -1044,6 +1049,8 @@
     )
     gains, shifts, in_biases, out_biases = lines
     upstream = exchange(sent)
+    wide_at, rep_at = lax.axis_index("wide"), lax.axis_index("rep")
+    side = (rep_at & 1).astype(jnp.int32).reshape(1)
     output = forward(0, as_item(arrived), None, None)
 
     upstream, output, later = tie((upstream, output, later))
@@ -1058,92 +1065,116 @@
     returned, output, arrived = tie((returned, output, arrived))
     delivered = exchange(output)
     mid_grad = backward_feed(1, 1, arrived, 1)
+    shard = D // wide
+    last_kept, last_sent = feed_sums[1][:2]
     grad = backward_spectral(1, 1, mid_grad)
-    last_sum, grad = tie((own_half(feed_sums[1][0], "rep", 0, 1), grad))
+    last_sum, grad = tie((traded(last_kept, last_sent, "rep", 0, grad), grad))
     mid_grad = backward_feed(1, 0, grad)
-    last_sum = own_half(last_sum, "rep", 1, 1)
-    first_sum = own_half(after(feed_sums[0][0], last_sum), "rep", 0, 1)
-    mid_grad, last_sum, first_sum = tie((mid_grad, last_sum, first_sum))
+    kept, sent = halves(last_sum, own_bit("rep", 1), 1)
+    last_sum, mid_grad, ready = tie(
+        (traded(kept, sent, "rep", 1, mid_grad), mid_grad, feed_sums[0][:2])
+    )
+    first_sum = traded(*ready, "rep", 0)
+    first_sum, mid_grad = tie((first_sum, mid_grad))
     grad = backward_spectral(1, 0, mid_grad)
-    last_sum = own_rows(last_sum, [0], wide)
-    first_sum = own_half(first_sum, "rep", 1, 1)
-
-    delivered, grad, last_sum, first_sum, feed_sums, mix_sums = tie(
-        (delivered, grad, last_sum, first_sum, feed_sums, mix_sums)
-    )
-    input_grad = widened(one_part(returned), 0, chunks, None)
+    kept, sent = row_halves(last_sum, 0, shard)
+    last_sum = traded(kept, sent, "wide", 0, grad)
+    kept, sent = halves(first_sum, own_bit("rep", 1), 1)
+    first_sum = traded(kept, sent, "rep", 1, grad)
+
+    last_sum, first_sum, grad, feed_sums, mix_sums = tie(
+        (last_sum, first_sum, grad, feed_sums, mix_sums)
+    )
+    last_kept, last_sent = row_halves(last_sum, 1, shard)
+    kept, sent = row_halves(first_sum, 0, shard)
+    first_sum = traded(kept, sent, "wide", 0)
+    delivered, grad, returned_first, first_sum, feed_sums, mix_sums = tie(
+        (delivered, grad, returned, first_sum, feed_sums, mix_sums)
+    )
     returned = exchange(grad.reshape(abroad))
+    lines = jnp.stack(
+        [
+            jnp.concatenate([jnp.sum(sums[layer][-1], axis=0) for sums in (feed_sums, mix_sums)])
+            for layer in range(LAYERS)
+        ]
+    )
+    lines_size = lines.size
+    kept, sent = (
+        jnp.concatenate(each, axis=1)
+        for each in zip(*[halves(sums[0], own_bit("rep", 0), 1) for sums in mix_sums])
+    )
+    lines = jnp.pad(lines.reshape(-1), (0, -lines_size % (16 * sent.shape[1])))
+    blocks, lines = traded_with(kept, sent, lines, "rep", 0)
+    last_sum = traded(last_kept, last_sent, "wide", 1, blocks)
+    blocks, returned_first, delivered = tie((blocks, returned_first, delivered))
+    input_grad = widened(one_part(returned_first), 0, chunks, None)
     output = widened(
         delivered.reshape(wide, chunks, *tokens.shape[1:]), 0, chunks, None
     ).reshape(tokens.shape)
-    packed = jnp.stack(
-        [
-            jnp.concatenate([jnp.sum(sums[layer][1], axis=0) for sums in (feed_sums, mix_sums)])
-            for layer in range(LAYERS)
-        ]
-    ).reshape(-1, 128)
-    blocks = jnp.concatenate([sums[0] for sums in mix_sums], axis=1)
-    rep, rep_at, wide_at = lax.axis_size("rep"), lax.axis_index("rep"), lax.axis_index("wide")
-    width = blocks.shape[1] // rep
-
-    def mixed_message(far):
-        return jnp.concatenate([share(blocks, rep_at ^ far, width, 1).reshape(-1, 128), packed])
-
-    summed = tree_sum(
-        [mixed_message(0)] + [swapped(mixed_message(far), "rep", far) for far in range(1, rep)]
-    )
-    blocks, packed = summed[: D * width // 128], summed[D * width // 128 :]
-    extra = (input_grad, output)
-    top = wide.bit_length() - 2
-    for bit in range(top):
-        if bit + 1 < top:
-            last_sum = own_rows(last_sum, [bit + 1], wide >> (bit + 1))
-        first_sum = own_rows(first_sum, [bit], wide >> bit)
-        if bit:
-            blocks, packed = wide_step(blocks, packed, bit - 1, wide)
-        last_sum, first_sum, blocks, packed, extra = tie(
-            (last_sum, first_sum, blocks, packed, extra)
-        )
-    blocks, packed = wide_step(blocks, packed, top - 1, wide)
-    blocks, packed = wide_step(blocks, packed, top, wide)
-    last_sum, first_sum = (own_rows(each, [top], wide >> top) for each in (last_sum, first_sum))
-    input_grad, output = extra
-    returned, output, packed, blocks, last_sum, first_sum = tie(
-        (returned, output, packed, blocks, last_sum, first_sum)
-    )
-    pieces = gathered(
-        jnp.concatenate([first_sum, last_sum, blocks.reshape(-1, width)], axis=1).astype(BF)
-    )
-    columns = first_sum.shape[1]
-    in_order = [pieces[reversed_bits(index, rep.bit_length() - 1)] for index in range(rep)]
+    kept, sent = row_halves(blocks, 0, shard)
+    blocks, lines = traded_with(kept, sent, lines, "wide", 0)
+    high_kept, high_sent = row_halves(blocks, 1, shard)
+    kept, sent = row_halves(first_sum, 1, shard)
+    first_sum = traded(kept, sent, "wide", 1, (high_sent, lines))
+    kept, sent = row_halves(first_sum, 2, shard)
+    first_sum = traded(kept, sent, "wide", 2)
+    kept, sent = row_halves(last_sum, 2, shard)
+    last_sum = traded(kept, sent, "wide", 2, first_sum)
+    blocks, lines = traded_with(high_kept, high_sent, lines, "wide", 1)
+    kept, sent = row_halves(blocks, 2, shard)
+    blocks, lines = traded_with(kept, sent, lines, "wide", 2)
+    returned, output, input_grad, first_sum, last_sum, blocks, lines = tie(
+        (returned, output, input_grad, first_sum, last_sum, blocks, lines)
+    )
+    chain = jnp.concatenate([first_sum, blocks], axis=1)
+    columns = last_sum.shape[1]
+    part = lines.size // shard
+    lines = lines.astype(BF)
+    message = jnp.concatenate(
+        [chain[:, :columns], last_sum, chain[:, columns:], lines.reshape(shard, part)], axis=1
+    ).astype(BF)
+    arrived = swapped(message, "rep", 2)
+    input_grad = widened(one_part(returned), 1, chunks, input_grad).reshape(tokens.shape)
+    arrived, input_grad = tie((arrived, input_grad))
+    first_sum, last_sum = (
+        side_by_side(message[:, at : at + columns], arrived[:, at : at + columns], 1)
+        for at in (0, columns)
+    )
+    blocks = message[:, 2 * columns : -part].astype(F32) + arrived[:, 2 * columns : -part].astype(F32)
+    lines = lines.astype(F32) + arrived[:, -part:].astype(F32).reshape(-1)
+    packed = lines[:lines_size].reshape(LAYERS, -1)
+    message = jnp.concatenate([first_sum, last_sum, blocks.astype(BF)], axis=1)
+    arrived = swapped(message, "rep", 1)
+    b_in_grad, b_out_grad, gain_two, shift_two, in_bias, out_bias, gain_one, shift_one = (
+        jnp.split(packed, np.cumsum([FF, D, D, D, 1024, 1024, D]), axis=1)
+    )
+    gain_grad, shift_grad = (
+        jnp.stack(pair, axis=1) for pair in ((gain_one, gain_two), (shift_one, shift_two))
+    )
+    in_bias_grad, out_bias_grad = small_bias(in_bias), small_bias(out_bias)
+    arrived, gain_grad, shift_grad, in_bias_grad, out_bias_grad, b_in_grad, b_out_grad = tie(
+        (arrived, gain_grad, shift_grad, in_bias_grad, out_bias_grad, b_in_grad, b_out_grad)
+    )
     matrices = [
-        jnp.concatenate([piece[:, at : at + columns] for piece in in_order], axis=1).astype(F32)
-        for at in (0, columns)
+        side_by_side(message[:, at : at + 2 * columns], arrived[:, at : at + 2 * columns], 0).astype(
+            F32
+        )
+        for at in (0, 2 * columns)
     ]
-    blocks = jnp.concatenate([piece[:, 2 * columns :] for piece in pieces], axis=1).astype(F32)
+    blocks = side_by_side(message[:, 4 * columns :], arrived[:, 4 * columns :], 0).astype(F32)
+    mix_grads = blocks.reshape(shard, 2, LAYERS, 2 * BS).transpose(1, 2, 0, 3)
     w_in_grad = jnp.stack([matrix[:, :FF] for matrix in matrices])
     w_out_grad = jnp.stack([matrix[:, FF:].T for matrix in matrices])
-    mix_grads = blocks.reshape(-1, LAYERS, 2, 2 * BS).transpose(2, 1, 0, 3)
-    packed = packed.reshape(LAYERS, -1)
-    input_grad = widened(one_part(returned), 1, chunks, input_grad).reshape(tokens.shape)
-
-    b_in_grad, b_out_grad, gain_two, shift_two, in_bias, out_bias, gain_one, shift_one = (
-        jnp.split(packed, np.cumsum([FF, D, D, D, 1024, 1024, D]), axis=1)
-    )
+
     return (
-        output, input_grad, jnp.stack([gain_one, gain_two], axis=1),
-        jnp.stack([shift_one, shift_two], axis=1), mix_grads[0], small_bias(in_bias),
-        mix_grads[1], small_bias(out_bias), w_in_grad, b_in_grad, w_out_grad, b_out_grad,
-    )
-
-
-def power_of_two(number):
-    return number > 0 and number & (number - 1) == 0
+        output, input_grad, gain_grad, shift_grad, mix_grads[0], in_bias_grad,
+        mix_grads[1], out_bias_grad, w_in_grad, b_in_grad, w_out_grad, b_out_grad,
+    )
 
 
 def any_size(tokens, *others):
     wide, rep = lax.axis_size("wide"), lax.axis_size("rep")
-    if tokens.shape[0] == 2 * wide and tokens.shape[1] * W == TT and power_of_two(rep):
+    if tokens.shape[0] == 2 * wide and tokens.shape[1] * W == TT and rep == 4 and wide == 8:
         return whole_items(tokens, *others)
     return body(tokens, *others)
 

time: 828 us -> 816 us (0.986)
  local copies, waits for them, and re-layouts: 45.1 us -> 34.9 us
    ppermute x18 -> x16, starting transfers between devices: 18.6 us -> 23.1 us  [swapped(): return lax.ppermute(array, axis_name, [(i, i ^ far) for i in range(size)])]
    ppermute x18 -> x16, waiting for transfers between devices: 81 us -> 84.2 us  [swapped(): return lax.ppermute(array, axis_name, [(i, i ^ far) for i in range(size)])]
  transfers between devices with their start and end apart: 24 -> 22, of which waited for: 14 -> 11; matrix products, arithmetic and copies ran while one was open for 9% -> 7% of each run, Pallas kernels for 59% -> 60%
where the time goes in v3:
time: 816 us; the launch traced here: 808 us
  Pallas kernels  481 us (59%)
  waiting for transfers between devices  200 us (25%)
  starting transfers between devices  58.2 us (7%)
  local copies, waits for them, and re-layouts  34.9 us (4%)
  other arithmetic  32.2 us (4%)
    pallas_call x4, Pallas kernels, feed_backward(): pl.pallas_call(functools.partial(feed_backward_kernel, len(start) > 0), g...  198 us
    all_to_all x6, waiting for transfers between devices, exchange(): lax.all_to_all(array, 'wide', split_axis=0, concat_axis=0, tiled=True)  115 us
    pallas_call x4, Pallas kernels, feed_forward(): pl.pallas_call(feed_forward_kernel, grid=(H * W // TT,), in_specs=[rows_s...  98.2 us
    pallas_call x4, Pallas kernels, spectral_backward(): pl.pallas_call(functools.partial(spectral_backward_kernel, len(start) > 0...  92.3 us
    ppermute x16, waiting for transfers between devices, swapped(): return lax.ppermute(array, axis_name, [(i, i ^ far) for i in range(size)])  84.2 us
    pallas_call x4, Pallas kernels, spectral_forward(): pl.pallas_call(spectral_forward_kernel, grid=(SPECTRAL_STEPS,), in_specs=...  64.7 us
    all_to_all x6, starting transfers between devices, exchange(): lax.all_to_all(array, 'wide', split_axis=0, concat_axis=0, tiled=True)  35.1 us
    pallas_call x3, Pallas kernels, widened(): pl.pallas_call(widen_kernel, grid=(parts, items), in_specs=[pl.BlockSpec(...  27.9 us
  transfers between devices with their start and end apart: 22, of which 11 were waited for; matrix products, arithmetic and copies ran while one was open for 7% of the time, Pallas kernels for 60%

profile of v3, /device:TPU:0, one launch (start us, length us, event | category | flops | bytes accessed | tf_op | source)
XLA Modules:
  0.0 808.2 jit_solution(8975198515391184142)
XLA Ops:
  0.6 4.7 slice.169
  5.3 7.4 all-to-all-start
  19.1 9.1 %convert.36 = bf16[16,8,64,512]{3,2,1,0:T(8,128)(2,1)} convert(f32[16,8,64,512]{3,2,1,0:T(8,128)} %param.21) | non-fusion elementwise | flops 4194304 | bytes 25165824 | tf_op jit(solution)/shard_map/convert.21
  32.1 1.1 fusion.3
  33.2 1.1 fusion.5
  36.2 4.1 fusion.11
  40.7 6.2 pad_maximum_fusion
  47.0 59.1 %all-to-all-done = bf16[8,8,64,512]{3,2,1,0:T(8,128)(2,1)} async-done(((bf16[8,8,64,512]{3,2,1,0:T(8,128)(2,1)}), bf16[8,8,64,512]{3,2,1,0:T(8,128)(2,1)}, u32[]{:S(2)}, u32[]{:S(2)}) %all-to-all-start) | async-done | bytes 4194336 | tf_op jit(solution)/shard_map/all_to_all | solution.py:904
  106.0 4.7 all-to-all-start.1
  110.8 1.0 copy.126.w1.refs_8_
  111.8 1.0 copy.127.w2.refs_10_
  112.8 1.0 copy.128.w1.refs_8_
  113.8 1.0 copy.129.w2.refs_10_
  114.9 16.1 %spectral_forward.4 = (bf16[4096,512]{1,0:T(8,128)(2,1)}, bf16[32,64,512]{2,1,0:T(8,128)(2,1)}) custom-call(bf16[4096,512]{1,0:T(8,128)(2,1)} %bitcast.26.x_ref.refs_0_, f32[1,512]{1,0:T(1,128)} %get-tuple-element.150.gain.refs_3_, f32[1,512]{1,0:T(1,128)} %get-tuple-element.151.shift, bf16[256,256]{1,0:T(8,128)(2,1)} %constant.44.clone.into, ...), custom_call_target="tpu_custom_call" | custom-call | flops 6400000000 | bytes 1000000 | tf_op jit(solution)/shard_map/spectral_forward/pallas_call | solution.py:754
  131.0 24.5 %feed_forward.4 = (bf16[4096,512]{1,0:T(8,128)(2,1)}, bf16[4096,2048]{1,0:T(8,128)(2,1)}) custom-call(bf16[4096,512]{1,0:T(8,128)(2,1)} %get-tuple-element.156.mid_ref.refs_1_, f32[1,512]{1,0:T(1,128)} %get-tuple-element.157.gain.refs_3_, f32[1,512]{1,0:T(1,128)} %get-tuple-element.158.shift.refs_4_, bf16[2,512,2048]{2,1,0:T(8,128)(2,1)} %refs_6_.11, ...), custom_call_target="tpu_custom_call" | custom-call | flops 9600000000 | bytes 1000000 | tf_op jit(solution)/shard_map/feed_forward/pallas_call | solution.py:814
  155.5 16.1 %spectral_forward.5 = (bf16[4096,512]{1,0:T(8,128)(2,1)}, bf16[32,64,512]{2,1,0:T(8,128)(2,1)}) custom-call(bf16[4096,512]{1,0:T(8,128)(2,1)} %get-tuple-element.161.x_ref.refs_0_, f32[1,512]{1,0:T(1,128)} %get-tuple-element.163.gain.refs_3_, f32[1,512]{1,0:T(1,128)} %get-tuple-element.164.shift, bf16[256,256]{1,0:T(8,128)(2,1)} %constant.44.clone.into, ...), custom_call_target="tpu_custom_call" | custom-call | flops 6400000000 | bytes 1000000 | tf_op jit(solution)/shard_map/spectral_forward/pallas_call | solution.py:754
  171.6 24.4 %feed_forward.5 = (bf16[8,2,512,512]{3,2,1,0:T(8,128)(2,1)}, bf16[4096,2048]{1,0:T(8,128)(2,1)}) custom-call(bf16[4096,512]{1,0:T(8,128)(2,1)} %get-tuple-element.169.mid_ref.refs_1_, f32[1,512]{1,0:T(1,128)} %get-tuple-element.170.gain.refs_3_, f32[1,512]{1,0:T(1,128)} %get-tuple-element.171.shift.refs_4_, bf16[2,512,2048]{2,1,0:T(8,128)(2,1)} %refs_6_.11, ...), custom_call_target="tpu_custom_call" | custom-call | flops 9600000000 | bytes 1000000 | tf_op jit(solution)/shard_map/feed_forward/pallas_call | solution.py:814
  196.1 7.3 all-to-all-done.1
  203.3 5.4 all-to-all-start.2
  208.7 48.9 %feed_backward.4 = (bf16[4096,512]{1,0:T(8,128)(2,1)}, f32[512,4096]{1,0:T(8,128)}, f32[8,3584]{1,0:T(8,128)}) custom-call(bf16[4096,512]{1,0:T(8,128)(2,1)} %bitcast.27.refs_0_, bf16[4096,512]{1,0:T(8,128)(2,1)} %get-tuple-element.169.mid_ref.refs_1_, bf16[4096,2048]{1,0:T(8,128)(2,1)} %get-tuple-element.177.refs_2_, ...), custom_call_target="tpu_custom_call" | custom-call | flops 19599998976 | bytes 1000000 | tf_op jit(solution)/shard_map/feed_backward/pallas_call | solution.py:841
  257.5 22.8 %spectral_backward.4 = (bf16[4096,512]{1,0:T(8,128)(2,1)}, f32[512,256]{1,0:T(8,128)}, f32[8,3072]{1,0:T(8,128)}) custom-call(bf16[4096,512]{1,0:T(8,128)(2,1)} %get-tuple-element.161.x_ref.refs_0_, bf16[4096,512]{1,0:T(8,128)(2,1)} %get-tuple-element.178.refs_1_, bf16[32,64,512]{2,1,0:T(8,128)(2,1)} %get-tuple-element.179.refs_2_, ...), custom_call_target="tpu_custom_call" | custom-call | flops 9600000000 | bytes 1000000 | tf_op jit(solution)/shard_map/spectral_backward/pallas_call | solution.py:780
  280.4 49.1 %feed_backward.5 = (bf16[4096,512]{1,0:T(8,128)(2,1)}, f32[512,4096]{1,0:T(8,128)}, f32[8,3584]{1,0:T(8,128)}) custom-call(bf16[4096,512]{1,0:T(8,128)(2,1)} %get-tuple-element.182.refs_0_, bf16[4096,512]{1,0:T(8,128)(2,1)} %get-tuple-element.156.mid_ref.refs_1_, bf16[4096,2048]{1,0:T(8,128)(2,1)} %get-tuple-element.183.refs_2_, ...), custom_call_target="tpu_custom_call" | custom-call | flops 19599998976 | bytes 1000000 | tf_op jit(solution)/shard_map/feed_backward/pallas_call | solution.py:841
  329.5 23.0 %spectral_backward.5 = (bf16[4096,512]{1,0:T(8,128)(2,1)}, f32[512,256]{1,0:T(8,128)}, f32[8,3072]{1,0:T(8,128)}) custom-call(bf16[4096,512]{1,0:T(8,128)(2,1)} %bitcast.26.x_ref.refs_0_, bf16[4096,512]{1,0:T(8,128)(2,1)} %get-tuple-element.184.refs_1_, bf16[32,64,512]{2,1,0:T(8,128)(2,1)} %get-tuple-element.185.refs_2_, ...), custom_call_target="tpu_custom_call" | custom-call | flops 9600000000 | bytes 1000000 | tf_op jit(solution)/shard_map/spectral_backward/pallas_call | solution.py:780
  352.5 38.2 %all-to-all-done.2.x_ref.refs_0_ = bf16[8,2,512,512]{3,2,1,0:T(8,128)(2,1)} async-done(((bf16[8,2,512,512]{3,2,1,0:T(8,128)(2,1)}), bf16[8,2,512,512]{3,2,1,0:T(8,128)(2,1)}, u32[]{:S(2)}, u32[]{:S(2)}) %all-to-all-start.2) | async-done | bytes 8388640 | tf_op jit(solution)/shard_map/all_to_all | solution.py:904
  390.7 4.8 all-to-all-start.3
  395.5 16.3 %spectral_forward.6 = (bf16[4096,512]{1,0:T(8,128)(2,1)}, bf16[32,64,512]{2,1,0:T(8,128)(2,1)}) custom-call(bf16[8,2,512,512]{3,2,1,0:T(8,128)(2,1)} %all-to-all-done.2.x_ref.refs_0_, f32[1,512]{1,0:T(1,128)} %get-tuple-element.150.gain.refs_3_, f32[1,512]{1,0:T(1,128)} %get-tuple-element.151.shift, bf16[256,256]{1,0:T(8,128)(2,1)} %constant.44.clone.into, ...), custom_call_target="tpu_custom_call" | custom-call | flops 6400000000 | bytes 1000000 | tf_op jit(solution)/shard_map/spectral_forward/pallas_call | solution.py:754
  411.8 24.5 %feed_forward.6 = (bf16[4096,512]{1,0:T(8,128)(2,1)}, bf16[4096,2048]{1,0:T(8,128)(2,1)}) custom-call(bf16[4096,512]{1,0:T(8,128)(2,1)} %get-tuple-element.193.mid_ref.refs_1_, f32[1,512]{1,0:T(1,128)} %get-tuple-element.157.gain.refs_3_, f32[1,512]{1,0:T(1,128)} %get-tuple-element.158.shift.refs_4_, bf16[2,512,2048]{2,1,0:T(8,128)(2,1)} %refs_6_.11, ...), custom_call_target="tpu_custom_call" | custom-call | flops 9600000000 | bytes 1000000 | tf_op jit(solution)/shard_map/feed_forward/pallas_call | solution.py:814
  436.3 16.2 %spectral_forward.7 = (bf16[4096,512]{1,0:T(8,128)(2,1)}, bf16[32,64,512]{2,1,0:T(8,128)(2,1)}) custom-call(bf16[4096,512]{1,0:T(8,128)(2,1)} %get-tuple-element.194.x_ref.refs_0_, f32[1,512]{1,0:T(1,128)} %get-tuple-element.163.gain.refs_3_, f32[1,512]{1,0:T(1,128)} %get-tuple-element.164.shift, bf16[256,256]{1,0:T(8,128)(2,1)} %constant.44.clone.into, ...), custom_call_target="tpu_custom_call" | custom-call | flops 6400000000 | bytes 1000000 | tf_op jit(solution)/shard_map/spectral_forward/pallas_call | solution.py:754
  452.4 24.9 %feed_forward.7 = (bf16[8,2,512,512]{3,2,1,0:T(8,128)(2,1)}, bf16[4096,2048]{1,0:T(8,128)(2,1)}) custom-call(bf16[4096,512]{1,0:T(8,128)(2,1)} %get-tuple-element.195.mid_ref.refs_1_, f32[1,512]{1,0:T(1,128)} %get-tuple-element.170.gain.refs_3_, f32[1,512]{1,0:T(1,128)} %get-tuple-element.171.shift.refs_4_, ...), custom_call_target="tpu_custom_call", output_to_operand_aliasing={{0}: (7, {})} | custom-call | flops 9600000000 | bytes 1000000 | tf_op jit(solution)/shard_map/feed_forward/pallas_call | solution.py:814
  477.3 10.9 %all-to-all-done.3 = bf16[8,8,64,512]{3,2,1,0:T(8,128)(2,1)} async-done(((bf16[8,8,64,512]{3,2,1,0:T(8,128)(2,1)}), bf16[8,8,64,512]{3,2,1,0:T(8,128)(2,1)}, u32[]{:S(2)}, u32[]{:S(2)}) %all-to-all-start.3) | async-done | bytes 4194336 | tf_op jit(solution)/shard_map/all_to_all | solution.py:904
  488.1 4.9 all-to-all-start.4
  493.1 49.9 %feed_backward.6 = (bf16[4096,512]{1,0:T(8,128)(2,1)}, bf16[512,2048]{1,0:T(8,128)(2,1)}, bf16[512,2048]{1,0:T(8,128)(2,1)}, f32[8,3584]{1,0:T(8,128)}) custom-call(bf16[8,2,512,512]{3,2,1,0:T(8,128)(2,1)} %all-to-all-done.2.x_ref.refs_0_, bf16[4096,512]{1,0:T(8,128)(2,1)} %get-tuple-element.195.mid_ref.refs_1_, ...), custom_call_target="tpu_custom_call" | custom-call | flops 19599998976 | bytes 1000000 | tf_op jit(solution)/shard_map/feed_backward/pallas_call | solution.py:841
  543.1 23.3 %spectral_backward.6 = (bf16[4096,512]{1,0:T(8,128)(2,1)}, f32[512,256]{1,0:T(8,128)}, f32[8,3072]{1,0:T(8,128)}) custom-call(bf16[4096,512]{1,0:T(8,128)(2,1)} %get-tuple-element.194.x_ref.refs_0_, bf16[4096,512]{1,0:T(8,128)(2,1)} %get-tuple-element.204.refs_1_, bf16[32,64,512]{2,1,0:T(8,128)(2,1)} %get-tuple-element.205.refs_2_, ...), custom_call_target="tpu_custom_call" | custom-call | flops 9600000000 | bytes 1000000 | tf_op jit(solution)/shard_map/spectral_backward/pallas_call | solution.py:780
  567.4 1.6 collective-permute-start.1
  569.1 50.1 %feed_backward.7 = (bf16[4096,512]{1,0:T(8,128)(2,1)}, bf16[512,2048]{1,0:T(8,128)(2,1)}, bf16[512,2048]{1,0:T(8,128)(2,1)}, f32[8,3584]{1,0:T(8,128)}) custom-call(bf16[4096,512]{1,0:T(8,128)(2,1)} %get-tuple-element.212.refs_0_, bf16[4096,512]{1,0:T(8,128)(2,1)} %get-tuple-element.193.mid_ref.refs_1_, bf16[4096,2048]{1,0:T(8,128)(2,1)} %get-tuple-element.213.refs_2_, ...), custom_call_target="tpu_custom_call" | custom-call | flops 19599998976 | bytes 1000000 | tf_op jit(solution)/shard_map/feed_backward/pallas_call | solution.py:841
  620.6 1.9 collective-permute-start.3
  622.6 1.5 collective-permute-done.2
  624.1 2.3 convert_add_fusion
  626.4 1.1 dynamic-slice_convert_fusion
  628.0 23.2 %spectral_backward.7 = (bf16[4096,512]{1,0:T(8,128)(2,1)}, f32[512,256]{1,0:T(8,128)}, f32[8,3072]{1,0:T(8,128)}) custom-call(bf16[8,2,512,512]{3,2,1,0:T(8,128)(2,1)} %all-to-all-done.2.x_ref.refs_0_, bf16[4096,512]{1,0:T(8,128)(2,1)} %get-tuple-element.224.refs_1_, bf16[32,64,512]{2,1,0:T(8,128)(2,1)} %get-tuple-element.225.refs_2_, ...), custom_call_target="tpu_custom_call" | custom-call | flops 9600000000 | bytes 1000000 | tf_op jit(solution)/shard_map/spectral_backward/pallas_call | solution.py:780
  651.4 3.6 collective-permute-done.3
  655.0 2.1 convert_add_fusion.5
  657.2 1.6 convert_add_fusion.2
  658.8 0.9 dynamic-slice_convert_fusion.2
  659.7 2.5 collective-permute-start.5
  664.0 10.1 %collective-permute-done.5 = bf16[256,1024]{1,0:T(8,128)(2,1)} collective-permute-done((bf16[256,1024]{1,0:T(8,128)(2,1)}, bf16[256,1024]{1,0:T(8,128)(2,1)}, u32[]{:S(2)}, u32[]{:S(2)}) %collective-permute-start.5) | collective-permute-done | bytes 524320 | tf_op jit(solution)/shard_map/ppermute | solution.py:913
  674.1 1.2 convert_add_fusion.4
  675.4 0.9 reduce_sum.36
  676.3 0.9 reduce_sum.37
  677.3 0.9 reduce_sum.39
  678.3 7.8 all-to-all-start.5
  686.6 2.1 collective-permute-start.8
  689.1 1.5 collective-permute-start.7
  690.7 2.4 collective-permute-start.11
  693.1 13.4 %widen.3 = f32[2,8,8,64,512]{4,3,2,1,0:T(8,128)} custom-call(bf16[8,2,8,64,512]{4,3,2,1,0:T(8,128)(2,1)} %bitcast.37.part), custom_call_target="tpu_custom_call" | custom-call | bytes 1000000 | tf_op jit(solution)/shard_map/widen/pallas_call | solution.py:887
  706.6 7.3 widen.4.refs_0_
  713.8 10.1 %collective-permute-done.7 = bf16[320,256]{1,0:T(8,128)(2,1)S(1)} collective-permute-done((bf16[320,256]{1,0:T(8,128)(2,1)S(1)}, bf16[320,256]{1,0:T(8,128)(2,1)S(1)}, u32[]{:S(2)}, u32[]{:S(2)}) %collective-permute-start.7) | collective-permute-done | bytes 163872 | tf_op jit(solution)/shard_map/ppermute | solution.py:913
  724.3 36.9 %collective-permute-done.8 = bf16[128,1024]{1,0:T(8,128)(2,1)S(1)} collective-permute-done((bf16[128,1024]{1,0:T(8,128)(2,1)S(1)}, bf16[128,1024]{1,0:T(8,128)(2,1)S(1)}, u32[]{:S(2)}, u32[]{:S(2)}) %collective-permute-start.8) | collective-permute-done | bytes 262176 | tf_op jit(solution)/shard_map/ppermute | solution.py:913
  761.3 4.3 collective-permute-start.9
  765.8 4.3 collective-permute-start.13
  770.1 21.3 %collective-permute-done.9 = bf16[64,1024]{1,0:T(8,128)(2,1)S(1)} collective-permute-done((bf16[64,1024]{1,0:T(8,128)(2,1)S(1)}, bf16[64,1024]{1,0:T(8,128)(2,1)S(1)}, u32[]{:S(2)}, u32[]{:S(2)}) %collective-permute-start.9) | collective-permute-done | bytes 131104 | tf_op jit(solution)/shard_map/ppermute | solution.py:913
  792.9 7.3 widen.5
  805.8 1.0 pad_maximum_fusion.2
  806.9 1.0 pad_maximum_fusion.1
  (209 shorter events, 25.6 us)
Async XLA Ops:
  5.3 7.4 copy-start.6
  5.3 100.7 %all-to-all-start = ((bf16[8,8,64,512]{3,2,1,0:T(8,128)(2,1)}), bf16[8,8,64,512]{3,2,1,0:T(8,128)(2,1)}, u32[]{:S(2)}, u32[]{:S(2)}) async-start(bf16[8,8,64,512]{3,2,1,0:T(8,128)(2,1)} %slice.169), calls=%async_computation | async-start | bytes 8388608 | tf_op jit(solution)/shard_map/all_to_all | solution.py:904
  12.7 1.6 copy-start.7
  28.1 0.7 copy-start.10
  28.1 1.5 copy-start.11
  31.9 2.4 copy-start.14
  31.9 3.0 copy-start.12
  31.9 3.0 copy-start.13
  31.9 3.7 copy-start.9
  31.9 4.3 copy-start
  36.2 4.5 slice-start
  106.0 97.3 %all-to-all-start.1 = ((bf16[8,8,64,512]{3,2,1,0:T(8,128)(2,1)}), bf16[8,8,64,512]{3,2,1,0:T(8,128)(2,1)}, u32[]{:S(2)}, u32[]{:S(2)}) async-start(bf16[8,8,64,512]{3,2,1,0:T(8,128)(2,1)} %get-tuple-element.162), calls=%async_computation.1 | async-start | bytes 8388608 | tf_op jit(solution)/shard_map/all_to_all | solution.py:904
  203.3 187.4 %all-to-all-start.2 = ((bf16[8,2,512,512]{3,2,1,0:T(8,128)(2,1)}), bf16[8,2,512,512]{3,2,1,0:T(8,128)(2,1)}, u32[]{:S(2)}, u32[]{:S(2)}) async-start(bf16[8,2,512,512]{3,2,1,0:T(8,128)(2,1)} %pad_maximum_fusion), calls=%async_computation.2 | async-start | bytes 16777216 | tf_op jit(solution)/shard_map/all_to_all | solution.py:904
  390.7 97.5 %all-to-all-start.3 = ((bf16[8,8,64,512]{3,2,1,0:T(8,128)(2,1)}), bf16[8,8,64,512]{3,2,1,0:T(8,128)(2,1)}, u32[]{:S(2)}, u32[]{:S(2)}) async-start(bf16[8,8,64,512]{3,2,1,0:T(8,128)(2,1)} %bitcast.175), calls=%async_computation.3 | async-start | bytes 8388608 | tf_op jit(solution)/shard_map/all_to_all | solution.py:904
  488.1 187.2 %all-to-all-start.4 = ((bf16[8,2,512,512]{3,2,1,0:T(8,128)(2,1)}), bf16[8,2,512,512]{3,2,1,0:T(8,128)(2,1)}, u32[]{:S(2)}, u32[]{:S(2)}) async-start(bf16[8,2,512,512]{3,2,1,0:T(8,128)(2,1)} %get-tuple-element.198), calls=%async_computation.4 | async-start | bytes 16777216 | tf_op jit(solution)/shard_map/all_to_all | solution.py:904
  543.0 23.4 %collective-permute-start = (bf16[512,2048]{1,0:T(8,128)(2,1)}, bf16[512,2048]{1,0:T(8,128)(2,1)S(1)}, u32[]{:S(2)}, u32[]{:S(2)}) collective-permute-start(bf16[512,2048]{1,0:T(8,128)(2,1)} %get-tuple-element.210), channel_id=1, source_target_pairs={{0,1},{1,0},{2,3},{3,2},{4,5},{5,4},{6,7},{7,6},{8,9},{9,8},{10,11... | collective-permute-start | bytes 6291464 | tf_op jit(solution)/shard_map/ppermute | solution.py:913
  543.1 23.3 %copy-start.3 = (bf16[512,2048]{1,0:T(8,128)(2,1)S(1)}, bf16[512,2048]{1,0:T(8,128)(2,1)}, u32[]{:S(2)}) copy-start(bf16[512,2048]{1,0:T(8,128)(2,1)} %get-tuple-element.209) | copy-start | bytes 6291460
  567.4 51.8 %collective-permute-start.1 = (bf16[512,1024]{1,0:T(8,128)(2,1)S(1)}, bf16[512,1024]{1,0:T(8,128)(2,1)S(1)}, u32[]{:S(2)}, u32[]{:S(2)}) collective-permute-start(bf16[512,1024]{1,0:T(8,128)(2,1)S(1)} %dynamic-slice_convert_fusion.1), channel_id=1, source_target_pairs={{0,2},{1,3},{2,0},{3,1},{4,6},{5,7},{6,4},{7,5},{8,10},{9,11},{10,... | collective-permute-start | bytes 3145736 | tf_op jit(solution)/shard_map/ppermute | solution.py:913
  619.5 4.6 collective-permute-start.2
  619.7 4.3 copy-start.2
  620.6 34.4 %collective-permute-start.3 = (bf16[256,1024]{1,0:T(8,128)(2,1)}, bf16[256,1024]{1,0:T(8,128)(2,1)}, u32[]{:S(2)}, u32[]{:S(2)}) collective-permute-start(bf16[256,1024]{1,0:T(8,128)(2,1)} %bitcast.32), channel_id=1, source_target_pairs={{0,4},{4,0},{8,12},{12,8},{16,20},{20,16},{24,28},{28,24},{1,5},{5... | collective-permute-start | bytes 1572872 | tf_op jit(solution)/shard_map/ppermute | solution.py:913
  627.5 29.6 %collective-permute-start.4 = (bf16[512,1024]{1,0:T(8,128)(2,1)}, bf16[512,1024]{1,0:T(8,128)(2,1)}, u32[]{:S(2)}, u32[]{:S(2)}) collective-permute-start(bf16[512,1024]{1,0:T(8,128)(2,1)} %dynamic-slice_convert_fusion), channel_id=1, source_target_pairs={{0,2},{1,3},{2,0},{3,1},{4,6},{5,7},{6,4},{7,5},{8,10},{9,11},{10,... | collective-permute-start | bytes 3145736 | tf_op jit(solution)/shard_map/ppermute | solution.py:913
  657.2 5.1 copy-start.1
  658.8 18.4 %copy-start.8 = (f32[8,3584]{1,0:T(8,128)S(1)}, f32[8,3584]{1,0:T(8,128)}, u32[]{:S(2)}) copy-start(f32[8,3584]{1,0:T(8,128)} %get-tuple-element.252) | copy-start | bytes 344068
  659.7 14.4 %collective-permute-start.5 = (bf16[256,1024]{1,0:T(8,128)(2,1)}, bf16[256,1024]{1,0:T(8,128)(2,1)}, u32[]{:S(2)}, u32[]{:S(2)}) collective-permute-start(bf16[256,1024]{1,0:T(8,128)(2,1)} %bitcast.35), channel_id=1, source_target_pairs={{0,4},{4,0},{8,12},{12,8},{16,20},{20,16},{24,28},{28,24},{1,5},{5... | collective-permute-start | bytes 1572872 | tf_op jit(solution)/shard_map/ppermute | solution.py:913
  663.0 27.6 %collective-permute-start.10 = (bf16[128,1024]{1,0:T(8,128)(2,1)}, bf16[128,1024]{1,0:T(8,128)(2,1)S(1)}, u32[]{:S(2)}, u32[]{:S(2)}) collective-permute-start(bf16[128,1024]{1,0:T(8,128)(2,1)} %bitcast.53), channel_id=1, source_target_pairs={{0,8},{4,12},{8,0},{12,4},{16,24},{20,28},{24,16},{28,20},{1,9},{5... | collective-permute-start | bytes 786440 | tf_op jit(solution)/shard_map/ppermute | solution.py:913
  678.3 8.0 copy-start.4
  678.3 8.0 copy-start.5
  678.3 113.9 %all-to-all-start.5 = ((bf16[8,8,64,512]{3,2,1,0:T(8,128)(2,1)}), bf16[8,8,64,512]{3,2,1,0:T(8,128)(2,1)}, u32[]{:S(2)}, u32[]{:S(2)}) async-start(bf16[8,8,64,512]{3,2,1,0:T(8,128)(2,1)} %bitcast.174), calls=%async_computation.5 | async-start | bytes 8388608 | tf_op jit(solution)/shard_map/all_to_all | solution.py:904
  686.4 2.4 collective-permute-start.6
  686.6 74.6 %collective-permute-start.8 = (bf16[128,1024]{1,0:T(8,128)(2,1)S(1)}, bf16[128,1024]{1,0:T(8,128)(2,1)S(1)}, u32[]{:S(2)}, u32[]{:S(2)}) collective-permute-start(bf16[128,1024]{1,0:T(8,128)(2,1)S(1)} %bitcast.203), channel_id=1, source_target_pairs={{0,8},{4,12},{8,0},{12,4},{16,24},{20,28},{24,16},{28,20},{1,9},{5... | collective-permute-start | bytes 786440 | tf_op jit(solution)/shard_map/ppermute | solution.py:913
  689.1 34.9 %collective-permute-start.7 = (bf16[320,256]{1,0:T(8,128)(2,1)S(1)}, bf16[320,256]{1,0:T(8,128)(2,1)S(1)}, u32[]{:S(2)}, u32[]{:S(2)}) collective-permute-start(bf16[320,256]{1,0:T(8,128)(2,1)S(1)} %pad_maximum_fusion.8), channel_id=1, source_target_pairs={{0,4},{4,0},{8,12},{12,8},{16,20},{20,16},{24,28},{28,24},{1,5},{5... | collective-permute-start | bytes 491528 | tf_op jit(solution)/shard_map/ppermute | solution.py:913
  690.7 100.7 %collective-permute-start.11 = (bf16[64,1024]{1,0:T(8,128)(2,1)S(1)}, bf16[64,1024]{1,0:T(8,128)(2,1)S(1)}, u32[]{:S(2)}, u32[]{:S(2)}) collective-permute-start(bf16[64,1024]{1,0:T(8,128)(2,1)S(1)} %fusion.1), channel_id=1, source_target_pairs={{0,16},{4,20},{8,24},{12,28},{16,0},{20,4},{24,8},{28,12},{1,17},{... | collective-permute-start | bytes 393224 | tf_op jit(solution)/shard_map/ppermute | solution.py:913
  724.1 41.5 %collective-permute-start.12 = (bf16[192,256]{1,0:T(8,128)(2,1)S(1)}, bf16[192,256]{1,0:T(8,128)(2,1)S(1)}, u32[]{:S(2)}, u32[]{:S(2)}) collective-permute-start(bf16[192,256]{1,0:T(8,128)(2,1)S(1)} %pad_maximum_fusion.9), channel_id=1, source_target_pairs={{0,8},{4,12},{8,0},{12,4},{16,24},{20,28},{24,16},{28,20},{1,9},{5... | collective-permute-start | bytes 294920 | tf_op jit(solution)/shard_map/ppermute | solution.py:913
  761.3 30.1 %collective-permute-start.9 = (bf16[64,1024]{1,0:T(8,128)(2,1)S(1)}, bf16[64,1024]{1,0:T(8,128)(2,1)S(1)}, u32[]{:S(2)}, u32[]{:S(2)}) collective-permute-start(bf16[64,1024]{1,0:T(8,128)(2,1)S(1)} %fusion), channel_id=1, source_target_pairs={{0,16},{4,20},{8,24},{12,28},{16,0},{20,4},{24,8},{28,12},{1,17},{... | collective-permute-start | bytes 393224 | tf_op jit(solution)/shard_map/ppermute | solution.py:913
  765.8 26.3 %collective-permute-start.13 = (bf16[128,256]{1,0:T(8,128)(2,1)S(1)}, bf16[128,256]{1,0:T(8,128)(2,1)S(1)}, u32[]{:S(2)}, u32[]{:S(2)}) collective-permute-start(bf16[128,256]{1,0:T(8,128)(2,1)S(1)} %pad_maximum_fusion.10), channel_id=1, source_target_pairs={{0,16},{4,20},{8,24},{12,28},{16,0},{20,4},{24,8},{28,12},{1,17},{... | collective-permute-start | bytes 196616 | tf_op jit(solution)/shard_map/ppermute | solution.py:913
  792.3 7.8 collective-permute-start.14
  800.4 2.9 collective-permute-start.15

commit v4 on v3

--- a/solution.py
+++ b/solution.py
@@ -729,7 +729,7 @@
 
 def cost(microseconds):
     return pl.CostEstimate(
-        flops=microseconds * 400_000_000, bytes_accessed=1_000_000, transcendentals=0
+        flops=microseconds * 150_000_000, bytes_accessed=1_000_000, transcendentals=0
     )
 
 
@@ -1085,13 +1085,10 @@
     last_sum, first_sum, grad, feed_sums, mix_sums = tie(
         (last_sum, first_sum, grad, feed_sums, mix_sums)
     )
-    last_kept, last_sent = row_halves(last_sum, 1, shard)
     kept, sent = row_halves(first_sum, 0, shard)
     first_sum = traded(kept, sent, "wide", 0)
-    delivered, grad, returned_first, first_sum, feed_sums, mix_sums = tie(
-        (delivered, grad, returned, first_sum, feed_sums, mix_sums)
-    )
-    returned = exchange(grad.reshape(abroad))
+    kept, sent = row_halves(last_sum, 1, shard)
+    last_sum = traded(kept, sent, "wide", 1, first_sum)
     lines = jnp.stack(
         [
             jnp.concatenate([jnp.sum(sums[layer][-1], axis=0) for sums in (feed_sums, mix_sums)])
@@ -1103,48 +1100,60 @@
         jnp.concatenate(each, axis=1)
         for each in zip(*[halves(sums[0], own_bit("rep", 0), 1) for sums in mix_sums])
     )
-    lines = jnp.pad(lines.reshape(-1), (0, -lines_size % (16 * sent.shape[1])))
+    width = sent.shape[1]
+    lines = jnp.pad(lines.reshape(-1), (0, -lines_size % (16 * width)))
     blocks, lines = traded_with(kept, sent, lines, "rep", 0)
-    last_sum = traded(last_kept, last_sent, "wide", 1, blocks)
-    blocks, returned_first, delivered = tie((blocks, returned_first, delivered))
+    delivered, grad, returned_first, first_sum, last_sum, blocks, lines = tie(
+        (delivered, grad, returned, first_sum, last_sum, blocks, lines)
+    )
+    kept, sent = row_halves(first_sum, 1, shard)
+    near = traded(kept, sent, "wide", 1)
+    kept, sent = row_halves(near, 2, shard)
+    first_sum = traded(kept, sent, "wide", 2)
+    kept, sent = row_halves(last_sum, 2, shard)
+    last_sum = traded(kept, sent, "wide", 2)
+    for bit in (0, 1):
+        kept, sent = row_halves(blocks, bit, shard)
+        blocks, lines = traded_with(kept, sent, lines, "wide", bit, near if bit else ())
+        if bit == 0:
+            blocks, lines, delivered, returned_first = tie(
+                (blocks, lines, delivered, returned_first)
+            )
+    returned = exchange(grad.reshape(abroad))
+    kept, sent = row_halves(blocks, 2, shard)
+    blocks, lines = traded_with(kept, sent, lines, "wide", 2)
     input_grad = widened(one_part(returned_first), 0, chunks, None)
     output = widened(
         delivered.reshape(wide, chunks, *tokens.shape[1:]), 0, chunks, None
     ).reshape(tokens.shape)
-    kept, sent = row_halves(blocks, 0, shard)
-    blocks, lines = traded_with(kept, sent, lines, "wide", 0)
-    high_kept, high_sent = row_halves(blocks, 1, shard)
-    kept, sent = row_halves(first_sum, 1, shard)
-    first_sum = traded(kept, sent, "wide", 1, (high_sent, lines))
-    kept, sent = row_halves(first_sum, 2, shard)
-    first_sum = traded(kept, sent, "wide", 2)
-    kept, sent = row_halves(last_sum, 2, shard)
-    last_sum = traded(kept, sent, "wide", 2, first_sum)
-    blocks, lines = traded_with(high_kept, high_sent, lines, "wide", 1)
-    kept, sent = row_halves(blocks, 2, shard)
-    blocks, lines = traded_with(kept, sent, lines, "wide", 2)
-    returned, output, input_grad, first_sum, last_sum, blocks, lines = tie(
-        (returned, output, input_grad, first_sum, last_sum, blocks, lines)
-    )
-    chain = jnp.concatenate([first_sum, blocks], axis=1)
     columns = last_sum.shape[1]
-    part = lines.size // shard
-    lines = lines.astype(BF)
-    message = jnp.concatenate(
-        [chain[:, :columns], last_sum, chain[:, columns:], lines.reshape(shard, part)], axis=1
-    ).astype(BF)
+    message = jnp.concatenate([first_sum, last_sum], axis=1).astype(BF)
     arrived = swapped(message, "rep", 2)
-    input_grad = widened(one_part(returned), 1, chunks, input_grad).reshape(tokens.shape)
-    arrived, input_grad = tie((arrived, input_grad))
     first_sum, last_sum = (
         side_by_side(message[:, at : at + columns], arrived[:, at : at + columns], 1)
         for at in (0, columns)
     )
-    blocks = message[:, 2 * columns : -part].astype(F32) + arrived[:, 2 * columns : -part].astype(F32)
-    lines = lines.astype(F32) + arrived[:, -part:].astype(F32).reshape(-1)
+    message = jnp.concatenate([first_sum, last_sum], axis=1)
+    arrived = swapped(message, "rep", 1)
+    matrices = [
+        side_by_side(message[:, at : at + 2 * columns], arrived[:, at : at + 2 * columns], 0).astype(
+            F32
+        )
+        for at in (0, 2 * columns)
+    ]
+    w_in_grad = jnp.stack([matrix[:, :FF] for matrix in matrices])
+    w_out_grad = jnp.stack([matrix[:, FF:].T for matrix in matrices])
+    returned, output, input_grad, w_in_grad, w_out_grad, blocks, lines = tie(
+        (returned, output, input_grad, w_in_grad, w_out_grad, blocks, lines)
+    )
+    mixed = jnp.concatenate([blocks, lines.reshape(shard, -1)], axis=1).astype(BF)
+    arrived = swapped(mixed, "rep", 2)
+    input_grad = widened(one_part(returned), 1, chunks, input_grad).reshape(tokens.shape)
+    arrived, input_grad = tie((arrived, input_grad))
+    mixed = mixed.astype(F32) + arrived.astype(F32)
+    blocks, lines = mixed[:, :width].astype(BF), mixed[:, width:].reshape(-1)
     packed = lines[:lines_size].reshape(LAYERS, -1)
-    message = jnp.concatenate([first_sum, last_sum, blocks.astype(BF)], axis=1)
-    arrived = swapped(message, "rep", 1)
+    arrived = swapped(blocks, "rep", 1)
     b_in_grad, b_out_grad, gain_two, shift_two, in_bias, out_bias, gain_one, shift_one = (
         jnp.split(packed, np.cumsum([FF, D, D, D, 1024, 1024, D]), axis=1)
     )
@@ -1155,16 +1164,8 @@
     arrived, gain_grad, shift_grad, in_bias_grad, out_bias_grad, b_in_grad, b_out_grad = tie(
         (arrived, gain_grad, shift_grad, in_bias_grad, out_bias_grad, b_in_grad, b_out_grad)
     )
-    matrices = [
-        side_by_side(message[:, at : at + 2 * columns], arrived[:, at : at + 2 * columns], 0).astype(
-            F32
-        )
-        for at in (0, 2 * columns)
-    ]
-    blocks = side_by_side(message[:, 4 * columns :], arrived[:, 4 * columns :], 0).astype(F32)
+    blocks = side_by_side(blocks, arrived, 0).astype(F32)
     mix_grads = blocks.reshape(shard, 2, LAYERS, 2 * BS).transpose(1, 2, 0, 3)
-    w_in_grad = jnp.stack([matrix[:, :FF] for matrix in matrices])
-    w_out_grad = jnp.stack([matrix[:, FF:].T for matrix in matrices])
 
     return (
         output, input_grad, gain_grad, shift_grad, mix_grads[0], in_bias_grad,

time: 816 us -> 830 us (1.017)
  waiting for transfers between devices: 200 us -> 216 us
    ppermute x16 -> x18, waiting for transfers between devices: 84.2 us -> 100 us  [swapped(): return lax.ppermute(array, axis_name, [(i, i ^ far) for i in range(size)])]
    ppermute x16 -> x18, starting transfers between devices: 23.1 us -> 20.8 us  [swapped(): return lax.ppermute(array, axis_name, [(i, i ^ far) for i in range(size)])]
  transfers between devices with their start and end apart: 22 -> 24, of which waited for: 11 -> 11; matrix products, arithmetic and copies ran while one was open for 7% -> 7% of each run, Pallas kernels for 60% -> 59%
where the time goes in v4:
time: 830 us; the launch traced here: 822 us
  Pallas kernels  481 us (58%)
  waiting for transfers between devices  216 us (26%)
  starting transfers between devices  52.7 us (6%)
  local copies, waits for them, and re-layouts  41.5 us (5%)
  other arithmetic  29.1 us (4%)
    pallas_call x4, Pallas kernels, feed_backward(): pl.pallas_call(functools.partial(feed_backward_kernel, len(start) > 0), g...  198 us
    all_to_all x6, waiting for transfers between devices, exchange(): lax.all_to_all(array, 'wide', split_axis=0, concat_axis=0, tiled=True)  115 us
    ppermute x18, waiting for transfers between devices, swapped(): return lax.ppermute(array, axis_name, [(i, i ^ far) for i in range(size)])  100 us
    pallas_call x4, Pallas kernels, feed_forward(): pl.pallas_call(feed_forward_kernel, grid=(H * W // TT,), in_specs=[rows_s...  98.2 us
    pallas_call x4, Pallas kernels, spectral_backward(): pl.pallas_call(functools.partial(spectral_backward_kernel, len(start) > 0...  92.2 us
    pallas_call x4, Pallas kernels, spectral_forward(): pl.pallas_call(spectral_forward_kernel, grid=(SPECTRAL_STEPS,), in_specs=...  64.7 us
    all_to_all x6, starting transfers between devices, exchange(): lax.all_to_all(array, 'wide', split_axis=0, concat_axis=0, tiled=True)  31.9 us
    pallas_call x3, Pallas kernels, widened(): pl.pallas_call(widen_kernel, grid=(parts, items), in_specs=[pl.BlockSpec(...  27.9 us
  transfers between devices with their start and end apart: 24, of which 11 were waited for; matrix products, arithmetic and copies ran while one was open for 7% of the time, Pallas kernels for 59%

profile of v4, /device:TPU:0, one launch (start us, length us, event | category | flops | bytes accessed | tf_op | source)
XLA Modules:
  0.0 822.2 jit_solution(8762243377523171693)
XLA Ops:
  0.6 4.7 slice.164
  5.3 7.4 all-to-all-start
  19.1 9.1 %convert.42 = bf16[16,8,64,512]{3,2,1,0:T(8,128)(2,1)} convert(f32[16,8,64,512]{3,2,1,0:T(8,128)} %param.21) | non-fusion elementwise | flops 4194304 | bytes 25165824 | tf_op jit(solution)/shard_map/convert.21
  32.1 1.1 fusion.3
  33.2 1.1 fusion.5
  36.2 4.1 fusion.11
  40.7 6.2 pad_maximum_fusion
  47.0 59.0 %all-to-all-done = bf16[8,8,64,512]{3,2,1,0:T(8,128)(2,1)} async-done(((bf16[8,8,64,512]{3,2,1,0:T(8,128)(2,1)}), bf16[8,8,64,512]{3,2,1,0:T(8,128)(2,1)}, u32[]{:S(2)}, u32[]{:S(2)}) %all-to-all-start) | async-done | bytes 4194336 | tf_op jit(solution)/shard_map/all_to_all | solution.py:904
  106.0 4.8 all-to-all-start.1
  110.8 1.0 copy.122.w1.refs_8_
  111.8 1.0 copy.123.w2.refs_10_
  112.8 1.0 copy.124.w1.refs_8_
  113.9 1.0 copy.125.w2.refs_10_
  114.9 16.2 %spectral_forward.4 = (bf16[4096,512]{1,0:T(8,128)(2,1)}, bf16[32,64,512]{2,1,0:T(8,128)(2,1)}) custom-call(bf16[4096,512]{1,0:T(8,128)(2,1)} %bitcast.26.x_ref.refs_0_, f32[1,512]{1,0:T(1,128)} %get-tuple-element.147.gain.refs_3_, f32[1,512]{1,0:T(1,128)} %get-tuple-element.148.shift, bf16[256,256]{1,0:T(8,128)(2,1)} %constant.44.clone.into, ...), custom_call_target="tpu_custom_call" | custom-call | flops 2400000000 | bytes 1000000 | tf_op jit(solution)/shard_map/spectral_forward/pallas_call | solution.py:754
  131.0 24.5 %feed_forward.4 = (bf16[4096,512]{1,0:T(8,128)(2,1)}, bf16[4096,2048]{1,0:T(8,128)(2,1)}) custom-call(bf16[4096,512]{1,0:T(8,128)(2,1)} %get-tuple-element.153.mid_ref.refs_1_, f32[1,512]{1,0:T(1,128)} %get-tuple-element.154.gain.refs_3_, f32[1,512]{1,0:T(1,128)} %get-tuple-element.155.shift.refs_4_, bf16[2,512,2048]{2,1,0:T(8,128)(2,1)} %refs_6_.11, ...), custom_call_target="tpu_custom_call" | custom-call | flops 3600000000 | bytes 1000000 | tf_op jit(solution)/shard_map/feed_forward/pallas_call | solution.py:814
  155.5 16.1 %spectral_forward.5 = (bf16[4096,512]{1,0:T(8,128)(2,1)}, bf16[32,64,512]{2,1,0:T(8,128)(2,1)}) custom-call(bf16[4096,512]{1,0:T(8,128)(2,1)} %get-tuple-element.158.x_ref.refs_0_, f32[1,512]{1,0:T(1,128)} %get-tuple-element.160.gain.refs_3_, f32[1,512]{1,0:T(1,128)} %get-tuple-element.161.shift, bf16[256,256]{1,0:T(8,128)(2,1)} %constant.44.clone.into, ...), custom_call_target="tpu_custom_call" | custom-call | flops 2400000000 | bytes 1000000 | tf_op jit(solution)/shard_map/spectral_forward/pallas_call | solution.py:754
  171.6 24.4 %feed_forward.5 = (bf16[8,2,512,512]{3,2,1,0:T(8,128)(2,1)}, bf16[4096,2048]{1,0:T(8,128)(2,1)}) custom-call(bf16[4096,512]{1,0:T(8,128)(2,1)} %get-tuple-element.166.mid_ref.refs_1_, f32[1,512]{1,0:T(1,128)} %get-tuple-element.167.gain.refs_3_, f32[1,512]{1,0:T(1,128)} %get-tuple-element.168.shift.refs_4_, bf16[2,512,2048]{2,1,0:T(8,128)(2,1)} %refs_6_.11, ...), custom_call_target="tpu_custom_call" | custom-call | flops 3600000000 | bytes 1000000 | tf_op jit(solution)/shard_map/feed_forward/pallas_call | solution.py:814
  196.1 7.2 all-to-all-done.1
  203.3 5.4 all-to-all-start.2
  208.7 48.8 %feed_backward.4 = (bf16[4096,512]{1,0:T(8,128)(2,1)}, f32[512,4096]{1,0:T(8,128)}, f32[8,3584]{1,0:T(8,128)}) custom-call(bf16[4096,512]{1,0:T(8,128)(2,1)} %bitcast.27.refs_0_, bf16[4096,512]{1,0:T(8,128)(2,1)} %get-tuple-element.166.mid_ref.refs_1_, bf16[4096,2048]{1,0:T(8,128)(2,1)} %get-tuple-element.174.refs_2_, ...), custom_call_target="tpu_custom_call" | custom-call | flops 7350000128 | bytes 1000000 | tf_op jit(solution)/shard_map/feed_backward/pallas_call | solution.py:841
  257.5 22.8 %spectral_backward.4 = (bf16[4096,512]{1,0:T(8,128)(2,1)}, f32[512,256]{1,0:T(8,128)}, f32[8,3072]{1,0:T(8,128)}) custom-call(bf16[4096,512]{1,0:T(8,128)(2,1)} %get-tuple-element.158.x_ref.refs_0_, bf16[4096,512]{1,0:T(8,128)(2,1)} %get-tuple-element.175.refs_1_, bf16[32,64,512]{2,1,0:T(8,128)(2,1)} %get-tuple-element.176.refs_2_, ...), custom_call_target="tpu_custom_call" | custom-call | flops 3600000000 | bytes 1000000 | tf_op jit(solution)/shard_map/spectral_backward/pallas_call | solution.py:780
  280.3 49.1 %feed_backward.5 = (bf16[4096,512]{1,0:T(8,128)(2,1)}, f32[512,4096]{1,0:T(8,128)}, f32[8,3584]{1,0:T(8,128)}) custom-call(bf16[4096,512]{1,0:T(8,128)(2,1)} %get-tuple-element.179.refs_0_, bf16[4096,512]{1,0:T(8,128)(2,1)} %get-tuple-element.153.mid_ref.refs_1_, bf16[4096,2048]{1,0:T(8,128)(2,1)} %get-tuple-element.180.refs_2_, ...), custom_call_target="tpu_custom_call" | custom-call | flops 7350000128 | bytes 1000000 | tf_op jit(solution)/shard_map/feed_backward/pallas_call | solution.py:841
  329.5 23.0 %spectral_backward.5 = (bf16[4096,512]{1,0:T(8,128)(2,1)}, f32[512,256]{1,0:T(8,128)}, f32[8,3072]{1,0:T(8,128)}) custom-call(bf16[4096,512]{1,0:T(8,128)(2,1)} %bitcast.26.x_ref.refs_0_, bf16[4096,512]{1,0:T(8,128)(2,1)} %get-tuple-element.181.refs_1_, bf16[32,64,512]{2,1,0:T(8,128)(2,1)} %get-tuple-element.182.refs_2_, ...), custom_call_target="tpu_custom_call" | custom-call | flops 3600000000 | bytes 1000000 | tf_op jit(solution)/shard_map/spectral_backward/pallas_call | solution.py:780
  352.4 38.3 %all-to-all-done.2.x_ref.refs_0_ = bf16[8,2,512,512]{3,2,1,0:T(8,128)(2,1)} async-done(((bf16[8,2,512,512]{3,2,1,0:T(8,128)(2,1)}), bf16[8,2,512,512]{3,2,1,0:T(8,128)(2,1)}, u32[]{:S(2)}, u32[]{:S(2)}) %all-to-all-start.2) | async-done | bytes 8388640 | tf_op jit(solution)/shard_map/all_to_all | solution.py:904
  390.7 4.8 all-to-all-start.3
  395.5 16.3 %spectral_forward.6 = (bf16[4096,512]{1,0:T(8,128)(2,1)}, bf16[32,64,512]{2,1,0:T(8,128)(2,1)}) custom-call(bf16[8,2,512,512]{3,2,1,0:T(8,128)(2,1)} %all-to-all-done.2.x_ref.refs_0_, f32[1,512]{1,0:T(1,128)} %get-tuple-element.147.gain.refs_3_, f32[1,512]{1,0:T(1,128)} %get-tuple-element.148.shift, bf16[256,256]{1,0:T(8,128)(2,1)} %constant.44.clone.into, ...), custom_call_target="tpu_custom_call" | custom-call | flops 2400000000 | bytes 1000000 | tf_op jit(solution)/shard_map/spectral_forward/pallas_call | solution.py:754
  411.8 24.5 %feed_forward.6 = (bf16[4096,512]{1,0:T(8,128)(2,1)}, bf16[4096,2048]{1,0:T(8,128)(2,1)}) custom-call(bf16[4096,512]{1,0:T(8,128)(2,1)} %get-tuple-element.190.mid_ref.refs_1_, f32[1,512]{1,0:T(1,128)} %get-tuple-element.154.gain.refs_3_, f32[1,512]{1,0:T(1,128)} %get-tuple-element.155.shift.refs_4_, bf16[2,512,2048]{2,1,0:T(8,128)(2,1)} %refs_6_.11, ...), custom_call_target="tpu_custom_call" | custom-call | flops 3600000000 | bytes 1000000 | tf_op jit(solution)/shard_map/feed_forward/pallas_call | solution.py:814
  436.2 16.2 %spectral_forward.7 = (bf16[4096,512]{1,0:T(8,128)(2,1)}, bf16[32,64,512]{2,1,0:T(8,128)(2,1)}) custom-call(bf16[4096,512]{1,0:T(8,128)(2,1)} %get-tuple-element.191.x_ref.refs_0_, f32[1,512]{1,0:T(1,128)} %get-tuple-element.160.gain.refs_3_, f32[1,512]{1,0:T(1,128)} %get-tuple-element.161.shift, bf16[256,256]{1,0:T(8,128)(2,1)} %constant.44.clone.into, ...), custom_call_target="tpu_custom_call" | custom-call | flops 2400000000 | bytes 1000000 | tf_op jit(solution)/shard_map/spectral_forward/pallas_call | solution.py:754
  452.4 24.8 %feed_forward.7 = (bf16[8,2,512,512]{3,2,1,0:T(8,128)(2,1)}, bf16[4096,2048]{1,0:T(8,128)(2,1)}) custom-call(bf16[4096,512]{1,0:T(8,128)(2,1)} %get-tuple-element.192.mid_ref.refs_1_, f32[1,512]{1,0:T(1,128)} %get-tuple-element.167.gain.refs_3_, f32[1,512]{1,0:T(1,128)} %get-tuple-element.168.shift.refs_4_, ...), custom_call_target="tpu_custom_call", output_to_operand_aliasing={{0}: (7, {})} | custom-call | flops 3600000000 | bytes 1000000 | tf_op jit(solution)/shard_map/feed_forward/pallas_call | solution.py:814
  477.2 10.9 %all-to-all-done.3 = bf16[8,8,64,512]{3,2,1,0:T(8,128)(2,1)} async-done(((bf16[8,8,64,512]{3,2,1,0:T(8,128)(2,1)}), bf16[8,8,64,512]{3,2,1,0:T(8,128)(2,1)}, u32[]{:S(2)}, u32[]{:S(2)}) %all-to-all-start.3) | async-done | bytes 4194336 | tf_op jit(solution)/shard_map/all_to_all | solution.py:904
  488.2 4.9 all-to-all-start.4
  493.1 49.9 %feed_backward.6 = (bf16[4096,512]{1,0:T(8,128)(2,1)}, bf16[512,2048]{1,0:T(8,128)(2,1)}, bf16[512,2048]{1,0:T(8,128)(2,1)}, f32[8,3584]{1,0:T(8,128)}) custom-call(bf16[8,2,512,512]{3,2,1,0:T(8,128)(2,1)} %all-to-all-done.2.x_ref.refs_0_, bf16[4096,512]{1,0:T(8,128)(2,1)} %get-tuple-element.192.mid_ref.refs_1_, ...), custom_call_target="tpu_custom_call" | custom-call | flops 7350000128 | bytes 1000000 | tf_op jit(solution)/shard_map/feed_backward/pallas_call | solution.py:841
  543.1 23.3 %spectral_backward.6 = (bf16[4096,512]{1,0:T(8,128)(2,1)}, f32[512,256]{1,0:T(8,128)}, f32[8,3072]{1,0:T(8,128)}) custom-call(bf16[4096,512]{1,0:T(8,128)(2,1)} %get-tuple-element.191.x_ref.refs_0_, bf16[4096,512]{1,0:T(8,128)(2,1)} %get-tuple-element.201.refs_1_, bf16[32,64,512]{2,1,0:T(8,128)(2,1)} %get-tuple-element.202.refs_2_, ...), custom_call_target="tpu_custom_call" | custom-call | flops 3600000000 | bytes 1000000 | tf_op jit(solution)/shard_map/spectral_backward/pallas_call | solution.py:780
  567.2 2.1 copy-done.1
  569.4 1.6 collective-permute-start.1
  571.0 1.8 constant_dynamic-slice_fusion.9
  572.8 50.1 %feed_backward.7 = (bf16[4096,512]{1,0:T(8,128)(2,1)}, bf16[512,2048]{1,0:T(8,128)(2,1)}, bf16[512,2048]{1,0:T(8,128)(2,1)}, f32[8,3584]{1,0:T(8,128)}) custom-call(bf16[4096,512]{1,0:T(8,128)(2,1)} %get-tuple-element.209.refs_0_, bf16[4096,512]{1,0:T(8,128)(2,1)} %get-tuple-element.190.mid_ref.refs_1_, bf16[4096,2048]{1,0:T(8,128)(2,1)} %get-tuple-element.210.refs_2_, ...), custom_call_target="tpu_custom_call" | custom-call | flops 7350000128 | bytes 1000000 | tf_op jit(solution)/shard_map/feed_backward/pallas_call | solution.py:841
  623.4 4.3 collective-permute-done.2
  627.7 3.0 convert_add_fusion
  630.8 1.1 dynamic-slice_convert_fusion
  633.3 1.9 collective-permute-start.3
  635.4 23.2 %spectral_backward.7 = (bf16[4096,512]{1,0:T(8,128)(2,1)}, f32[512,256]{1,0:T(8,128)}, f32[8,3072]{1,0:T(8,128)}) custom-call(bf16[8,2,512,512]{3,2,1,0:T(8,128)(2,1)} %all-to-all-done.2.x_ref.refs_0_, bf16[4096,512]{1,0:T(8,128)(2,1)} %get-tuple-element.221.refs_1_, bf16[32,64,512]{2,1,0:T(8,128)(2,1)} %get-tuple-element.222.refs_2_, ...), custom_call_target="tpu_custom_call" | custom-call | flops 3600000000 | bytes 1000000 | tf_op jit(solution)/shard_map/spectral_backward/pallas_call | solution.py:780
  658.7 4.2 collective-permute-done.3
  662.9 1.1 convert_add_fusion.5
  664.0 1.5 convert_add_fusion.2
  665.6 1.0 reduce_sum.37
  671.2 2.6 collective-permute-start.5
  674.1 12.1 %collective-permute-done.5 = bf16[256,1024]{1,0:T(8,128)(2,1)S(1)} collective-permute-done((bf16[256,1024]{1,0:T(8,128)(2,1)S(1)}, bf16[256,1024]{1,0:T(8,128)(2,1)S(1)}, u32[]{:S(2)}, u32[]{:S(2)}) %collective-permute-start.5) | collective-permute-done | bytes 524320 | tf_op jit(solution)/shard_map/ppermute | solution.py:913
  686.7 1.8 collective-permute-start.11
  688.8 2.7 collective-permute-start.9
  691.6 4.6 all-to-all-start.5
  696.5 2.0 collective-permute-start.14
  698.4 13.4 %widen.3 = f32[2,8,8,64,512]{4,3,2,1,0:T(8,128)} custom-call(bf16[8,2,8,64,512]{4,3,2,1,0:T(8,128)(2,1)} %bitcast.43.part), custom_call_target="tpu_custom_call" | custom-call | bytes 1000000 | tf_op jit(solution)/shard_map/widen/pallas_call | solution.py:887
  711.9 7.3 widen.4.refs_0_
  719.1 47.8 %collective-permute-done.14 = bf16[192,256]{1,0:T(8,128)(2,1)S(1)} collective-permute-done((bf16[192,256]{1,0:T(8,128)(2,1)S(1)}, bf16[192,256]{1,0:T(8,128)(2,1)S(1)}, u32[]{:S(2)}, u32[]{:S(2)}) %collective-permute-start.14) | collective-permute-done | bytes 98336 | tf_op jit(solution)/shard_map/ppermute | solution.py:913
  767.2 3.6 collective-permute-start.10
  771.0 25.2 %collective-permute-done.10 = bf16[64,1024]{1,0:T(8,128)(2,1)S(1)} collective-permute-done((bf16[64,1024]{1,0:T(8,128)(2,1)S(1)}, bf16[64,1024]{1,0:T(8,128)(2,1)S(1)}, u32[]{:S(2)}, u32[]{:S(2)}) %collective-permute-start.10) | collective-permute-done | bytes 131104 | tf_op jit(solution)/shard_map/ppermute | solution.py:913
  796.2 1.6 collective-permute-start.12
  797.9 4.8 collective-permute-done.12
  802.9 1.8 collective-permute-done.13
  805.3 1.1 pad_maximum_fusion.2
  806.4 1.1 pad_maximum_fusion.1
  807.5 1.6 collective-permute-start.16
  809.1 7.3 widen.5
  (212 shorter events, 27.9 us)
Async XLA Ops:
  5.3 7.4 copy-start.4
  5.3 100.7 %all-to-all-start = ((bf16[8,8,64,512]{3,2,1,0:T(8,128)(2,1)}), bf16[8,8,64,512]{3,2,1,0:T(8,128)(2,1)}, u32[]{:S(2)}, u32[]{:S(2)}) async-start(bf16[8,8,64,512]{3,2,1,0:T(8,128)(2,1)} %slice.164), calls=%async_computation | async-start | bytes 8388608 | tf_op jit(solution)/shard_map/all_to_all | solution.py:904
  12.7 1.6 copy-start.5
  28.1 0.7 copy-start.10
  28.1 1.5 copy-start.11
  31.9 2.5 copy-start.14
  31.9 3.1 copy-start.12
  31.9 3.1 copy-start.13
  31.9 3.7 copy-start.9
  31.9 4.3 copy-start
  36.2 4.5 slice-start
  106.0 97.3 %all-to-all-start.1 = ((bf16[8,8,64,512]{3,2,1,0:T(8,128)(2,1)}), bf16[8,8,64,512]{3,2,1,0:T(8,128)(2,1)}, u32[]{:S(2)}, u32[]{:S(2)}) async-start(bf16[8,8,64,512]{3,2,1,0:T(8,128)(2,1)} %get-tuple-element.159), calls=%async_computation.1 | async-start | bytes 8388608 | tf_op jit(solution)/shard_map/all_to_all | solution.py:904
  203.3 187.4 %all-to-all-start.2 = ((bf16[8,2,512,512]{3,2,1,0:T(8,128)(2,1)}), bf16[8,2,512,512]{3,2,1,0:T(8,128)(2,1)}, u32[]{:S(2)}, u32[]{:S(2)}) async-start(bf16[8,2,512,512]{3,2,1,0:T(8,128)(2,1)} %pad_maximum_fusion), calls=%async_computation.2 | async-start | bytes 16777216 | tf_op jit(solution)/shard_map/all_to_all | solution.py:904
  390.7 97.5 %all-to-all-start.3 = ((bf16[8,8,64,512]{3,2,1,0:T(8,128)(2,1)}), bf16[8,8,64,512]{3,2,1,0:T(8,128)(2,1)}, u32[]{:S(2)}, u32[]{:S(2)}) async-start(bf16[8,8,64,512]{3,2,1,0:T(8,128)(2,1)} %bitcast.170), calls=%async_computation.3 | async-start | bytes 8388608 | tf_op jit(solution)/shard_map/all_to_all | solution.py:904
  488.2 198.3 %all-to-all-start.4 = ((bf16[8,2,512,512]{3,2,1,0:T(8,128)(2,1)}), bf16[8,2,512,512]{3,2,1,0:T(8,128)(2,1)}, u32[]{:S(2)}, u32[]{:S(2)}) async-start(bf16[8,2,512,512]{3,2,1,0:T(8,128)(2,1)} %get-tuple-element.195), calls=%async_computation.4 | async-start | bytes 16777216 | tf_op jit(solution)/shard_map/all_to_all | solution.py:904
  543.0 23.4 %collective-permute-start = (bf16[512,2048]{1,0:T(8,128)(2,1)}, bf16[512,2048]{1,0:T(8,128)(2,1)S(1)}, u32[]{:S(2)}, u32[]{:S(2)}) collective-permute-start(bf16[512,2048]{1,0:T(8,128)(2,1)} %get-tuple-element.207), channel_id=1, source_target_pairs={{0,1},{1,0},{2,3},{3,2},{4,5},{5,4},{6,7},{7,6},{8,9},{9,8},{10,11... | collective-permute-start | bytes 6291464 | tf_op jit(solution)/shard_map/ppermute | solution.py:913
  543.1 23.3 %copy-start.3 = (bf16[512,2048]{1,0:T(8,128)(2,1)S(1)}, bf16[512,2048]{1,0:T(8,128)(2,1)}, u32[]{:S(2)}) copy-start(bf16[512,2048]{1,0:T(8,128)(2,1)} %get-tuple-element.206) | copy-start | bytes 6291460
  567.1 2.1 copy-start.1
  569.4 53.5 %collective-permute-start.1 = (bf16[512,1024]{1,0:T(8,128)(2,1)S(1)}, bf16[512,1024]{1,0:T(8,128)(2,1)S(1)}, u32[]{:S(2)}, u32[]{:S(2)}) collective-permute-start(bf16[512,1024]{1,0:T(8,128)(2,1)S(1)} %dynamic-slice_convert_fusion.1), channel_id=1, source_target_pairs={{0,2},{1,3},{2,0},{3,1},{4,6},{5,7},{6,4},{7,5},{8,10},{9,11},{10,... | collective-permute-start | bytes 3145736 | tf_op jit(solution)/shard_map/ppermute | solution.py:913
  623.2 4.6 collective-permute-start.2
  631.9 32.1 %collective-permute-start.4 = (bf16[512,1024]{1,0:T(8,128)(2,1)}, bf16[512,1024]{1,0:T(8,128)(2,1)}, u32[]{:S(2)}, u32[]{:S(2)}) collective-permute-start(bf16[512,1024]{1,0:T(8,128)(2,1)} %dynamic-slice_convert_fusion), channel_id=1, source_target_pairs={{0,2},{1,3},{2,0},{3,1},{4,6},{5,7},{6,4},{7,5},{8,10},{9,11},{10,... | collective-permute-start | bytes 3145736 | tf_op jit(solution)/shard_map/ppermute | solution.py:913
  633.3 29.6 %collective-permute-start.3 = (bf16[256,1024]{1,0:T(8,128)(2,1)}, bf16[256,1024]{1,0:T(8,128)(2,1)S(1)}, u32[]{:S(2)}, u32[]{:S(2)}) collective-permute-start(bf16[256,1024]{1,0:T(8,128)(2,1)} %bitcast.32), channel_id=1, source_target_pairs={{0,4},{4,0},{8,12},{12,8},{16,20},{20,16},{24,28},{28,24},{1,5},{5... | collective-permute-start | bytes 1572872 | tf_op jit(solution)/shard_map/ppermute | solution.py:913
  658.6 6.9 copy-start.7
  658.6 8.0 copy-start.6
  658.7 8.0 copy-start.8
  665.5 8.2 %copy-start.2 = (f32[256,1024]{1,0:T(8,128)S(1)}, f32[256,1024]{1,0:T(8,128)}, u32[]{:S(2)}) copy-start(f32[256,1024]{1,0:T(8,128)} %convert_add_fusion.5) | copy-start | bytes 3145732
  668.9 5.0 collective-permute-start.7
  671.2 15.0 %collective-permute-start.5 = (bf16[256,1024]{1,0:T(8,128)(2,1)S(1)}, bf16[256,1024]{1,0:T(8,128)(2,1)S(1)}, u32[]{:S(2)}, u32[]{:S(2)}) collective-permute-start(bf16[256,1024]{1,0:T(8,128)(2,1)S(1)} %bitcast.196), channel_id=1, source_target_pairs={{0,4},{4,0},{8,12},{12,8},{16,20},{20,16},{24,28},{28,24},{1,5},{5... | collective-permute-start | bytes 1572872 | tf_op jit(solution)/shard_map/ppermute | solution.py:913
  673.8 12.6 %collective-permute-start.6 = (bf16[128,1024]{1,0:T(8,128)(2,1)S(1)}, bf16[128,1024]{1,0:T(8,128)(2,1)S(1)}, u32[]{:S(2)}, u32[]{:S(2)}) collective-permute-start(bf16[128,1024]{1,0:T(8,128)(2,1)S(1)} %bitcast.200), channel_id=1, source_target_pairs={{0,8},{4,12},{8,0},{12,4},{16,24},{20,28},{24,16},{28,20},{1,9},{5... | collective-permute-start | bytes 786440 | tf_op jit(solution)/shard_map/ppermute | solution.py:913
  686.7 9.5 %collective-permute-start.11 = (bf16[64,1024]{1,0:T(8,128)(2,1)S(1)}, bf16[64,1024]{1,0:T(8,128)(2,1)S(1)}, u32[]{:S(2)}, u32[]{:S(2)}) collective-permute-start(bf16[64,1024]{1,0:T(8,128)(2,1)S(1)} %fusion.1), channel_id=1, source_target_pairs={{0,16},{4,20},{8,24},{12,28},{16,0},{20,4},{24,8},{28,12},{1,17},{... | collective-permute-start | bytes 393224 | tf_op jit(solution)/shard_map/ppermute | solution.py:913
  688.5 7.8 collective-permute-start.8
  688.8 78.2 %collective-permute-start.9 = (bf16[128,1024]{1,0:T(8,128)(2,1)S(1)}, bf16[128,1024]{1,0:T(8,128)(2,1)S(1)}, u32[]{:S(2)}, u32[]{:S(2)}) collective-permute-start(bf16[128,1024]{1,0:T(8,128)(2,1)S(1)} %bitcast.199), channel_id=1, source_target_pairs={{0,8},{4,12},{8,0},{12,4},{16,24},{20,28},{24,16},{28,20},{1,9},{5... | collective-permute-start | bytes 786440 | tf_op jit(solution)/shard_map/ppermute | solution.py:913
  691.6 115.8 %all-to-all-start.5 = ((bf16[8,8,64,512]{3,2,1,0:T(8,128)(2,1)}), bf16[8,8,64,512]{3,2,1,0:T(8,128)(2,1)}, u32[]{:S(2)}, u32[]{:S(2)}) async-start(bf16[8,8,64,512]{3,2,1,0:T(8,128)(2,1)} %bitcast.169), calls=%async_computation.5 | async-start | bytes 8388608 | tf_op jit(solution)/shard_map/all_to_all | solution.py:904
  696.5 70.5 %collective-permute-start.14 = (bf16[192,256]{1,0:T(8,128)(2,1)S(1)}, bf16[192,256]{1,0:T(8,128)(2,1)S(1)}, u32[]{:S(2)}, u32[]{:S(2)}) collective-permute-start(bf16[192,256]{1,0:T(8,128)(2,1)S(1)} %pad_maximum_fusion.10), channel_id=1, source_target_pairs={{0,8},{4,12},{8,0},{12,4},{16,24},{20,28},{24,16},{28,20},{1,9},{5... | collective-permute-start | bytes 294920 | tf_op jit(solution)/shard_map/ppermute | solution.py:913
  767.2 29.0 %collective-permute-start.10 = (bf16[64,1024]{1,0:T(8,128)(2,1)S(1)}, bf16[64,1024]{1,0:T(8,128)(2,1)S(1)}, u32[]{:S(2)}, u32[]{:S(2)}) collective-permute-start(bf16[64,1024]{1,0:T(8,128)(2,1)S(1)} %fusion), channel_id=1, source_target_pairs={{0,16},{4,20},{8,24},{12,28},{16,0},{20,4},{24,8},{28,12},{1,17},{... | collective-permute-start | bytes 393224 | tf_op jit(solution)/shard_map/ppermute | solution.py:913
  770.8 27.0 %collective-permute-start.15 = (bf16[128,256]{1,0:T(8,128)(2,1)S(1)}, bf16[128,256]{1,0:T(8,128)(2,1)S(1)}, u32[]{:S(2)}, u32[]{:S(2)}) collective-permute-start(bf16[128,256]{1,0:T(8,128)(2,1)S(1)} %pad_maximum_fusion.11), channel_id=1, source_target_pairs={{0,16},{4,20},{8,24},{12,28},{16,0},{20,4},{24,8},{28,12},{1,17},{... | collective-permute-start | bytes 196616 | tf_op jit(solution)/shard_map/ppermute | solution.py:913
  796.2 6.4 collective-permute-start.12
  802.8 2.0 collective-permute-start.13
  807.5 8.8 %collective-permute-start.16 = (bf16[64,512]{1,0:T(8,128)(2,1)S(1)}, bf16[64,512]{1,0:T(8,128)(2,1)S(1)}, u32[]{:S(2)}, u32[]{:S(2)}) collective-permute-start(bf16[64,512]{1,0:T(8,128)(2,1)S(1)} %pad_maximum_fusion.12), channel_id=1, source_target_pairs={{0,2},{1,3},{2,0},{3,1},{4,6},{5,7},{6,4},{7,5},{8,10},{9,11},{10,... | collective-permute-start | bytes 196616 | tf_op jit(solution)/shard_map/ppermute | solution.py:913
  817.0 2.3 collective-permute-start.17
